TPU v7x, 256 devices: a whole 4x4x8 slice. The times are simulated.
256 devices in a mesh: seq: 32 (over x, y, core), mp: 8 (over z).
Axes of the slice: x: 4, y: 4, z: 8, core: 2. Of those that a mesh axis runs over, the one named last changes fastest.
Arguments:
- hidden: bfloat16 [8192, 8192], P('seq'), may hold values from -6 to 6
- query_weight: bfloat16 [8192, 4096], P('seq', 'mp'), may hold values from -0.0625 to 0.0625
- key_memory: bfloat16 [8192, 4096], P('seq', 'mp'), may hold values from -96 to 96
- value_memory: bfloat16 [8192, 4096], P('seq', 'mp'), may hold values from -6 to 6
- block_len: int32 [64], P('seq'), may hold values from 65 to 128, as said below
- nbr_block: int32 [128, 2], P('seq'), may hold values from 0 to 63, as said below
- out_grad: bfloat16 [8192, 4096], P('seq', 'mp'), may hold values from -6 to 6
Outputs:
- attended: bfloat16 [8192, 4096], P('seq', 'mp')
- d_hidden: bfloat16 [8192, 8192], P(('seq', 'mp'))
- d_key: bfloat16 [8192, 4096], P('seq', 'mp')
- d_value: bfloat16 [8192, 4096], P('seq', 'mp')
Inputs may be any that keep to these rules, and one draw needn't show every extreme that they name: `nbr_block`: each retrieval group names two blocks. Block b is held by index b // 2 of seq. The 64-row groups of one index of seq (aligned runs of 4 rows) form 2 * 4 pairs, of which at most one names a block held by any given index of seq; in every draw there is one index of seq whose blocks are named by exactly one pair from every index of seq. `block_len`: some block is full in every draw.
All inputs are finite; a program needn't handle non-finite values.
Results may differ from a plain program's by a relative error of at most 0.035.
Values may be sent and summed in bfloat16 or wider, within the bound.
No kernel may reach another device: no remote copies, remote signals or barrier semaphores. Data moves between devices by JAX's collectives and lax.ppermute only.
A program may use at most 128 MiB of HBM per device.

v0:
```python
import jax
import jax.numpy as jnp
from jax import lax
from jax.sharding import PartitionSpec as P

HD = 128
GROUP = 64
NLEN = 128
SEQ_LEN = 2048


NEG_FILL = -1e30


def from_behind(shard, axis, by):
    count = lax.axis_size(axis)
    pairs = [(i, i + by) for i in range(count) if 0 <= i + by < count]
    return lax.ppermute(shard, axis, pairs)


def pair_scores(query_rows, key_rows, length):
    pair_total, row_count, feat_count = query_rows.shape
    head_count = feat_count // HD
    key_count = key_rows.shape[1]
    scores = jnp.einsum(
        "pqhd,pkhd->pqhk",
        query_rows.reshape(pair_total, row_count, head_count, HD),
        key_rows.reshape(pair_total, key_count, head_count, HD),
        preferred_element_type=jnp.float32,
    ) * HD ** (-0.5)
    valid_keys = (jnp.arange(key_count, dtype=jnp.int32)[None, :] < length[:, None])[
        :, None, None, :
    ]
    return (jnp.where(valid_keys, scores, NEG_FILL), valid_keys)


def pair_forward(query_rows, key_rows, value_rows, length):
    pair_total, row_count, feat_count = query_rows.shape
    head_count = feat_count // HD
    scores, valid_keys = pair_scores(query_rows, key_rows, length)
    peak_score = jnp.max(scores, axis=3)
    exp_score = jnp.where(valid_keys, jnp.exp(scores - peak_score[..., None]), 0.0)
    exp_total = jnp.sum(exp_score, axis=3)
    partial_value = jnp.einsum(
        "pqhk,pkhd->pqhd",
        exp_score.astype(jnp.bfloat16),
        value_rows.reshape(pair_total, -1, head_count, HD),
        preferred_element_type=jnp.float32,
    )
    return (partial_value.reshape(pair_total, row_count, feat_count), peak_score, exp_total)


def pair_backward(query_rows, key_rows, value_rows, length, grad_rows, logsum, row_delta):
    pair_total, row_count, feat_count = query_rows.shape
    head_count = feat_count // HD
    key_count = key_rows.shape[1]
    scores, valid_keys = pair_scores(query_rows, key_rows, length)
    prob_full = jnp.where(valid_keys, jnp.exp(scores - logsum[..., None]), 0.0)
    grad_four = grad_rows.reshape(pair_total, row_count, head_count, HD)
    key_four = key_rows.reshape(pair_total, key_count, head_count, HD)
    value_four = value_rows.reshape(pair_total, key_count, head_count, HD)
    value_term = jnp.einsum(
        "pqhk,pqhd->pkhd",
        prob_full.astype(jnp.bfloat16),
        grad_four,
        preferred_element_type=jnp.float32,
    ).astype(jnp.bfloat16)
    grad_prob = jnp.einsum(
        "pqhd,pkhd->pqhk", grad_four, value_four, preferred_element_type=jnp.float32
    )
    dscore = (prob_full * (grad_prob - row_delta[..., None]) * HD ** (-0.5)).astype(jnp.bfloat16)
    query_term = jnp.einsum("pqhk,pkhd->pqhd", dscore, key_four, preferred_element_type=jnp.float32)
    key_term = jnp.einsum(
        "pqhk,pqhd->pkhd",
        dscore,
        query_rows.reshape(pair_total, row_count, head_count, HD),
        preferred_element_type=jnp.float32,
    ).astype(jnp.bfloat16)
    return (
        query_term.reshape(pair_total, row_count, feat_count),
        key_term.reshape(pair_total, key_count, feat_count),
        value_term.reshape(pair_total, key_count, feat_count),
    )


def merge_pairs(partial_value, peak_score, exp_total):
    pair_total, row_count, feat_count = partial_value.shape
    head_count = feat_count // HD
    group_total = pair_total // 2
    partial_value = partial_value.reshape(group_total, 2, row_count, head_count, HD)
    peak_score = peak_score.reshape(group_total, 2, row_count, head_count)
    exp_total = exp_total.reshape(group_total, 2, row_count, head_count)
    top_peak = jnp.max(peak_score, axis=1)
    factor = jnp.exp(peak_score - top_peak[:, None])
    norm_sum = jnp.sum(factor * exp_total, axis=1)
    mixed_rows = jnp.sum(factor[..., None] * partial_value, axis=1) / norm_sum[..., None]
    attended_al = mixed_rows.astype(jnp.bfloat16).reshape(group_total * row_count, feat_count)
    logsum = (top_peak + jnp.log(norm_sum)).reshape(group_total * row_count, head_count)
    return (attended_al, logsum)


def shards(hidden, query_weight, key_memory, value_memory, block_len, nbr_block, out_grad):
    tokens = hidden.shape[0]
    feat_count = query_weight.shape[1]
    head_count = feat_count // HD
    rim_rows = GROUP - 1
    peer_count = lax.axis_size("seq")
    group_total = tokens // GROUP
    pair_count = 2 * group_total
    seat_cap = (pair_count + peer_count - 1) // peer_count
    slot_count = peer_count * seat_cap
    owned_blocks = block_len.shape[0]
    zero_bf = jnp.zeros((), jnp.bfloat16)
    weight_full = lax.all_gather(query_weight, "seq", axis=0, tiled=True)
    queries = jnp.dot(hidden, weight_full, preferred_element_type=jnp.float32).astype(jnp.bfloat16)
    next_query, next_grad = from_behind((queries[:rim_rows], out_grad[:rim_rows]), "seq", -1)
    positions = lax.axis_index("seq") * tokens + jnp.arange(tokens, dtype=jnp.int32)
    live_tok = positions % SEQ_LEN >= rim_rows
    live_al = (positions + rim_rows) % SEQ_LEN >= rim_rows
    query_al = jnp.concatenate([queries[rim_rows:], next_query], 0)
    grad_al = jnp.where(
        live_al[:, None], jnp.concatenate([out_grad[rim_rows:], next_grad], 0), zero_bf
    )
    pair_blocks = nbr_block.reshape(pair_count)
    owner_of = pair_blocks // owned_blocks
    local_block = pair_blocks % owned_blocks
    pair_index = jnp.arange(pair_count, dtype=jnp.int32)
    earlier = jnp.sum(
        (owner_of[None, :] == owner_of[:, None]) & (pair_index[None, :] < pair_index[:, None]),
        axis=1,
    )
    slot_of = owner_of * seat_cap + earlier
    slot_hits = slot_of[None, :] == jnp.arange(slot_count, dtype=jnp.int32)[:, None]
    filled = jnp.any(slot_hits, axis=1)
    pair_of = jnp.sum(jnp.where(slot_hits, pair_index[None, :], 0), axis=1)
    request = jnp.where(
        filled, jnp.sum(jnp.where(slot_hits, local_block[None, :], 0), axis=1), -1
    ).reshape(peer_count, seat_cap)
    query_pairs = jnp.repeat(query_al.reshape(group_total, GROUP, feat_count), 2, axis=0)
    grad_pairs = jnp.repeat(grad_al.reshape(group_total, GROUP, feat_count), 2, axis=0)
    key_blocks = key_memory.reshape(owned_blocks, NLEN, feat_count)
    value_blocks = value_memory.reshape(owned_blocks, NLEN, feat_count)

    def place_slots(values):
        picked = jnp.take(values, pair_of, axis=0)
        shaped_mask = filled.reshape((slot_count,) + (1,) * (values.ndim - 1))
        return jnp.where(shaped_mask, picked, jnp.zeros((), values.dtype)).reshape(
            (peer_count, seat_cap) + values.shape[1:]
        )

    def collect(terms, sources):
        pick_rows = (sources[None, :] == jnp.arange(owned_blocks, dtype=jnp.int32)[:, None]).astype(
            jnp.bfloat16
        )
        summed = jnp.dot(
            pick_rows,
            terms.reshape(slot_count, NLEN * feat_count),
            preferred_element_type=jnp.float32,
        )
        return summed.astype(jnp.bfloat16).reshape(owned_blocks * NLEN, feat_count)

    asked_blocks = lax.all_to_all(request, "seq", split_axis=0, concat_axis=0, tiled=True).reshape(
        slot_count
    )
    safe_blocks = jnp.maximum(asked_blocks, 0)
    sent_keys = jnp.take(key_blocks, safe_blocks, axis=0).reshape(
        peer_count, seat_cap, NLEN, feat_count
    )
    sent_values = jnp.take(value_blocks, safe_blocks, axis=0).reshape(
        peer_count, seat_cap, NLEN, feat_count
    )
    sent_len = jnp.take(block_len, safe_blocks, axis=0).reshape(peer_count, seat_cap)
    rows_key, rows_value, rows_len = (
        lax.all_to_all(sent_keys, "seq", split_axis=0, concat_axis=0, tiled=True),
        lax.all_to_all(sent_values, "seq", split_axis=0, concat_axis=0, tiled=True),
        lax.all_to_all(sent_len, "seq", split_axis=0, concat_axis=0, tiled=True),
    )
    pair_keys = jnp.take(rows_key.reshape(slot_count, NLEN, feat_count), slot_of, axis=0)
    pair_values = jnp.take(rows_value.reshape(slot_count, NLEN, feat_count), slot_of, axis=0)
    pair_len = jnp.take(rows_len.reshape(slot_count), slot_of, axis=0)
    partial_value, peak_score, exp_total = pair_forward(
        query_pairs, pair_keys, pair_values, pair_len
    )
    attended_al, logsum = merge_pairs(partial_value, peak_score, exp_total)
    row_delta = jnp.sum(
        (grad_al.astype(jnp.float32) * attended_al.astype(jnp.float32)).reshape(
            tokens, head_count, HD
        ),
        axis=2,
    )
    logsum_pairs = jnp.repeat(logsum.reshape(group_total, GROUP, head_count), 2, axis=0)
    delta_pairs = jnp.repeat(row_delta.reshape(group_total, GROUP, head_count), 2, axis=0)
    logsum_pairs, delta_pairs = (logsum_pairs, delta_pairs)
    query_term, key_term, value_term = pair_backward(
        query_pairs, pair_keys, pair_values, pair_len, grad_pairs, logsum_pairs, delta_pairs
    )
    got_keys, got_values = (
        lax.all_to_all(place_slots(key_term), "seq", split_axis=0, concat_axis=0, tiled=True),
        lax.all_to_all(place_slots(value_term), "seq", split_axis=0, concat_axis=0, tiled=True),
    )
    d_key = collect(got_keys, asked_blocks)
    d_value = collect(got_values, asked_blocks)
    grad_query_al = (
        jnp.sum(query_term.reshape(group_total, 2, GROUP, feat_count), axis=1)
        .astype(jnp.bfloat16)
        .reshape(tokens, feat_count)
    )
    prev_attended, prev_grad = from_behind(
        (attended_al[tokens - rim_rows :], grad_query_al[tokens - rim_rows :]), "seq", 1
    )
    attended = jnp.where(
        live_tok[:, None],
        jnp.concatenate([prev_attended, attended_al[: tokens - rim_rows]], 0),
        zero_bf,
    )
    query_grad = jnp.where(
        live_tok[:, None],
        jnp.concatenate([prev_grad, grad_query_al[: tokens - rim_rows]], 0),
        zero_bf,
    )
    d_hidden = lax.psum_scatter(
        lax.dot_general(
            query_grad, weight_full, (((1,), (1,)), ((), ())), preferred_element_type=jnp.float32
        ).astype(jnp.bfloat16),
        "mp",
        scatter_dimension=0,
        tiled=True,
    )
    return (attended, d_hidden, d_key, d_value)


def solution(mesh):
    return jax.shard_map(
        shards,
        mesh=mesh,
        in_specs=(
            P("seq", None),
            P("seq", "mp"),
            P("seq", "mp"),
            P("seq", "mp"),
            P("seq"),
            P("seq", None),
            P("seq", "mp"),
        ),
        out_specs=(P("seq", "mp"), P(("seq", "mp"), None), P("seq", "mp"), P("seq", "mp")),
        check_vma=False,
    )
```

profile of v0, /device:TPU:2, one launch (start us, length us, event | category | flops | bytes accessed | tf_op | source)
XLA Modules:
  0.0 369.6 jit_solution(14449672935077774101)
XLA Ops:
  7.2 0.7 all-gather.2.cloned.1.call-update
  7.9 0.8 copy.116
  9.2 0.4 copy-done.8
  9.6 0.7 copy.117
  10.3 7.6 %all-to-all-start = ((s32[32,1,1]{2,1,0:T(1,128)}), s32[32,1,1]{2,1,0:T(1,128)S(1)}, u32[]{:S(2)}, u32[]{:S(2)}) async-start(s32[32,1,1]{2,1,0:T(1,128)} %copy.117), calls=%async_computation | async-start | bytes 32768 | tf_op jit(solution)/shard_map/all_to_all | solution.py:162
  17.9 1.3 fusion.44
  19.2 4.8 %all-to-all-done = s32[32,1,1]{2,1,0:T(1,128)S(1)} async-done(((s32[32,1,1]{2,1,0:T(1,128)}), s32[32,1,1]{2,1,0:T(1,128)S(1)}, u32[]{:S(2)}, u32[]{:S(2)}) %all-to-all-start) | async-done | bytes 160 | tf_op jit(solution)/shard_map/all_to_all | solution.py:162
  24.0 2.5 compare_select_fusion.1
  26.6 2.8 gather_fusion.3
  29.3 2.7 gather_fusion.1
  32.1 4.9 %all-to-all-start.1 = ((s32[32,1,1]{2,1,0:T(1,128)}), s32[32,1,1]{2,1,0:T(1,128)S(1)}, u32[]{:S(2)}, u32[]{:S(2)}) async-start(s32[32,1,1]{2,1,0:T(1,128)} %get-tuple-element.15), calls=%async_computation.1 | async-start | bytes 32768 | tf_op jit(solution)/shard_map/all_to_all | solution.py:176
  37.1 5.9 %select_bitcast_fusion = (bf16[32,1,128,512]{3,2,1,0:T(8,128)(2,1)}, bf16[32,1,128,512]{3,2,1,0:T(8,128)(2,1)}) fusion(bf16[32,128,512]{2,1,0:T(8,128)(2,1)} %gather_fusion.3, pred[32]{0:T(512)(128)(4,1)S(1)} %broadcast_compare_fusion, bf16[32,128,512]{2,1,0:T(8,128)(2,1)} %gather_fusion.1), kind=kLoop, calls=%fused_computation.14 | loop fusion | flops 4194304 | bytes 16777248 | tf_op jit(solution)/shard_map/reshape | solution.py:169
  43.0 0.3 all-to-all-done.1
  43.2 70.9 %all_to_all.32 = bf16[32,1,128,512]{3,2,1,0:T(8,128)(2,1)} all-to-all(bf16[32,1,128,512]{3,2,1,0:T(8,128)(2,1)} %get-tuple-element.21), channel_id=1, replica_groups=mesh['seq'=32,'mp'=8] {'seq'}, dimensions={0} | all-to-all | bytes 8388608 | tf_op jit(solution)/shard_map/all_to_all | solution.py:175
  114.1 7.7 %all-to-all-start.2 = ((bf16[32,1,128,512]{3,2,1,0:T(8,128)(2,1)}), bf16[32,1,128,512]{3,2,1,0:T(8,128)(2,1)}, u32[]{:S(2)}, u32[]{:S(2)}) async-start(bf16[32,1,128,512]{3,2,1,0:T(8,128)(2,1)} %get-tuple-element.22), calls=%async_computation.2 | async-start | bytes 8388608 | tf_op jit(solution)/shard_map/all_to_all | solution.py:174
  121.9 4.3 %collective-permute-start.2 = (bf16[63,512]{1,0:T(8,128)(2,1)S(1)}, bf16[63,512]{1,0:T(8,128)(2,1)S(1)}, u32[]{:S(2)}, u32[]{:S(2)}) collective-permute-start(bf16[63,512]{1,0:T(8,128)(2,1)S(1)} %slice.29), channel_id=1, source_target_pairs={{8,0},{16,8},{24,16},{32,24},{40,32},{48,40},{56,48},{64,56},{72,6... | collective-permute-start | bytes 193544 | tf_op jit(solution)/shard_map/ppermute | solution.py:18
  126.3 0.8 concatenate.25
  127.2 0.6 broadcast_in_dim.181
  127.8 0.6 pad_clamp_fusion
  128.4 0.6 compare_and_fusion
  129.0 0.7 reduce.4
  129.6 0.7 gather_fusion
  130.4 41.2 %collective-permute-done.2 = bf16[63,512]{1,0:T(8,128)(2,1)S(1)} collective-permute-done((bf16[63,512]{1,0:T(8,128)(2,1)S(1)}, bf16[63,512]{1,0:T(8,128)(2,1)S(1)}, u32[]{:S(2)}, u32[]{:S(2)}) %collective-permute-start.2) | collective-permute-done | bytes 64544 | tf_op jit(solution)/shard_map/ppermute | solution.py:18
  171.7 0.9 reshape_reshape.16
  172.6 0.7 concatenate.26
  173.3 2.8 gather_fusion.4
  176.1 2.8 gather_fusion.2
  179.0 7.0 %convolution_convert_fusion.5 = bf16[256,512]{1,0:T(8,128)(2,1)S(1)} fusion(bf16[256,8192]{1,0:T(8,128)(2,1)} %param.13, bf16[8192,512]{1,0:T(8,128)(2,1)} %all-gather.2.cloned.1.call-done), kind=kOutput, calls=%fused_computation.27 | convolution fusion | flops 2147614720 | bytes 12845056 | tf_op jit(solution)/shard_map/dot_general | solution.py:115
  186.0 6.5 %collective-permute-start = (bf16[63,512]{1,0:T(8,128)(2,1)S(1)}, bf16[63,512]{1,0:T(8,128)(2,1)S(1)}, u32[]{:S(2)}, u32[]{:S(2)}) collective-permute-start(bf16[63,512]{1,0:T(8,128)(2,1)S(1)} %slice.50), channel_id=1, source_target_pairs={{8,0},{16,8},{24,16},{32,24},{40,32},{48,40},{56,48},{64,56},{72,6... | collective-permute-start | bytes 193544 | tf_op jit(solution)/shard_map/ppermute | solution.py:18
  192.4 1.3 broadcast_select_fusion
  193.7 1.6 copy.119
  195.4 1.3 copy.122
  196.9 0.5 fusion.45
  197.5 0.7 fusion.8
  198.3 2.7 multiply_reduce_fusion
  201.1 3.7 %multiply_reduce_fusion.1 = f32[256,4]{1,0:T(8,128)} fusion(bf16[63,4,128]{2,1,0:T(4,128)(2,1)} %concatenate.26, bf16[193,4,128]{2,1,0:T(4,128)(2,1)S(1)} %copy-done.4, pred[256]{0:T(512)(128)(4,1)S(1)} %copy-done.11, f32[256,4]{1,0:T(8,128)S(1)} %bitcast.116, f32[256,4,128]{2,0,1:T(8,128)S(1)} %bitcast.108), kind=kLoop, calls=%fused_computation.38 | loop fusion | flops 1047552 | bytes 794880 | tf_op jit(solution)/shard_map/reduce_sum | solution.py:185
  204.8 1.0 copy.132
  205.8 2.9 convolution_convert_fusion.3
  208.7 2.0 fusion.7
  210.8 0.8 convolution_bitcast_fusion.1
  211.6 1.5 convolution_convert_fusion.4
  213.1 1.7 copy.134
  214.7 1.6 reshape_reshape.17
  216.5 1.9 collective-permute-start.3
  218.4 0.5 copy.139
  219.0 1.5 copy.136
  220.5 2.9 gather_fusion.6
  223.4 3.0 gather_fusion.5
  226.4 6.0 %fusion = (bf16[32,1,128,512]{3,2,1,0:T(8,128)(2,1)}, bf16[32,1,128,512]{3,2,1,0:T(8,128)(2,1)}) fusion(bf16[32,128,512]{2,1,0:T(8,128)(2,1)} %gather_fusion.6, pred[32]{0:T(512)(128)(4,1)S(1)} %copy-done.10, pred[32]{0:T(512)(128)(4,1)S(1)} %copy-done.9, bf16[32,128,512]{2,1,0:T(8,128)(2,1)} %gather_fusion.5), kind=kLoop, calls=%fused_computation.11 | loop fusion | flops 8388608 | bytes 16777280 | tf_op jit(solution)/shard_map/reshape | solution.py:147
  232.4 6.1 %all-to-all-start.4 = ((bf16[32,1,128,512]{3,2,1,0:T(8,128)(2,1)}), bf16[32,1,128,512]{3,2,1,0:T(8,128)(2,1)}, u32[]{:S(2)}, u32[]{:S(2)}) async-start(bf16[32,1,128,512]{3,2,1,0:T(8,128)(2,1)} %get-tuple-element.18), calls=%async_computation.5 | async-start | bytes 8388608 | tf_op jit(solution)/shard_map/all_to_all | solution.py:198
  238.6 7.7 %convolution_convert_fusion.2 = bf16[256,8192]{1,0:T(8,128)(2,1)} fusion(bf16[8192,512]{1,0:T(8,128)(2,1)} %all-gather.2.cloned.1.call-done, bf16[193,512]{1,0:T(8,128)(2,1)S(1)} %slice.54, bf16[63,512]{1,0:T(8,128)(2,1)S(1)} %collective-permute-done.3, pred[256]{0:T(512)(128)(4,1)S(1)} %fusion.35), kind=kOutput, calls=%fused_computation.9 | convolution fusion | flops 2150236160 | bytes 12845312 | tf_op jit(solution)/shard_map/dot_general | solution.py:222
  246.4 42.4 %all-to-all-done.4 = bf16[32,1,128,512]{3,2,1,0:T(8,128)(2,1)} async-done(((bf16[32,1,128,512]{3,2,1,0:T(8,128)(2,1)}), bf16[32,1,128,512]{3,2,1,0:T(8,128)(2,1)}, u32[]{:S(2)}, u32[]{:S(2)}) %all-to-all-start.4) | async-done | bytes 4194336 | tf_op jit(solution)/shard_map/all_to_all | solution.py:198
  288.8 9.4 %all-to-all-start.5 = ((bf16[32,1,128,512]{3,2,1,0:T(8,128)(2,1)}), bf16[32,1,128,512]{3,2,1,0:T(8,128)(2,1)}, u32[]{:S(2)}, u32[]{:S(2)}) async-start(bf16[32,1,128,512]{3,2,1,0:T(8,128)(2,1)} %get-tuple-element.17), calls=%async_computation.6 | async-start | bytes 8388608 | tf_op jit(solution)/shard_map/all_to_all | solution.py:199
  298.1 0.2 divide_convert_fusion
  298.4 0.2 copy.124
  298.6 2.1 collective-permute-start.1
  300.7 48.9 %collective-permute-done.1 = bf16[63,512]{1,0:T(8,128)(2,1)S(1)} collective-permute-done((bf16[63,512]{1,0:T(8,128)(2,1)S(1)}, bf16[63,512]{1,0:T(8,128)(2,1)S(1)}, u32[]{:S(2)}, u32[]{:S(2)}) %collective-permute-start.1) | collective-permute-done | bytes 64544 | tf_op jit(solution)/shard_map/ppermute | solution.py:18
  349.6 0.8 maximum_select_fusion
  350.5 4.6 %copy.150 = bf16[4,8,128,512]{3,1,2,0:T(8,128)(2,1)S(1)} copy(bf16[4,8,128,512]{3,2,1,0:T(8,128)(2,1)} %bitcast.47) | data formatting | bytes 8388608
  355.0 0.7 convolution_convert_fusion.1
  355.7 0.9 reshape.449
  356.6 4.6 %copy.151 = bf16[4,8,128,512]{3,1,2,0:T(8,128)(2,1)S(1)} copy(bf16[4,8,128,512]{3,2,1,0:T(8,128)(2,1)} %bitcast.50) | data formatting | bytes 8388608
  361.2 0.7 convolution_convert_fusion
  361.9 0.9 reshape.453
  (74 shorter events, 1.8 us)
Async XLA Ops:
  7.2 19.4 %copy-start = (bf16[256,512]{1,0:T(8,128)(2,1)S(1)}, bf16[256,512]{1,0:T(8,128)(2,1)}, u32[]{:S(2)}) copy-start(bf16[256,512]{1,0:T(8,128)(2,1)} %param.16) | copy-start | bytes 786436
  7.2 171.8 %all-gather.2.cloned.1.call-start = ((), (), s32[]{:S(2)}) async-start(), calls=%async_computation.7 | async-start | bytes 8650752 | tf_op jit(solution)/shard_map/all_gather | solution.py:114
  9.1 0.5 copy-start.8
  10.3 13.7 %all-to-all-start = ((s32[32,1,1]{2,1,0:T(1,128)}), s32[32,1,1]{2,1,0:T(1,128)S(1)}, u32[]{:S(2)}, u32[]{:S(2)}) async-start(s32[32,1,1]{2,1,0:T(1,128)} %copy.117), calls=%async_computation | async-start | bytes 32768 | tf_op jit(solution)/shard_map/all_to_all | solution.py:162
  26.5 10.5 %copy-start.6 = (s32[32]{0:T(128)}, s32[32]{0:T(128)S(1)}, u32[]{:S(2)}) copy-start(s32[32]{0:T(128)S(1)} %get-tuple-element.16) | copy-start | bytes 388
  26.5 2.8 copy-start.2
  32.1 11.1 %all-to-all-start.1 = ((s32[32,1,1]{2,1,0:T(1,128)}), s32[32,1,1]{2,1,0:T(1,128)S(1)}, u32[]{:S(2)}, u32[]{:S(2)}) async-start(s32[32,1,1]{2,1,0:T(1,128)} %get-tuple-element.15), calls=%async_computation.1 | async-start | bytes 32768 | tf_op jit(solution)/shard_map/all_to_all | solution.py:176
  114.1 7.7 %copy-start.5 = (bf16[256,512]{1,0:T(8,128)(2,1)S(1)}, bf16[256,512]{1,0:T(8,128)(2,1)}, u32[]{:S(2)}) copy-start(bf16[256,512]{1,0:T(8,128)(2,1)} %param.19) | copy-start | bytes 786436
  114.1 62.0 %all-to-all-start.2 = ((bf16[32,1,128,512]{3,2,1,0:T(8,128)(2,1)}), bf16[32,1,128,512]{3,2,1,0:T(8,128)(2,1)}, u32[]{:S(2)}, u32[]{:S(2)}) async-start(bf16[32,1,128,512]{3,2,1,0:T(8,128)(2,1)} %get-tuple-element.22), calls=%async_computation.2 | async-start | bytes 8388608 | tf_op jit(solution)/shard_map/all_to_all | solution.py:174
  121.9 49.7 %collective-permute-start.2 = (bf16[63,512]{1,0:T(8,128)(2,1)S(1)}, bf16[63,512]{1,0:T(8,128)(2,1)S(1)}, u32[]{:S(2)}, u32[]{:S(2)}) collective-permute-start(bf16[63,512]{1,0:T(8,128)(2,1)S(1)} %slice.29), channel_id=1, source_target_pairs={{8,0},{16,8},{24,16},{32,24},{40,32},{48,40},{56,48},{64,56},{72,6... | collective-permute-start | bytes 193544 | tf_op jit(solution)/shard_map/ppermute | solution.py:18
  186.0 10.7 %collective-permute-start = (bf16[63,512]{1,0:T(8,128)(2,1)S(1)}, bf16[63,512]{1,0:T(8,128)(2,1)S(1)}, u32[]{:S(2)}, u32[]{:S(2)}) collective-permute-start(bf16[63,512]{1,0:T(8,128)(2,1)S(1)} %slice.50), channel_id=1, source_target_pairs={{8,0},{16,8},{24,16},{32,24},{40,32},{48,40},{56,48},{64,56},{72,6... | collective-permute-start | bytes 193544 | tf_op jit(solution)/shard_map/ppermute | solution.py:18
  196.8 4.3 %copy-start.4 = (bf16[193,4,128]{2,1,0:T(4,128)(2,1)S(1)}, bf16[193,4,128]{2,1,0:T(4,128)(2,1)}, u32[]{:S(2)}) copy-start(bf16[193,4,128]{2,1,0:T(4,128)(2,1)} %concatenate.25) | copy-start | bytes 592900
  196.8 4.3 %copy-start.11 = (pred[256]{0:T(512)(128)(4,1)S(1)}, pred[256]{0:T(512)(128)(4,1)}, u32[]{:S(2)}) copy-start(pred[256]{0:T(512)(128)(4,1)} %broadcast_in_dim.181) | copy-start | bytes 772
  211.6 6.9 %copy-start.3 = (bf16[8,4,128,128]{3,2,1,0:T(8,128)(2,1)S(1)}, bf16[8,4,128,128]{3,2,1,0:T(8,128)(2,1)}, u32[]{:S(2)}) copy-start(bf16[8,4,128,128]{3,2,1,0:T(8,128)(2,1)} %convolution_convert_fusion.3) | copy-start | bytes 3145732
  216.5 22.1 %collective-permute-start.3 = (bf16[63,512]{1,0:T(8,128)(2,1)S(1)}, bf16[63,512]{1,0:T(8,128)(2,1)S(1)}, u32[]{:S(2)}, u32[]{:S(2)}) collective-permute-start(bf16[63,512]{1,0:T(8,128)(2,1)S(1)} %slice.53), channel_id=1, source_target_pairs={{0,8},{8,16},{16,24},{24,32},{32,40},{40,48},{48,56},{56,64},{64,7... | collective-permute-start | bytes 193544 | tf_op jit(solution)/shard_map/ppermute | solution.py:18
  223.4 3.0 copy-start.9
  223.4 3.0 copy-start.10
  232.4 56.4 %all-to-all-start.4 = ((bf16[32,1,128,512]{3,2,1,0:T(8,128)(2,1)}), bf16[32,1,128,512]{3,2,1,0:T(8,128)(2,1)}, u32[]{:S(2)}, u32[]{:S(2)}) async-start(bf16[32,1,128,512]{3,2,1,0:T(8,128)(2,1)} %get-tuple-element.18), calls=%async_computation.5 | async-start | bytes 8388608 | tf_op jit(solution)/shard_map/all_to_all | solution.py:198
  238.5 124.3 %reduce-scatter.2.cloned.1.call-start = ((), (), s32[]{:S(2)}) async-start(), calls=%async_computation.8 | async-start | bytes 4718592 | tf_op jit(solution)/shard_map/reduce_scatter | solution.py:221
  288.8 67.8 %all-to-all-start.5 = ((bf16[32,1,128,512]{3,2,1,0:T(8,128)(2,1)}), bf16[32,1,128,512]{3,2,1,0:T(8,128)(2,1)}, u32[]{:S(2)}, u32[]{:S(2)}) async-start(bf16[32,1,128,512]{3,2,1,0:T(8,128)(2,1)} %get-tuple-element.17), calls=%async_computation.6 | async-start | bytes 8388608 | tf_op jit(solution)/shard_map/all_to_all | solution.py:199
  298.6 51.0 %collective-permute-start.1 = (bf16[63,512]{1,0:T(8,128)(2,1)S(1)}, bf16[63,512]{1,0:T(8,128)(2,1)S(1)}, u32[]{:S(2)}, u32[]{:S(2)}) collective-permute-start(bf16[63,512]{1,0:T(8,128)(2,1)S(1)} %slice.51), channel_id=1, source_target_pairs={{0,8},{8,16},{16,24},{24,32},{32,40},{40,48},{48,56},{56,64},{64,7... | collective-permute-start | bytes 193544 | tf_op jit(solution)/shard_map/ppermute | solution.py:18
  350.5 4.6 %copy-start.7 = (s32[32]{0:T(128)S(1)}, s32[32]{0:T(128)}, u32[]{:S(2)}) copy-start(s32[32]{0:T(128)} %copy-done.6) | copy-start | bytes 388
  356.6 6.2 %copy-start.1 = (bf16[256,512]{1,0:T(8,128)(2,1)S(1)}, bf16[256,512]{1,0:T(8,128)(2,1)}, u32[]{:S(2)}) copy-start(bf16[256,512]{1,0:T(8,128)(2,1)} %param.16) | copy-start | bytes 786436
Sparse Core Ops, SparseCore 0:
  10.6 104.0 all-gather.1
  246.5 56.5 reduce-scatter.1
where the time goes:
time: 371 us; the launch traced here: 370 us
  waiting for transfers between devices  138 us (37%)
  blocking collectives  70.9 us (19%)
  starting transfers between devices  50.6 us (14%)
  local copies, waits for them, and re-layouts  45.1 us (12%)
  matrix products  26.5 us (7%)
  other arithmetic  23.8 us (6%)
  between operations  14.5 us (4%)
    ppermute x4, waiting for transfers between devices, from_behind(): return lax.ppermute(shard, axis, pairs)  90.1 us
    all_to_all x1, blocking collectives, shards(): lax.all_to_all(sent_values, 'seq', split_axis=0, concat_axis=0, tiled=True)  70.9 us
    all_to_all x1, waiting for transfers between devices, shards(): lax.all_to_all(place_slots(key_term), 'seq', split_axis=0, concat_axis=0,...  42.4 us
    ppermute x4, starting transfers between devices, from_behind(): return lax.ppermute(shard, axis, pairs)  14.8 us
    unnamed x28, local copies, waits for them, and re-layouts  10.5 us
    all_to_all x1, starting transfers between devices, shards(): lax.all_to_all(place_slots(value_term), 'seq', split_axis=0, concat_axis=...  9.35 us
    dot_general x1, matrix products, shards(): lax.dot_general(query_grad, weight_full, (((1,), (1,)), ((), ())), prefer...  7.74 us
    all_to_all x1, starting transfers between devices, shards(): lax.all_to_all(sent_keys, 'seq', split_axis=0, concat_axis=0, tiled=True)  7.71 us
  transfers between devices with their start and end apart: 11, of which 5 were waited for; matrix products, arithmetic and copies ran while one was open for 18% of the time, Pallas kernels for 0%

commit v1 on v0

v1 whole, which is shorter than its diff:
```python
import functools

import jax
import jax.numpy as jnp
from jax import lax
from jax.experimental import pallas as pl
from jax.experimental.pallas import tpu as pltpu
from jax.sharding import PartitionSpec as P

HD = 128
GROUP = 64
NLEN = 128
SEQ_LEN = 2048
RIM = GROUP - 1
NX, NY, NC = 4, 4, 2
NS = NX * NY * NC
NM = 8
TOK = 256
FT = 512
DM = 8192
HALF = FT // 2
NH = FT // HD
NP = 8
NB = 64
RQ = 4
QR = NLEN // RQ
BF = jnp.bfloat16
F32 = jnp.float32
NEG_FILL = -1e30
MIB = 1 << 20


def hop(v, dx=0, dy=0, dc=0):
    pairs = []
    for x in range(NX):
        for y in range(NY):
            for c in range(NC):
                to = (((x + dx) % NX) * NY + (y + dy) % NY) * NC + (c ^ dc)
                pairs.append(((x * NY + y) * NC + c, to))
    return lax.ppermute(v, "seq", pairs)


def to_seq(v, by):
    return lax.ppermute(v, "seq", [(i, (i + by) % NS) for i in range(NS)])


def ring4(v, axis):
    def go(u, d):
        return hop(u, dx=d) if axis == 0 else hop(u, dy=d)

    low, high = go(v, 1), go(v, -1)
    half = v.shape[0] // 2
    far = jnp.concatenate([go(low[:half], 1), go(high[half:], -1)], 0)
    return low, far, high


OFF = (0, -1, -2, 1)


def gather_weight(w):
    left, right = w[:, :HALF], w[:, HALF:]
    a1 = jnp.concatenate((left,) + ring4(left, 0), 0).reshape(4, 256, HALF)
    b1 = jnp.concatenate((right,) + ring4(right, 1), 0).reshape(4, 256, HALF)
    a2 = jnp.concatenate((a1,) + ring4(a1, 1), 0)
    b2 = jnp.concatenate((b1,) + ring4(b1, 0), 0)
    return a2, b2, hop(a2, dc=1), hop(b2, dc=1)


def query_kernel(chip, core, hid, ao, asb, bo, bsb, out, acc):
    k = pl.program_id(0)

    @pl.when(k == 0)
    def _():
        acc[...] = jnp.zeros_like(acc)

    c = core[0]
    ho = hid[:, pl.ds(pl.multiple_of(c * 256, 256), 256)]
    hs = hid[:, pl.ds(pl.multiple_of((1 - c) * 256, 256), 256)]

    def dot(p, r):
        return jnp.dot(p, r, preferred_element_type=F32)

    acc[:, :HALF] += dot(ho, ao[0]) + dot(hs, asb[0])
    acc[:, HALF:] += dot(ho, bo[0]) + dot(hs, bsb[0])

    @pl.when(k == pl.num_programs(0) - 1)
    def _():
        out[...] = acc[...].astype(BF)


def weight_specs():
    first = pl.BlockSpec((1, 256, HALF), lambda k, *_: (k, 0, 0))
    second = pl.BlockSpec((1, 256, HALF), lambda k, *_: ((k % 4) * 4 + k // 4, 0, 0))
    return [first, first, second, second]


def project(hidden, chips, core, ao, asb, bo, bsb):
    return pl.pallas_call(
        query_kernel,
        out_shape=jax.ShapeDtypeStruct((TOK, FT), BF),
        grid_spec=pltpu.PrefetchScalarGridSpec(
            num_scalar_prefetch=2,
            grid=(NX * NY,),
            in_specs=[pl.BlockSpec((TOK, 512), lambda k, chip, core: (0, chip[k]))] + weight_specs(),
            out_specs=pl.BlockSpec((TOK, FT), lambda k, *_: (0, 0)),
            scratch_shapes=[pltpu.VMEM((TOK, FT), F32)],
        ),
        compiler_params=pltpu.CompilerParams(vmem_limit_bytes=16 * MIB),
        cost_estimate=pl.CostEstimate(flops=2 * TOK * DM * FT, bytes_accessed=12 * MIB, transcendentals=0),
    )(chips, core, hidden, ao, asb, bo, bsb)


def pick_kernel(ids, table, out):
    def step(p, _):
        out[p] = table[ids[p]]
        return 0

    lax.fori_loop(0, NS * NP, step, 0, unroll=8)


def pick(ids, table):
    return pl.pallas_call(
        pick_kernel,
        out_shape=jax.ShapeDtypeStruct((NS * NP, QR, HD), BF),
        in_specs=[pl.BlockSpec(memory_space=pltpu.SMEM), pl.BlockSpec(memory_space=pltpu.VMEM)],
        out_specs=pl.BlockSpec(memory_space=pltpu.VMEM),
        compiler_params=pltpu.CompilerParams(vmem_limit_bytes=16 * MIB),
    )(ids, table)


def total_kernel(ids, terms, out, acc):
    acc[...] = jnp.zeros_like(acc)

    def step(p, _):
        b = ids[p]
        acc[b] = acc[b] + terms[p].astype(F32)
        return 0

    lax.fori_loop(0, NS * NP, step, 0, unroll=4)
    out[...] = acc[...].astype(BF)


def total(ids, terms):
    return pl.pallas_call(
        total_kernel,
        out_shape=jax.ShapeDtypeStruct((NB, QR, HD), BF),
        in_specs=[pl.BlockSpec(memory_space=pltpu.SMEM), pl.BlockSpec(memory_space=pltpu.VMEM)],
        out_specs=pl.BlockSpec(memory_space=pltpu.VMEM),
        scratch_shapes=[pltpu.VMEM((NB, QR, HD), F32)],
        compiler_params=pltpu.CompilerParams(vmem_limit_bytes=16 * MIB),
    )(ids, terms)


def attend_kernel(mine, lens, last, q, qn, g, gn, kv, att, gq, terms):
    def mm(p, r, dims):
        return lax.dot_general(p, r, (dims, ((), ())), preferred_element_type=F32)

    row = lax.broadcasted_iota(jnp.int32, (TOK, TOK + GROUP), 0)
    col = lax.broadcasted_iota(jnp.int32, (TOK, TOK + GROUP), 1)
    shift = (col == row + RIM).astype(F32).astype(BF)
    q_ext = jnp.concatenate([q[...], qn[...]], 0)
    g_next = gn[...]
    g_next = jnp.where(last[0] == 1, jnp.zeros_like(g_next), g_next)
    g_ext = jnp.concatenate([g[...], g_next], 0)
    q_al = mm(shift, q_ext, ((1,), (0,))).astype(BF)
    g_al = mm(shift, g_ext, ((1,), (0,))).astype(BF)
    scale = HD ** (-0.5)
    lane = lax.broadcasted_iota(jnp.int32, (GROUP, 2 * NLEN), 1)
    for grp in range(TOK // GROUP):
        rows = slice(grp * GROUP, (grp + 1) * GROUP)
        qg, gg = q_al[rows], g_al[rows]
        keys = jnp.concatenate([kv[0, 0, r, 2 * grp + n] for n in range(2) for r in range(RQ)], 0)
        vals = jnp.concatenate([kv[1, 0, r, 2 * grp + n] for n in range(2) for r in range(RQ)], 0)
        len0 = lens[mine[2 * grp]]
        len1 = lens[mine[2 * grp + 1]]
        valid = lane < jnp.where(lane < NLEN, len0, len1 + NLEN)
        scores = jnp.where(valid, mm(qg, keys, ((1,), (1,))) * scale, NEG_FILL)
        top = jnp.max(scores, axis=1, keepdims=True)
        ex = jnp.where(valid, jnp.exp(scores - top), 0.0)
        norm = jnp.sum(ex, axis=1, keepdims=True)
        inv = 1.0 / norm
        out = (mm(ex.astype(BF), vals, ((1,), (0,))) * inv).astype(BF)
        att[rows, :] = out
        delta = jnp.sum(gg.astype(F32) * out.astype(F32), axis=1, keepdims=True)
        prob = ex * inv
        grad_prob = mm(gg, vals, ((1,), (1,)))
        ds = (prob * (grad_prob - delta) * scale).astype(BF)
        gq[rows, :] = mm(ds, keys, ((1,), (0,))).astype(BF)
        vt = mm(prob.astype(BF), gg, ((0,), (0,))).astype(BF)
        kt = mm(ds, qg, ((0,), (0,))).astype(BF)
        for n in range(2):
            for r in range(RQ):
                part = slice((n * RQ + r) * QR, (n * RQ + r + 1) * QR)
                terms[0, 0, r, 2 * grp + n] = kt[part]
                terms[1, 0, r, 2 * grp + n] = vt[part]


def attend(mine, lens, last, q, qn, g, gn, kv):
    tok = pl.BlockSpec((TOK, HD), lambda h, *_: (0, h))
    rim = pl.BlockSpec((GROUP, HD), lambda h, *_: (0, h))
    mem = pl.BlockSpec((2, 1, RQ, NP, QR, HD), lambda h, *_: (0, h, 0, 0, 0, 0))
    rows = jax.ShapeDtypeStruct((TOK, FT), BF)
    return pl.pallas_call(
        attend_kernel,
        out_shape=(rows, rows, jax.ShapeDtypeStruct((2, NH, RQ, NP, QR, HD), BF)),
        grid_spec=pltpu.PrefetchScalarGridSpec(
            num_scalar_prefetch=3,
            grid=(NH,),
            in_specs=[tok, rim, tok, rim, mem],
            out_specs=(tok, tok, mem),
        ),
        compiler_params=pltpu.CompilerParams(vmem_limit_bytes=24 * MIB),
        cost_estimate=pl.CostEstimate(flops=400_000_000, bytes_accessed=6 * MIB, transcendentals=TOK * NLEN * 2 * NH),
    )(mine, lens, last, q, qn, g, gn, kv)


def hidden_kernel(lo, chip, order, core, gq, tail, ao, asb, bo, bsb, out, rows):
    count = rows.shape[0]
    k = pl.program_id(0)

    def mm(p, r, dims):
        return lax.dot_general(p, r, (dims, ((), ())), preferred_element_type=F32)

    @pl.when(k == 0)
    def _():
        ext = jnp.concatenate([gq[...], tail[...]], 0)
        base = lax.broadcasted_iota(jnp.int32, (32, TOK + GROUP), 0)
        col = lax.broadcasted_iota(jnp.int32, (32, TOK + GROUP), 1)
        first = order[NM]
        for part in range(count // 32):
            tok = base + order[lo + part] * 32
            src = jnp.where(tok < RIM, jnp.where(first == 1, -1, tok + (TOK + 1)), tok - RIM)
            pickm = (col == src).astype(F32).astype(BF)
            rows[part * 32 : (part + 1) * 32, :] = mm(pickm, ext, ((1,), (0,))).astype(BF)

    c = core[0]
    own = mm(rows[:, :HALF], ao[0], ((1,), (1,))) + mm(rows[:, HALF:], bo[0], ((1,), (1,)))
    sib = mm(rows[:, :HALF], asb[0], ((1,), (1,))) + mm(rows[:, HALF:], bsb[0], ((1,), (1,)))
    out[:, pl.ds(pl.multiple_of(c * 256, 256), 256)] = own.astype(BF)
    out[:, pl.ds(pl.multiple_of((1 - c) * 256, 256), 256)] = sib.astype(BF)


def hidden_part(lo, count, chips, order, core, gq, tail, ao, asb, bo, bsb):
    return pl.pallas_call(
        functools.partial(hidden_kernel, lo),
        out_shape=jax.ShapeDtypeStruct((count * 32, DM), BF),
        grid_spec=pltpu.PrefetchScalarGridSpec(
            num_scalar_prefetch=3,
            grid=(NX * NY,),
            in_specs=[
                pl.BlockSpec((TOK, FT), lambda k, *_: (0, 0)),
                pl.BlockSpec((GROUP, FT), lambda k, *_: (0, 0)),
            ]
            + weight_specs(),
            out_specs=pl.BlockSpec((count * 32, 512), lambda k, chip, *_: (0, chip[k])),
            scratch_shapes=[pltpu.VMEM((count * 32, FT), BF)],
        ),
        compiler_params=pltpu.CompilerParams(vmem_limit_bytes=16 * MIB),
        cost_estimate=pl.CostEstimate(flops=2 * 32 * count * DM * FT, bytes_accessed=12 * MIB, transcendentals=0),
    )(chips, order, core, gq, tail, ao, asb, bo, bsb)


def ring_pairs():
    pairs = []
    for s in range(NS):
        step = 1 if s % 2 == 0 else -1
        for m in range(NM):
            pairs.append((s * NM + m, s * NM + (m + step) % NM))
    return pairs


def around(v):
    return lax.ppermute(v, ("seq", "mp"), ring_pairs())


def swap_all(v):
    return lax.all_to_all(v, "seq", split_axis=0, concat_axis=0, tiled=True)


def shards(hidden, query_weight, key_memory, value_memory, block_len, nbr_block, out_grad):
    s = lax.axis_index("seq")
    m = lax.axis_index("mp")
    core = s % NC
    cx, cy = s // (NY * NC), (s // NC) % NY
    off = jnp.array(OFF, jnp.int32)
    chips = (((cx + off[None, :]) % NX) * NY + (cy + off[:, None]) % NY).reshape(-1).astype(jnp.int32)
    core1 = core.reshape(1).astype(jnp.int32)
    last = (s % 8 == 7).astype(jnp.int32).reshape(1)
    first = (s % 8 == 0).astype(jnp.int32).reshape(1)
    way = 1 - 2 * core
    order = (m - way * (1 + jnp.arange(NM, dtype=jnp.int32))) % NM
    order = jnp.concatenate([order, first]).astype(jnp.int32)
    mine = nbr_block.reshape(NP)

    def sliced(v):
        return v.reshape(2, RQ, QR, NH, HD).transpose(3, 1, 0, 2, 4).reshape(NH * RQ, 2 * QR, HD)

    meta = jnp.concatenate([mine, block_len]).astype(BF)
    meta = jnp.broadcast_to(jnp.pad(meta, (0, HD - NP - 2))[None, None, :], (NS, 16, HD))
    pay = jnp.concatenate([jnp.concatenate([sliced(key_memory), sliced(value_memory)], 0), meta], 1)
    held = swap_all(pay)
    table = held[:, : 2 * QR].reshape(NB, QR, HD)
    facts = held[:, 2 * QR, : NP + 2].astype(jnp.int32)
    ids = facts[:, :NP].reshape(NS * NP)
    lens = facts[:, NP:].reshape(NB)
    sent = pick(ids, table).reshape(NS, NP * QR, HD)
    kv = swap_all(sent).reshape(2, NH, RQ, NP, QR, HD)

    ao, bo, asb, bsb = gather_weight(query_weight)
    g_next = to_seq(out_grad[:GROUP], -1)
    queries = project(hidden, chips, core1, ao, asb, bo, bsb)
    q_next = to_seq(queries[:GROUP], -1)

    att_al, gq_al, terms = attend(mine, lens, last, queries, q_next, out_grad, g_next, kv)
    gq_tail = to_seq(gq_al[TOK - GROUP :], 1)
    att_tail = to_seq(att_al[TOK - GROUP :], 1)

    def part(lo, count):
        return hidden_part(lo, count, chips, order, core1, gq_al, gq_tail, ao, asb, bo, bsb)

    run = part(0, 1)
    rest = part(1, NM - 1)
    for k in range(NM - 1):
        run = around(run)
        run = (run.astype(F32) + rest[k * 32 : (k + 1) * 32].astype(F32)).astype(BF)

    got = swap_all(terms.reshape(NS, NP * QR, HD)).reshape(NS * NP, QR, HD)
    sums = total(ids, got).reshape(NS, 2 * QR, HD)
    back = swap_all(sums).reshape(2, NH, RQ, 2, QR, HD)
    grads = back.transpose(0, 3, 2, 4, 1, 5).reshape(2, 2 * NLEN, FT)

    dead = jnp.where(first[0] == 1, jnp.zeros((), BF), att_tail[1:])
    attended = jnp.concatenate([dead, att_al[: TOK - RIM]], 0)
    return attended, run, grads[0], grads[1]


def solution(mesh):
    return jax.shard_map(
        shards,
        mesh=mesh,
        in_specs=(
            P("seq", None),
            P("seq", "mp"),
            P("seq", "mp"),
            P("seq", "mp"),
            P("seq"),
            P("seq", None),
            P("seq", "mp"),
        ),
        out_specs=(P("seq", "mp"), P(("seq", "mp"), None), P("seq", "mp"), P("seq", "mp")),
        check_vma=False,
    )
```

time: 371 us -> 231 us (0.62)
  blocking collectives: 70.9 us -> 0 us
  waiting for transfers between devices: 138 us -> 83.1 us
  Pallas kernels: 0 us -> 51.2 us
  matrix products: 26.5 us -> 0 us
  local copies, waits for them, and re-layouts: 45.1 us -> 25.1 us
  other arithmetic: 23.8 us -> 7.03 us
  between operations: 14.5 us -> 1.12 us
  starting transfers between devices: 50.6 us -> 59.3 us
    all_to_all x1 -> x0, blocking collectives: 70.9 us -> none  [shards(): lax.all_to_all(sent_values, 'seq', split_axis=0, concat_axis=0, tiled=True)]
    pallas_call x0 -> x6, Pallas kernels: none -> 51.2 us  [the longest x2 24.7 us: hidden_part(): pl.pallas_call(functools.partial(hidden_kernel, lo), out_shape=jax.ShapeD...]
    all_to_all x5 -> x4, waiting for transfers between devices: 47.5 us -> 9.49 us  [swap_all(): return lax.all_to_all(v, 'seq', split_axis=0, concat_axis=0, tiled=True)]
    dot_general x10 -> x0, matrix products: 26.5 us -> none  [the longest x1 7.74 us: shards(): lax.dot_general(query_grad, weight_full, (((1,), (1,)), ((), ())), prefer...]
    gather x8 -> x0, local copies, waits for them, and re-layouts: 19 us -> none  [the longest x2 5.9 us: place_slots(): picked = jnp.take(values, pair_of, axis=0)]
    ppermute x4 -> x29, waiting for transfers between devices: 90.1 us -> 73.6 us  [the longest x4 34.5 us: to_seq(): return lax.ppermute(v, 'seq', [(i, (i + by) % NS) for i in range(NS)])]
    ppermute x4 -> x29, starting transfers between devices: 14.8 us -> 30.7 us  [the longest x18 22 us: hop(): return lax.ppermute(v, 'seq', pairs)]
    reshape x2 -> x0, other arithmetic: 11.9 us -> none  [the longest x1 5.98 us: place_slots(): jnp.where(shaped_mask, picked, jnp.zeros((), values.dtype))]
  transfers between devices with their start and end apart: 11 -> 33, of which waited for: 5 -> 13; matrix products, arithmetic and copies ran while one was open for 18% -> 11% of each run, Pallas kernels for 0% -> 13%
where the time goes in v1:
time: 231 us; the launch traced here: 227 us
  waiting for transfers between devices  83.1 us (36%)
  starting transfers between devices  59.3 us (26%)
  Pallas kernels  51.2 us (22%)
  local copies, waits for them, and re-layouts  25.1 us (11%)
  other arithmetic  7.03 us (3%)
    ppermute x4, waiting for transfers between devices, to_seq(): return lax.ppermute(v, 'seq', [(i, (i + by) % NS) for i in range(NS)])  34.5 us
    ppermute x7, waiting for transfers between devices, around(): return lax.ppermute(v, ('seq', 'mp'), ring_pairs())  33 us
    all_to_all x4, starting transfers between devices, swap_all(): return lax.all_to_all(v, 'seq', split_axis=0, concat_axis=0, tiled=True)  28.6 us
    pallas_call x2, Pallas kernels, hidden_part(): pl.pallas_call(functools.partial(hidden_kernel, lo), out_shape=jax.ShapeD...  24.7 us
    ppermute x18, starting transfers between devices, hop(): return lax.ppermute(v, 'seq', pairs)  22 us
    unnamed x35, local copies, waits for them, and re-layouts  14.9 us
    pallas_call x1, Pallas kernels, project(): pl.pallas_call(query_kernel, out_shape=jax.ShapeDtypeStruct((TOK, FT), BF...  12.2 us
    pallas_call x1, Pallas kernels, attend(): pl.pallas_call(attend_kernel, out_shape=(rows, rows, jax.ShapeDtypeStruct...  10.8 us
  transfers between devices with their start and end apart: 33, of which 13 were waited for; matrix products, arithmetic and copies ran while one was open for 11% of the time, Pallas kernels for 13%

profile of v1, /device:TPU:2, one launch (start us, length us, event | category | flops | bytes accessed | tf_op | source)
XLA Modules:
  0.0 226.9 jit_solution(2804690984091585321)
XLA Ops:
  0.7 1.8 fusion.6
  2.4 3.0 %collective-permute-start.11 = (bf16[256,256]{1,0:T(8,128)(2,1)S(1)}, bf16[256,256]{1,0:T(8,128)(2,1)S(1)}, u32[]{:S(2)}, u32[]{:S(2)}) collective-permute-start(bf16[256,256]{1,0:T(8,128)(2,1)S(1)} %get-tuple-element.12), channel_id=1, source_target_pairs={{0,48},{8,56},{16,0},{24,8},{32,16},{40,24},{48,32},{56,40},{64,11... | collective-permute-start | bytes 393224 | tf_op jit(solution)/shard_map/ppermute | solution.py:40
  5.4 1.3 collective-permute-start.2
  6.7 0.7 collective-permute-start
  7.5 0.7 collective-permute-done.11
  8.2 3.7 %collective-permute-start.12 = (bf16[128,256]{1,0:T(8,128)(2,1)S(1)}, bf16[128,256]{1,0:T(8,128)(2,1)S(1)}, u32[]{:S(2)}, u32[]{:S(2)}) collective-permute-start(bf16[128,256]{1,0:T(8,128)(2,1)S(1)} %slice.125), channel_id=1, source_target_pairs={{0,48},{8,56},{16,0},{24,8},{32,16},{40,24},{48,32},{56,40},{64,11... | collective-permute-start | bytes 196616 | tf_op jit(solution)/shard_map/ppermute | solution.py:40
  12.7 1.6 collective-permute-start.1
  14.2 0.7 constant_dynamic-update-slice_fusion.13
  14.9 0.7 constant_dynamic-update-slice_fusion.3
  15.5 1.9 collective-permute-done.10
  17.5 0.6 constant_dynamic-update-slice_fusion.12
  18.1 0.6 constant_dynamic-update-slice_fusion.11
  18.7 0.7 constant_dynamic-update-slice_fusion.10
  19.4 1.5 collective-permute-start.13
  20.9 0.6 constant_dynamic-update-slice_fusion.2
  21.5 0.6 constant_dynamic-update-slice_fusion.1
  22.1 0.7 constant_dynamic-update-slice_fusion
  22.8 1.3 collective-permute-start.6
  24.1 0.7 collective-permute-start.4
  24.8 1.6 collective-permute-start.15
  27.1 0.9 pad_maximum_fusion
  28.0 6.9 %all-to-all-start = ((bf16[32,80,128]{2,1,0:T(8,128)(2,1)}), bf16[32,80,128]{2,1,0:T(8,128)(2,1)S(1)}, u32[]{:S(2)}, u32[]{:S(2)}) async-start(bf16[32,80,128]{2,1,0:T(8,128)(2,1)} %pad_maximum_fusion), calls=%async_computation | async-start | bytes 1310720 | tf_op jit(solution)/shard_map/all_to_all | solution.py:277
  34.8 1.1 constant_dynamic-update-slice_fusion.9
  35.9 1.0 slice.126
  36.9 1.5 collective-permute-start.14
  38.4 1.9 constant_dynamic-update-slice_fusion.19
  40.3 2.8 %collective-permute-start.7 = (bf16[2,256,256]{2,1,0:T(8,128)(2,1)S(1)}, bf16[2,256,256]{2,1,0:T(8,128)(2,1)S(1)}, u32[]{:S(2)}, u32[]{:S(2)}) collective-permute-start(bf16[2,256,256]{2,1,0:T(8,128)(2,1)S(1)} %slice.123), channel_id=1, source_target_pairs={{0,48},{8,56},{16,0},{24,8},{32,16},{40,24},{48,32},{56,40},{64,11... | collective-permute-start | bytes 786440 | tf_op jit(solution)/shard_map/ppermute | solution.py:40
  43.1 1.0 slice.122
  44.4 1.0 slice.127
  45.9 1.1 constant_dynamic-update-slice_fusion.8
  47.0 1.9 constant_dynamic-update-slice_fusion.18
  48.9 0.8 constant_dynamic-update-slice_fusion.17
  49.7 3.5 %collective-permute-done.16 = bf16[2,256,256]{2,1,0:T(8,128)(2,1)S(1)} collective-permute-done((bf16[2,256,256]{2,1,0:T(8,128)(2,1)S(1)}, bf16[2,256,256]{2,1,0:T(8,128)(2,1)S(1)}, u32[]{:S(2)}, u32[]{:S(2)}) %collective-permute-start.16) | collective-permute-done | bytes 262176 | tf_op jit(solution)/shard_map/ppermute | solution.py:40
  53.2 0.7 constant_dynamic-update-slice_fusion.16
  54.0 1.9 constant_dynamic-update-slice_fusion.15.bo
  56.7 1.0 shard_map.112
  57.7 1.3 copy-done.1
  59.1 7.5 %all-to-all-start.1 = ((bf16[32,256,128]{2,1,0:T(8,128)(2,1)}), bf16[32,256,128]{2,1,0:T(8,128)(2,1)}, u32[]{:S(2)}, u32[]{:S(2)}) async-start(bf16[32,256,128]{2,1,0:T(8,128)(2,1)} %bitcast.31), calls=%async_computation.1 | async-start | bytes 4194304 | tf_op jit(solution)/shard_map/all_to_all | solution.py:277
  66.6 2.5 %collective-permute-start.19 = (bf16[64,512]{1,0:T(8,128)(2,1)S(1)}, bf16[64,512]{1,0:T(8,128)(2,1)S(1)}, u32[]{:S(2)}, u32[]{:S(2)}) collective-permute-start(bf16[64,512]{1,0:T(8,128)(2,1)S(1)} %slice.102), channel_id=1, source_target_pairs={{0,248},{8,0},{16,8},{24,16},{32,24},{40,32},{48,40},{56,48},{64,5... | collective-permute-start | bytes 196616 | tf_op jit(solution)/shard_map/ppermute | solution.py:44
  69.3 2.2 copy-done.2
  71.5 12.2 %shard_map.111.q = bf16[256,512]{1,0:T(8,128)(2,1)S(1)} custom-call(s32[16]{0:T(128)S(1)} %add.101.chip, s32[1]{0:T(128)} %bitcast.6.core, bf16[256,8192]{1,0:T(8,128)(2,1)S(1)} %copy-done.2, bf16[16,256,256]{2,1,0:T(8,128)(2,1)S(1)} %constant_dynamic-update-slice_fusion.5.ao, bf16[16,256,256]{2,1,0:T(8,128)(2,1)} %collective-permute-done.8.asb, ...), custom_call_target="tpu_custom_call" | custom-call | flops 2147483648 | bytes 12582912 | tf_op jit(solution)/shard_map/pallas_call | solution.py:98
  84.3 6.3 %collective-permute-done.19.gn = bf16[64,512]{1,0:T(8,128)(2,1)S(1)} collective-permute-done((bf16[64,512]{1,0:T(8,128)(2,1)S(1)}, bf16[64,512]{1,0:T(8,128)(2,1)S(1)}, u32[]{:S(2)}, u32[]{:S(2)}) %collective-permute-start.19) | collective-permute-done | bytes 65568 | tf_op jit(solution)/shard_map/ppermute | solution.py:44
  90.7 2.0 all-to-all-done.1
  92.7 10.8 %shard_map.113 = (bf16[256,512]{1,0:T(8,128)(2,1)S(1)}, bf16[256,512]{1,0:T(8,128)(2,1)S(1)}, bf16[2,4,4,8,32,128]{5,4,3,2,1,0:T(8,128)(2,1)S(1)}) custom-call(s32[8]{0:T(128)S(1)} %reshape.96.mine, s32[64]{0:T(128)S(1)} %reshape.101.lens, s32[1]{0:T(128)} %bitcast.5.last, bf16[256,512]{1,0:T(8,128)(2,1)S(1)} %shard_map.111.q, ...), custom_call_target="tpu_custom_call" | custom-call | flops 400000000 | bytes 6291456 | tf_op jit(solution)/shard_map/pallas_call | solution.py:203
  104.0 5.4 %collective-permute-done.21.tail = bf16[64,512]{1,0:T(8,128)(2,1)S(1)} collective-permute-done((bf16[64,512]{1,0:T(8,128)(2,1)S(1)}, bf16[64,512]{1,0:T(8,128)(2,1)S(1)}, u32[]{:S(2)}, u32[]{:S(2)}) %collective-permute-start.21) | collective-permute-done | bytes 65568 | tf_op jit(solution)/shard_map/ppermute | solution.py:44
  109.4 11.8 %shard_map.114 = bf16[32,8192]{1,0:T(8,128)(2,1)S(1)} custom-call(s32[16]{0:T(128)S(1)} %add.101.chip, s32[9]{0:T(128)S(1)} %pad_add_fusion.order, s32[1]{0:T(128)} %bitcast.6.core, bf16[256,512]{1,0:T(8,128)(2,1)S(1)} %get-tuple-element.8.gq, bf16[64,512]{1,0:T(8,128)(2,1)S(1)} %collective-permute-done.21.tail, ...), custom_call_target="tpu_custom_call" | custom-call | flops 268435456 | bytes 12582912 | tf_op jit(solution)/shard_map/pallas_call | solution.py:244
  121.2 2.0 collective-permute-start.22
  123.2 12.9 %shard_map.115 = bf16[224,8192]{1,0:T(8,128)(2,1)S(1)} custom-call(s32[16]{0:T(128)S(1)} %add.101.chip, s32[9]{0:T(128)S(1)} %pad_add_fusion.order, s32[1]{0:T(128)} %bitcast.6.core, bf16[256,512]{1,0:T(8,128)(2,1)S(1)} %get-tuple-element.8.gq, bf16[64,512]{1,0:T(8,128)(2,1)S(1)} %collective-permute-done.21.tail, ...), custom_call_target="tpu_custom_call" | custom-call | flops 1879048192 | bytes 12582912 | tf_op jit(solution)/shard_map/pallas_call | solution.py:244
  136.2 2.0 collective-permute-start.23
  138.2 9.2 %collective-permute-done.23 = bf16[32,8192]{1,0:T(8,128)(2,1)S(1)} collective-permute-done((bf16[32,8192]{1,0:T(8,128)(2,1)S(1)}, bf16[32,8192]{1,0:T(8,128)(2,1)S(1)}, u32[]{:S(2)}, u32[]{:S(2)}) %collective-permute-start.23) | collective-permute-done | bytes 524320 | tf_op jit(solution)/shard_map/ppermute | solution.py:273
  147.6 10.4 %collective-permute-done.24 = bf16[32,8192]{1,0:T(8,128)(2,1)S(1)} collective-permute-done((bf16[32,8192]{1,0:T(8,128)(2,1)S(1)}, bf16[32,8192]{1,0:T(8,128)(2,1)S(1)}, u32[]{:S(2)}, u32[]{:S(2)}) %collective-permute-start.24) | collective-permute-done | bytes 524320 | tf_op jit(solution)/shard_map/ppermute | solution.py:273
  158.2 10.4 %collective-permute-done.25 = bf16[32,8192]{1,0:T(8,128)(2,1)S(1)} collective-permute-done((bf16[32,8192]{1,0:T(8,128)(2,1)S(1)}, bf16[32,8192]{1,0:T(8,128)(2,1)S(1)}, u32[]{:S(2)}, u32[]{:S(2)}) %collective-permute-start.25) | collective-permute-done | bytes 524320 | tf_op jit(solution)/shard_map/ppermute | solution.py:273
  169.0 8.0 %all-to-all-start.2 = ((bf16[32,256,128]{2,1,0:T(8,128)(2,1)}), bf16[32,256,128]{2,1,0:T(8,128)(2,1)S(1)}, u32[]{:S(2)}, u32[]{:S(2)}) async-start(bf16[32,256,128]{2,1,0:T(8,128)(2,1)} %bitcast.34), calls=%async_computation.2 | async-start | bytes 4194304 | tf_op jit(solution)/shard_map/all_to_all | solution.py:277
  177.1 2.4 %collective-permute-done.26 = bf16[32,8192]{1,0:T(8,128)(2,1)} collective-permute-done((bf16[32,8192]{1,0:T(8,128)(2,1)S(1)}, bf16[32,8192]{1,0:T(8,128)(2,1)}, u32[]{:S(2)}, u32[]{:S(2)}) %collective-permute-start.26) | collective-permute-done | bytes 524320 | tf_op jit(solution)/shard_map/ppermute | solution.py:273
  179.5 1.3 add_convert_fusion.2
  180.9 0.6 collective-permute-start.20
  181.6 22.8 %collective-permute-done.20 = bf16[64,512]{1,0:T(8,128)(2,1)S(1)} collective-permute-done((bf16[64,512]{1,0:T(8,128)(2,1)S(1)}, bf16[64,512]{1,0:T(8,128)(2,1)S(1)}, u32[]{:S(2)}, u32[]{:S(2)}) %collective-permute-start.20) | collective-permute-done | bytes 65568 | tf_op jit(solution)/shard_map/ppermute | solution.py:44
  204.4 2.5 %shard_map.116 = bf16[64,32,128]{2,1,0:T(8,128)(2,1)} custom-call(s32[256]{0:T(256)S(1)} %reshape.107.ids, bf16[256,32,128]{2,1,0:T(8,128)(2,1)S(1)} %bitcast.32), custom_call_target="tpu_custom_call" | custom-call | tf_op jit(solution)/shard_map/pallas_call | solution.py:144
  206.9 6.2 %all-to-all-start.3 = ((bf16[32,64,128]{2,1,0:T(8,128)(2,1)}), bf16[32,64,128]{2,1,0:T(8,128)(2,1)S(1)}, u32[]{:S(2)}, u32[]{:S(2)}) async-start(bf16[32,64,128]{2,1,0:T(8,128)(2,1)} %bitcast.15), calls=%async_computation.3 | async-start | bytes 1048576 | tf_op jit(solution)/shard_map/all_to_all | solution.py:277
  213.1 1.3 add_convert_fusion.1
  214.6 0.8 pad_maximum_fusion.1
  215.4 7.5 %all-to-all-done.3 = bf16[32,64,128]{2,1,0:T(8,128)(2,1)S(1)} async-done(((bf16[32,64,128]{2,1,0:T(8,128)(2,1)}), bf16[32,64,128]{2,1,0:T(8,128)(2,1)S(1)}, u32[]{:S(2)}, u32[]{:S(2)}) %all-to-all-start.3) | async-done | bytes 524320 | tf_op jit(solution)/shard_map/all_to_all | solution.py:277
  223.5 0.9 copy_bitcast_fusion.1
  224.9 2.0 add_convert_fusion
  (93 shorter events, 6.8 us)
Async XLA Ops:
  0.6 25.9 %copy-start.9 = (s32[2]{0:T(128)S(1)}, s32[2]{0:T(128)}, u32[]{:S(2)}) copy-start(s32[2]{0:T(128)} %param.12) | copy-start | bytes 28
  0.6 25.9 %copy-start.7 = (s32[4,2]{0,1:T(2,128)S(1)}, s32[4,2]{0,1:T(2,128)}, u32[]{:S(2)}) copy-start(s32[4,2]{0,1:T(2,128)} %param.13) | copy-start | bytes 100
  0.7 26.0 %copy-start.5 = (bf16[256,512]{1,0:T(8,128)(2,1)S(1)}, bf16[256,512]{1,0:T(8,128)(2,1)}, u32[]{:S(2)}) copy-start(bf16[256,512]{1,0:T(8,128)(2,1)} %param.10) | copy-start | bytes 786436
  0.7 26.2 %copy-start.6 = (bf16[256,512]{1,0:T(8,128)(2,1)S(1)}, bf16[256,512]{1,0:T(8,128)(2,1)}, u32[]{:S(2)}) copy-start(bf16[256,512]{1,0:T(8,128)(2,1)} %param.11) | copy-start | bytes 786436
  2.4 5.8 %collective-permute-start.11 = (bf16[256,256]{1,0:T(8,128)(2,1)S(1)}, bf16[256,256]{1,0:T(8,128)(2,1)S(1)}, u32[]{:S(2)}, u32[]{:S(2)}) collective-permute-start(bf16[256,256]{1,0:T(8,128)(2,1)S(1)} %get-tuple-element.12), channel_id=1, source_target_pairs={{0,48},{8,56},{16,0},{24,8},{32,16},{40,24},{48,32},{56,40},{64,11... | collective-permute-start | bytes 393224 | tf_op jit(solution)/shard_map/ppermute | solution.py:40
  5.4 6.5 %collective-permute-start.9 = (bf16[256,256]{1,0:T(8,128)(2,1)S(1)}, bf16[256,256]{1,0:T(8,128)(2,1)S(1)}, u32[]{:S(2)}, u32[]{:S(2)}) collective-permute-start(bf16[256,256]{1,0:T(8,128)(2,1)S(1)} %get-tuple-element.12), channel_id=1, source_target_pairs={{0,16},{8,24},{16,32},{24,40},{32,48},{40,56},{48,0},{56,8},{64,80... | collective-permute-start | bytes 393224 | tf_op jit(solution)/shard_map/ppermute | solution.py:40
  5.4 6.6 %collective-permute-start.2 = (bf16[256,256]{1,0:T(8,128)(2,1)S(1)}, bf16[256,256]{1,0:T(8,128)(2,1)S(1)}, u32[]{:S(2)}, u32[]{:S(2)}) collective-permute-start(bf16[256,256]{1,0:T(8,128)(2,1)S(1)} %get-tuple-element.15), channel_id=1, source_target_pairs={{0,192},{8,200},{16,208},{24,216},{32,224},{40,232},{48,240},{56,2... | collective-permute-start | bytes 393224 | tf_op jit(solution)/shard_map/ppermute | solution.py:40
  6.7 5.9 %collective-permute-start = (bf16[256,256]{1,0:T(8,128)(2,1)S(1)}, bf16[256,256]{1,0:T(8,128)(2,1)S(1)}, u32[]{:S(2)}, u32[]{:S(2)}) collective-permute-start(bf16[256,256]{1,0:T(8,128)(2,1)S(1)} %get-tuple-element.15), channel_id=1, source_target_pairs={{0,64},{8,72},{16,80},{24,88},{32,96},{40,104},{48,112},{56,120},{... | collective-permute-start | bytes 393224 | tf_op jit(solution)/shard_map/ppermute | solution.py:40
  8.2 9.9 %collective-permute-start.12 = (bf16[128,256]{1,0:T(8,128)(2,1)S(1)}, bf16[128,256]{1,0:T(8,128)(2,1)S(1)}, u32[]{:S(2)}, u32[]{:S(2)}) collective-permute-start(bf16[128,256]{1,0:T(8,128)(2,1)S(1)} %slice.125), channel_id=1, source_target_pairs={{0,48},{8,56},{16,0},{24,8},{32,16},{40,24},{48,32},{56,40},{64,11... | collective-permute-start | bytes 196616 | tf_op jit(solution)/shard_map/ppermute | solution.py:40
  11.9 5.6 %collective-permute-start.10 = (bf16[128,256]{1,0:T(8,128)(2,1)S(1)}, bf16[128,256]{1,0:T(8,128)(2,1)S(1)}, u32[]{:S(2)}, u32[]{:S(2)}) collective-permute-start(bf16[128,256]{1,0:T(8,128)(2,1)S(1)} %slice.124), channel_id=1, source_target_pairs={{0,16},{8,24},{16,32},{24,40},{32,48},{40,56},{48,0},{56,8},{64,80... | collective-permute-start | bytes 196616 | tf_op jit(solution)/shard_map/ppermute | solution.py:40
  12.0 9.5 %collective-permute-start.3 = (bf16[128,256]{1,0:T(8,128)(2,1)S(1)}, bf16[128,256]{1,0:T(8,128)(2,1)S(1)}, u32[]{:S(2)}, u32[]{:S(2)}) collective-permute-start(bf16[128,256]{1,0:T(8,128)(2,1)S(1)} %slice.121), channel_id=1, source_target_pairs={{0,192},{8,200},{16,208},{24,216},{32,224},{40,232},{48,240},{56,2... | collective-permute-start | bytes 196616 | tf_op jit(solution)/shard_map/ppermute | solution.py:40
  12.7 8.2 %collective-permute-start.1 = (bf16[128,256]{1,0:T(8,128)(2,1)S(1)}, bf16[128,256]{1,0:T(8,128)(2,1)S(1)}, u32[]{:S(2)}, u32[]{:S(2)}) collective-permute-start(bf16[128,256]{1,0:T(8,128)(2,1)S(1)} %slice.120), channel_id=1, source_target_pairs={{0,64},{8,72},{16,80},{24,88},{32,96},{40,104},{48,112},{56,120},{... | collective-permute-start | bytes 196616 | tf_op jit(solution)/shard_map/ppermute | solution.py:40
  19.4 16.5 %collective-permute-start.13 = (bf16[4,256,256]{2,1,0:T(8,128)(2,1)}, bf16[4,256,256]{2,1,0:T(8,128)(2,1)}, u32[]{:S(2)}, u32[]{:S(2)}) collective-permute-start(bf16[4,256,256]{2,1,0:T(8,128)(2,1)} %bitcast.8), channel_id=1, source_target_pairs={{0,64},{8,72},{16,80},{24,88},{32,96},{40,104},{48,112},{56,120},{... | collective-permute-start | bytes 1572872 | tf_op jit(solution)/shard_map/ppermute | solution.py:40
  22.8 17.5 %collective-permute-start.6 = (bf16[4,256,256]{2,1,0:T(8,128)(2,1)}, bf16[4,256,256]{2,1,0:T(8,128)(2,1)S(1)}, u32[]{:S(2)}, u32[]{:S(2)}) collective-permute-start(bf16[4,256,256]{2,1,0:T(8,128)(2,1)} %bitcast.7), channel_id=1, source_target_pairs={{0,48},{8,56},{16,0},{24,8},{32,16},{40,24},{48,32},{56,40},{64,11... | collective-permute-start | bytes 1572872 | tf_op jit(solution)/shard_map/ppermute | solution.py:40
  24.1 19.0 %collective-permute-start.4 = (bf16[4,256,256]{2,1,0:T(8,128)(2,1)}, bf16[4,256,256]{2,1,0:T(8,128)(2,1)}, u32[]{:S(2)}, u32[]{:S(2)}) collective-permute-start(bf16[4,256,256]{2,1,0:T(8,128)(2,1)} %bitcast.7), channel_id=1, source_target_pairs={{0,16},{8,24},{16,32},{24,40},{32,48},{40,56},{48,0},{56,8},{64,80... | collective-permute-start | bytes 1572872 | tf_op jit(solution)/shard_map/ppermute | solution.py:40
  24.8 19.5 %collective-permute-start.15 = (bf16[4,256,256]{2,1,0:T(8,128)(2,1)}, bf16[4,256,256]{2,1,0:T(8,128)(2,1)}, u32[]{:S(2)}, u32[]{:S(2)}) collective-permute-start(bf16[4,256,256]{2,1,0:T(8,128)(2,1)} %bitcast.8), channel_id=1, source_target_pairs={{0,192},{8,200},{16,208},{24,216},{32,224},{40,232},{48,240},{56,2... | collective-permute-start | bytes 1572872 | tf_op jit(solution)/shard_map/ppermute | solution.py:40
  28.0 28.6 %all-to-all-start = ((bf16[32,80,128]{2,1,0:T(8,128)(2,1)}), bf16[32,80,128]{2,1,0:T(8,128)(2,1)S(1)}, u32[]{:S(2)}, u32[]{:S(2)}) async-start(bf16[32,80,128]{2,1,0:T(8,128)(2,1)} %pad_maximum_fusion), calls=%async_computation | async-start | bytes 1310720 | tf_op jit(solution)/shard_map/all_to_all | solution.py:277
  36.9 12.0 %collective-permute-start.14 = (bf16[2,256,256]{2,1,0:T(8,128)(2,1)S(1)}, bf16[2,256,256]{2,1,0:T(8,128)(2,1)S(1)}, u32[]{:S(2)}, u32[]{:S(2)}) collective-permute-start(bf16[2,256,256]{2,1,0:T(8,128)(2,1)S(1)} %slice.126), channel_id=1, source_target_pairs={{0,64},{8,72},{16,80},{24,88},{32,96},{40,104},{48,112},{56,120},{... | collective-permute-start | bytes 786440 | tf_op jit(solution)/shard_map/ppermute | solution.py:40
  40.3 15.6 %collective-permute-start.7 = (bf16[2,256,256]{2,1,0:T(8,128)(2,1)S(1)}, bf16[2,256,256]{2,1,0:T(8,128)(2,1)S(1)}, u32[]{:S(2)}, u32[]{:S(2)}) collective-permute-start(bf16[2,256,256]{2,1,0:T(8,128)(2,1)S(1)} %slice.123), channel_id=1, source_target_pairs={{0,48},{8,56},{16,0},{24,8},{32,16},{40,24},{48,32},{56,40},{64,11... | collective-permute-start | bytes 786440 | tf_op jit(solution)/shard_map/ppermute | solution.py:40
  44.1 11.8 %collective-permute-start.5 = (bf16[2,256,256]{2,1,0:T(8,128)(2,1)S(1)}, bf16[2,256,256]{2,1,0:T(8,128)(2,1)S(1)}, u32[]{:S(2)}, u32[]{:S(2)}) collective-permute-start(bf16[2,256,256]{2,1,0:T(8,128)(2,1)S(1)} %slice.122), channel_id=1, source_target_pairs={{0,16},{8,24},{16,32},{24,40},{32,48},{40,56},{48,0},{56,8},{64,80... | collective-permute-start | bytes 786440 | tf_op jit(solution)/shard_map/ppermute | solution.py:40
  45.3 7.9 %collective-permute-start.16 = (bf16[2,256,256]{2,1,0:T(8,128)(2,1)S(1)}, bf16[2,256,256]{2,1,0:T(8,128)(2,1)S(1)}, u32[]{:S(2)}, u32[]{:S(2)}) collective-permute-start(bf16[2,256,256]{2,1,0:T(8,128)(2,1)S(1)} %slice.127), channel_id=1, source_target_pairs={{0,192},{8,200},{16,208},{24,216},{32,224},{40,232},{48,240},{56,2... | collective-permute-start | bytes 786440 | tf_op jit(solution)/shard_map/ppermute | solution.py:40
  55.9 13.4 %collective-permute-start.17 = (bf16[16,256,256]{2,1,0:T(8,128)(2,1)}, bf16[16,256,256]{2,1,0:T(8,128)(2,1)}, u32[]{:S(2)}, u32[]{:S(2)}) collective-permute-start(bf16[16,256,256]{2,1,0:T(8,128)(2,1)} %constant_dynamic-update-slice_fusion.15.bo), channel_id=1, source_target_pairs={{0,8},{8,0},{16,24},{24,16},{32,40},{40,32},{48,56},{56,48},{64,72... | collective-permute-start | bytes 6291464 | tf_op jit(solution)/shard_map/ppermute | solution.py:40
  56.0 13.3 %collective-permute-start.8 = (bf16[16,256,256]{2,1,0:T(8,128)(2,1)S(1)}, bf16[16,256,256]{2,1,0:T(8,128)(2,1)}, u32[]{:S(2)}, u32[]{:S(2)}) collective-permute-start(bf16[16,256,256]{2,1,0:T(8,128)(2,1)S(1)} %constant_dynamic-update-slice_fusion.5.ao), channel_id=1, source_target_pairs={{0,8},{8,0},{16,24},{24,16},{32,40},{40,32},{48,56},{56,48},{64,72... | collective-permute-start | bytes 6291464 | tf_op jit(solution)/shard_map/ppermute | solution.py:40
  57.7 1.3 copy-start.1
  59.0 7.5 %copy-start.4 = (bf16[256,512]{1,0:T(8,128)(2,1)S(1)}, bf16[256,512]{1,0:T(8,128)(2,1)}, u32[]{:S(2)}) copy-start(bf16[256,512]{1,0:T(8,128)(2,1)} %g.1) | copy-start | bytes 786436
  59.0 10.0 %copy-start.8 = (s32[4]{0:T(128)S(1)}, s32[4]{0:T(128)}, u32[]{:S(2)}) copy-start(s32[4]{0:T(128)} %constant.97.clone) | copy-start | bytes 52
  59.1 33.6 %all-to-all-start.1 = ((bf16[32,256,128]{2,1,0:T(8,128)(2,1)}), bf16[32,256,128]{2,1,0:T(8,128)(2,1)}, u32[]{:S(2)}, u32[]{:S(2)}) async-start(bf16[32,256,128]{2,1,0:T(8,128)(2,1)} %bitcast.31), calls=%async_computation.1 | async-start | bytes 4194304 | tf_op jit(solution)/shard_map/all_to_all | solution.py:277
  66.6 24.1 %collective-permute-start.19 = (bf16[64,512]{1,0:T(8,128)(2,1)S(1)}, bf16[64,512]{1,0:T(8,128)(2,1)S(1)}, u32[]{:S(2)}, u32[]{:S(2)}) collective-permute-start(bf16[64,512]{1,0:T(8,128)(2,1)S(1)} %slice.102), channel_id=1, source_target_pairs={{0,248},{8,0},{16,8},{24,16},{32,24},{40,32},{48,40},{56,48},{64,5... | collective-permute-start | bytes 196616 | tf_op jit(solution)/shard_map/ppermute | solution.py:44
  69.3 2.2 copy-start.2
  83.7 9.0 %collective-permute-start.18 = (bf16[64,512]{1,0:T(8,128)(2,1)S(1)}, bf16[64,512]{1,0:T(8,128)(2,1)S(1)}, u32[]{:S(2)}, u32[]{:S(2)}) collective-permute-start(bf16[64,512]{1,0:T(8,128)(2,1)S(1)} %slice.128), channel_id=1, source_target_pairs={{0,248},{8,0},{16,8},{24,16},{32,24},{40,32},{48,40},{56,48},{64,5... | collective-permute-start | bytes 196616 | tf_op jit(solution)/shard_map/ppermute | solution.py:44
  103.5 17.7 %copy-start.3 = (bf16[2,4,4,8,32,128]{5,4,3,2,1,0:T(8,128)(2,1)}, bf16[2,4,4,8,32,128]{5,4,3,2,1,0:T(8,128)(2,1)S(1)}, u32[]{:S(2)}) copy-start(bf16[2,4,4,8,32,128]{5,4,3,2,1,0:T(8,128)(2,1)S(1)} %get-tuple-element.9) | copy-start | bytes 6291460
  103.5 5.9 %collective-permute-start.21 = (bf16[64,512]{1,0:T(8,128)(2,1)S(1)}, bf16[64,512]{1,0:T(8,128)(2,1)S(1)}, u32[]{:S(2)}, u32[]{:S(2)}) collective-permute-start(bf16[64,512]{1,0:T(8,128)(2,1)S(1)} %slice.108), channel_id=1, source_target_pairs={{0,8},{8,16},{16,24},{24,32},{32,40},{40,48},{48,56},{56,64},{64,7... | collective-permute-start | bytes 196616 | tf_op jit(solution)/shard_map/ppermute | solution.py:44
  121.2 14.9 %collective-permute-start.22 = (bf16[32,8192]{1,0:T(8,128)(2,1)S(1)}, bf16[32,8192]{1,0:T(8,128)(2,1)S(1)}, u32[]{:S(2)}, u32[]{:S(2)}) collective-permute-start(bf16[32,8192]{1,0:T(8,128)(2,1)S(1)} %shard_map.114), channel_id=1, source_target_pairs={{0,1},{1,2},{2,3},{3,4},{4,5},{5,6},{6,7},{7,0},{8,15},{9,8},{10,9... | collective-permute-start | bytes 1572872 | tf_op jit(solution)/shard_map/ppermute | solution.py:273
  136.1 32.5 %copy-start = (bf16[224,8192]{1,0:T(8,128)(2,1)}, bf16[224,8192]{1,0:T(8,128)(2,1)S(1)}, u32[]{:S(2)}) copy-start(bf16[224,8192]{1,0:T(8,128)(2,1)S(1)} %shard_map.115) | copy-start | bytes 11010052
  136.2 11.2 %collective-permute-start.23 = (bf16[32,8192]{1,0:T(8,128)(2,1)S(1)}, bf16[32,8192]{1,0:T(8,128)(2,1)S(1)}, u32[]{:S(2)}, u32[]{:S(2)}) collective-permute-start(bf16[32,8192]{1,0:T(8,128)(2,1)S(1)} %add_convert_fusion.6), channel_id=1, source_target_pairs={{0,1},{1,2},{2,3},{3,4},{4,5},{5,6},{6,7},{7,0},{8,15},{9,8},{10,9... | collective-permute-start | bytes 1572872 | tf_op jit(solution)/shard_map/ppermute | solution.py:273
  147.5 10.5 %collective-permute-start.24 = (bf16[32,8192]{1,0:T(8,128)(2,1)S(1)}, bf16[32,8192]{1,0:T(8,128)(2,1)S(1)}, u32[]{:S(2)}, u32[]{:S(2)}) collective-permute-start(bf16[32,8192]{1,0:T(8,128)(2,1)S(1)} %add_convert_fusion.5), channel_id=1, source_target_pairs={{0,1},{1,2},{2,3},{3,4},{4,5},{5,6},{6,7},{7,0},{8,15},{9,8},{10,9... | collective-permute-start | bytes 1572872 | tf_op jit(solution)/shard_map/ppermute | solution.py:273
  158.1 10.5 %collective-permute-start.25 = (bf16[32,8192]{1,0:T(8,128)(2,1)S(1)}, bf16[32,8192]{1,0:T(8,128)(2,1)S(1)}, u32[]{:S(2)}, u32[]{:S(2)}) collective-permute-start(bf16[32,8192]{1,0:T(8,128)(2,1)S(1)} %add_convert_fusion.4), channel_id=1, source_target_pairs={{0,1},{1,2},{2,3},{3,4},{4,5},{5,6},{6,7},{7,0},{8,15},{9,8},{10,9... | collective-permute-start | bytes 1572872 | tf_op jit(solution)/shard_map/ppermute | solution.py:273
  168.7 10.8 %collective-permute-start.26 = (bf16[32,8192]{1,0:T(8,128)(2,1)S(1)}, bf16[32,8192]{1,0:T(8,128)(2,1)}, u32[]{:S(2)}, u32[]{:S(2)}) collective-permute-start(bf16[32,8192]{1,0:T(8,128)(2,1)S(1)} %add_convert_fusion.3), channel_id=1, source_target_pairs={{0,1},{1,2},{2,3},{3,4},{4,5},{5,6},{6,7},{7,0},{8,15},{9,8},{10,9... | collective-permute-start | bytes 1572872 | tf_op jit(solution)/shard_map/ppermute | solution.py:273
  169.0 35.4 %all-to-all-start.2 = ((bf16[32,256,128]{2,1,0:T(8,128)(2,1)}), bf16[32,256,128]{2,1,0:T(8,128)(2,1)S(1)}, u32[]{:S(2)}, u32[]{:S(2)}) async-start(bf16[32,256,128]{2,1,0:T(8,128)(2,1)} %bitcast.34), calls=%async_computation.2 | async-start | bytes 4194304 | tf_op jit(solution)/shard_map/all_to_all | solution.py:277
  180.8 32.3 %collective-permute-start.27 = (bf16[32,8192]{1,0:T(8,128)(2,1)S(1)}, bf16[32,8192]{1,0:T(8,128)(2,1)}, u32[]{:S(2)}, u32[]{:S(2)}) collective-permute-start(bf16[32,8192]{1,0:T(8,128)(2,1)S(1)} %add_convert_fusion.2), channel_id=1, source_target_pairs={{0,1},{1,2},{2,3},{3,4},{4,5},{5,6},{6,7},{7,0},{8,15},{9,8},{10,9... | collective-permute-start | bytes 1572872 | tf_op jit(solution)/shard_map/ppermute | solution.py:273
  180.9 23.4 %collective-permute-start.20 = (bf16[64,512]{1,0:T(8,128)(2,1)S(1)}, bf16[64,512]{1,0:T(8,128)(2,1)S(1)}, u32[]{:S(2)}, u32[]{:S(2)}) collective-permute-start(bf16[64,512]{1,0:T(8,128)(2,1)S(1)} %slice.105), channel_id=1, source_target_pairs={{0,8},{8,16},{16,24},{24,32},{32,40},{40,48},{48,56},{56,64},{64,7... | collective-permute-start | bytes 196616 | tf_op jit(solution)/shard_map/ppermute | solution.py:44
  206.9 16.0 %all-to-all-start.3 = ((bf16[32,64,128]{2,1,0:T(8,128)(2,1)}), bf16[32,64,128]{2,1,0:T(8,128)(2,1)S(1)}, u32[]{:S(2)}, u32[]{:S(2)}) async-start(bf16[32,64,128]{2,1,0:T(8,128)(2,1)} %bitcast.15), calls=%async_computation.3 | async-start | bytes 1048576 | tf_op jit(solution)/shard_map/all_to_all | solution.py:277
  214.5 10.5 %collective-permute-start.28 = (bf16[32,8192]{1,0:T(8,128)(2,1)S(1)}, bf16[32,8192]{1,0:T(8,128)(2,1)S(1)}, u32[]{:S(2)}, u32[]{:S(2)}) collective-permute-start(bf16[32,8192]{1,0:T(8,128)(2,1)S(1)} %add_convert_fusion.1), channel_id=1, source_target_pairs={{0,1},{1,2},{2,3},{3,4},{4,5},{5,6},{6,7},{7,0},{8,15},{9,8},{10,9... | collective-permute-start | bytes 1572872 | tf_op jit(solution)/shard_map/ppermute | solution.py:273

commit v2 on v1

v2 whole, which is shorter than its diff:
```python
import functools

import jax
import jax.numpy as jnp
from jax import lax
from jax.experimental import pallas as pl
from jax.experimental.pallas import tpu as pltpu
from jax.sharding import PartitionSpec as P

HD = 128
GROUP = 64
NLEN = 128
SEQ_LEN = 2048
RIM = GROUP - 1
NX, NY, NC = 4, 4, 2
NS = NX * NY * NC
NM = 8
TOK = 256
FT = 512
DM = 8192
HALF = FT // 2
NH = FT // HD
NP = 8
NB = 64
RQ = 4
QR = NLEN // RQ
BF = jnp.bfloat16
F32 = jnp.float32
NEG_FILL = -1e30
MIB = 1 << 20
WIDE = 56 * MIB


def hop(v, dx=0, dy=0, dc=0):
    pairs = []
    for x in range(NX):
        for y in range(NY):
            for c in range(NC):
                to = (((x + dx) % NX) * NY + (y + dy) % NY) * NC + (c ^ dc)
                pairs.append(((x * NY + y) * NC + c, to))
    return lax.ppermute(v, "seq", pairs)


def to_seq(v, by):
    return lax.ppermute(v, "seq", [(i, (i + by) % NS) for i in range(NS)])


def along(v, axis, by):
    return hop(v, dx=by) if axis == 0 else hop(v, dy=by)


OFF = (0, -1, -2, 1)


def near(v, axis):
    return along(v, axis, 1), along(v, axis, 2), along(v, axis, -1)


def prepare_kernel(mine, lens, key, value, w, g, pay, left, right, g_head):
    lane = lax.broadcasted_iota(jnp.int32, (16, HD), 1)
    meta = jnp.zeros((16, HD), jnp.int32)
    for i in range(NP):
        meta = jnp.where(lane == i, mine[i % 2, i // 2], meta)
    for i in range(2):
        meta = jnp.where(lane == NP + i, lens[i], meta)
    meta = meta.astype(F32).astype(BF)
    for which, ref in ((0, key), (1, value)):
        for h in range(NH):
            for r in range(RQ):
                j = (which * NH + h) * RQ + r
                for blk in range(2):
                    at = blk * NLEN + r * QR
                    pay[j, blk * QR : (blk + 1) * QR] = ref[at : at + QR, h * HD : (h + 1) * HD]
                pay[j, 2 * QR :] = meta
    left[...] = w[:, :HALF]
    right[...] = w[:, HALF:]
    g_head[...] = g[...]


def prepare(mine, lens, key, value, w, g):
    smem = pl.BlockSpec(memory_space=pltpu.SMEM)

    def full(*shape):
        return pl.BlockSpec(shape, lambda i: (0,) * len(shape))

    half = jax.ShapeDtypeStruct((256, HALF), BF)
    return pl.pallas_call(
        prepare_kernel,
        grid=(1,),
        out_shape=(
            jax.ShapeDtypeStruct((NS, 2 * QR + 16, HD), BF),
            half,
            half,
            jax.ShapeDtypeStruct((GROUP, FT), BF),
        ),
        in_specs=[smem, smem, full(256, FT), full(256, FT), full(256, FT), full(GROUP, FT)],
        out_specs=(full(NS, 2 * QR + 16, HD), full(256, HALF), full(256, HALF), full(GROUP, FT)),
        compiler_params=pltpu.CompilerParams(vmem_limit_bytes=WIDE),
    )(mine, lens, key, value, w, g)


def stack_kernel(*refs):
    a, b, oa, ob = refs[:4], refs[4:8], refs[8], refs[9]
    for i in range(4):
        oa[i] = a[i][...]
        ob[i] = b[i][...]


def stack(a, b):
    shape = jax.ShapeDtypeStruct((4, 256, HALF), BF)
    return pl.pallas_call(
        stack_kernel,
        out_shape=(shape, shape),
        compiler_params=pltpu.CompilerParams(vmem_limit_bytes=16 * MIB),
        cost_estimate=pl.CostEstimate(flops=0, bytes_accessed=2 * MIB, transcendentals=0),
    )(*a, *b)


def block_of(pieces, i, j):
    own, low, f0, f1, high = pieces
    if i == 0:
        return own[j]
    if i == 1:
        return low[j]
    if i == 2:
        return f0[j] if j < 2 else f1[j - 2]
    return high[j]


def join_kernel(*refs):
    a, b, out = refs[:5], refs[5:10], refs[10]
    for dy in range(4):
        for dx in range(4):
            out[dy * 4 + dx, :HALF] = block_of(a, dy, dx).T
            out[dy * 4 + dx, HALF:] = block_of(b, dx, dy).T


def join(a, b):
    return pl.pallas_call(
        join_kernel,
        out_shape=jax.ShapeDtypeStruct((NX * NY, FT, 256), BF),
        compiler_params=pltpu.CompilerParams(vmem_limit_bytes=WIDE),
        cost_estimate=pl.CostEstimate(flops=0, bytes_accessed=1024, transcendentals=0),
    )(*a, *b)


def query_kernel(chip, core, hid, hsib, *refs):
    a, b = refs[:5], refs[5:10]
    own, sib, own_head, sib_head, cols, acc, sems = refs[10:]
    c = core[0]

    def copies(k):
        src = pl.ds(pl.multiple_of(chip[k] * 512 + c * 256, 256), 256)
        dst = pl.ds(k * 256, 256)
        return (
            pltpu.make_async_copy(hid.at[:, src], cols.at[pl.ds(0, TOK), dst], sems.at[0, k]),
            pltpu.make_async_copy(hsib.at[:, src], cols.at[pl.ds(TOK, TOK), dst], sems.at[1, k]),
        )

    for k in range(16):
        for cp in copies(k):
            cp.start()
    for dy in range(4):
        for k in range(4 * dy, 4 * dy + 4):
            for cp in copies(k):
                cp.wait()
        left = jnp.concatenate([block_of(a, dy, dx) for dx in range(4)], 0)
        right = jnp.concatenate([block_of(b, dx, dy) for dx in range(4)], 0)
        h = cols[:, dy * 1024 : (dy + 1) * 1024]
        for n, w in ((0, left), (1, right)):
            part = jnp.dot(h, w, preferred_element_type=F32)
            if dy:
                part = part + acc[:, n * HALF : (n + 1) * HALF]
            acc[:, n * HALF : (n + 1) * HALF] = part
    own[...] = acc[:TOK]
    sib[...] = acc[TOK:]
    own_head[...] = acc[:GROUP]
    sib_head[...] = acc[TOK : TOK + GROUP]


def project(hidden, hsib, chips, core, a, b):
    whole = jax.ShapeDtypeStruct((TOK, FT), F32)
    head = jax.ShapeDtypeStruct((GROUP, FT), F32)
    smem = pl.BlockSpec(memory_space=pltpu.SMEM)
    hbm = pl.BlockSpec(memory_space=pl.ANY)
    vmem = pl.BlockSpec(memory_space=pltpu.VMEM)
    return pl.pallas_call(
        query_kernel,
        out_shape=(whole, whole, head, head),
        in_specs=[smem, smem, hbm, hbm] + [vmem] * 10,
        out_specs=(vmem,) * 4,
        scratch_shapes=[
            pltpu.VMEM((2 * TOK, DM // 2), BF),
            pltpu.VMEM((2 * TOK, FT), F32),
            pltpu.SemaphoreType.DMA((2, 16)),
        ],
        compiler_params=pltpu.CompilerParams(vmem_limit_bytes=WIDE),
        cost_estimate=pl.CostEstimate(flops=0, bytes_accessed=1024, transcendentals=0),
    )(chips, core, hidden, hsib, *a, *b)


def pick_kernel(facts, held, out):
    count = out.shape[0] // NP
    base = pl.program_id(0) * count

    def step(i, _):
        for n in range(NP):
            b = facts[base + i, n]
            at = pl.multiple_of(jnp.bitwise_and(b, 1) * QR, QR)
            out[i * NP + n] = held[lax.shift_right_logical(b, 1), pl.ds(at, QR)]
        return 0

    lax.fori_loop(0, count, step, 0, unroll=2)


def pick(facts, held):
    count = NS * NP // 2
    return pl.pallas_call(
        pick_kernel,
        out_shape=jax.ShapeDtypeStruct((NS * NP, QR, HD), BF),
        grid=(2,),
        in_specs=[pl.BlockSpec(memory_space=pltpu.SMEM), pl.BlockSpec(held.shape, lambda i: (0, 0, 0))],
        out_specs=pl.BlockSpec((count, QR, HD), lambda i: (i, 0, 0)),
        compiler_params=pltpu.CompilerParams(vmem_limit_bytes=WIDE),
        cost_estimate=pl.CostEstimate(flops=0, bytes_accessed=1024, transcendentals=0),
    )(facts, held)


def total_kernel(facts, terms, out, acc):
    acc[...] = jnp.zeros_like(acc)

    def step(i, _):
        for n in range(NP):
            b = facts[i, n]
            acc[b] = acc[b] + terms[i * NP + n].astype(F32)
        return 0

    lax.fori_loop(0, NS, step, 0, unroll=2)
    out[...] = acc[...].astype(BF)


def total(facts, terms):
    return pl.pallas_call(
        total_kernel,
        out_shape=jax.ShapeDtypeStruct((NB, QR, HD), BF),
        in_specs=[pl.BlockSpec(memory_space=pltpu.SMEM), pl.BlockSpec(memory_space=pltpu.VMEM)],
        out_specs=pl.BlockSpec(memory_space=pltpu.VMEM),
        scratch_shapes=[pltpu.VMEM((NB, QR, HD), F32)],
        compiler_params=pltpu.CompilerParams(vmem_limit_bytes=16 * MIB),
    )(facts, terms)


def attend_kernel(groups, mine, facts, last, qa, qb, na, nb, g, gn, kv, *rest):
    att, gq, terms = rest[-3:]

    def mm(p, r, dims):
        return lax.dot_general(p, r, (dims, ((), ())), preferred_element_type=F32)

    count = len(groups) * GROUP
    lo = groups[0] * GROUP
    ext = min(count + GROUP, TOK - lo)
    row = lax.broadcasted_iota(jnp.int32, (count, ext + GROUP), 0)
    col = lax.broadcasted_iota(jnp.int32, (count, ext + GROUP), 1)
    shift = (col == row + RIM).astype(F32).astype(BF)
    q_next = (na[...] + nb[...]).astype(BF)
    g_next = gn[...]
    g_next = jnp.where(last[0] == 1, jnp.zeros_like(g_next), g_next)
    q_ext = jnp.concatenate([(qa[lo : lo + ext] + qb[lo : lo + ext]).astype(BF), q_next], 0)
    g_ext = jnp.concatenate([g[lo : lo + ext], g_next], 0)
    q_al = mm(shift, q_ext, ((1,), (0,))).astype(BF)
    g_al = mm(shift, g_ext, ((1,), (0,))).astype(BF)
    scale = HD ** (-0.5)
    lane = lax.broadcasted_iota(jnp.int32, (GROUP, 2 * NLEN), 1)
    for i, grp in enumerate(groups):
        rows = slice(i * GROUP, (i + 1) * GROUP)
        qg, gg = q_al[rows], g_al[rows]
        keys = jnp.concatenate([kv[0, 0, r, 2 * i + n] for n in range(2) for r in range(RQ)], 0)
        vals = jnp.concatenate([kv[1, 0, r, 2 * i + n] for n in range(2) for r in range(RQ)], 0)
        blk0, blk1 = mine[0, grp], mine[1, grp]
        len0 = facts[lax.shift_right_logical(blk0, 1), NP + jnp.bitwise_and(blk0, 1)]
        len1 = facts[lax.shift_right_logical(blk1, 1), NP + jnp.bitwise_and(blk1, 1)]
        valid = lane < jnp.where(lane < NLEN, len0, len1 + NLEN)
        scores = jnp.where(valid, mm(qg, keys, ((1,), (1,))) * scale, NEG_FILL)
        top = jnp.max(scores, axis=1, keepdims=True)
        ex = jnp.where(valid, jnp.exp(scores - top), 0.0)
        norm = jnp.sum(ex, axis=1, keepdims=True)
        inv = 1.0 / norm
        out = (mm(ex.astype(BF), vals, ((1,), (0,))) * inv).astype(BF)
        att[rows, :] = out
        delta = jnp.sum(gg.astype(F32) * out.astype(F32), axis=1, keepdims=True)
        prob = ex * inv
        grad_prob = mm(gg, vals, ((1,), (1,)))
        ds = (prob * (grad_prob - delta) * scale).astype(BF)
        gq[rows, :] = mm(ds, keys, ((1,), (0,))).astype(BF)
        vt = mm(prob.astype(BF), gg, ((0,), (0,))).astype(BF)
        kt = mm(ds, qg, ((0,), (0,))).astype(BF)
        for n in range(2):
            for r in range(RQ):
                part = slice((n * RQ + r) * QR, (n * RQ + r + 1) * QR)
                terms[0, 0, r, 2 * i + n] = kt[part]
                terms[1, 0, r, 2 * i + n] = vt[part]


def attend(groups, mine, facts, last, qa, qb, na, nb, g, gn, kv, into=None):
    count = len(groups) * GROUP
    place = groups[0] // len(groups)
    tok = pl.BlockSpec((TOK, HD), lambda h, *_: (0, h))
    rim = pl.BlockSpec((GROUP, HD), lambda h, *_: (0, h))
    out = pl.BlockSpec((count, HD), lambda h, *_: (0, h))
    mem = pl.BlockSpec((2, 1, RQ, 2 * len(groups), QR, HD), lambda h, *_: (0, h, 0, place, 0, 0))
    rows = jax.ShapeDtypeStruct((count, FT), BF)
    specs, operands, alias = [tok, tok, rim, rim, tok, rim, mem], (qa, qb, na, nb, g, gn, kv), {}
    if into is not None:
        specs, operands, alias = specs + [pl.BlockSpec(memory_space=pl.ANY)], operands + (into,), {10: 2}
    return pl.pallas_call(
        functools.partial(attend_kernel, groups),
        out_shape=(rows, rows, jax.ShapeDtypeStruct((2, NH, RQ, NP, QR, HD), BF)),
        grid_spec=pltpu.PrefetchScalarGridSpec(
            num_scalar_prefetch=3,
            grid=(NH,),
            in_specs=specs,
            out_specs=(out, out, mem),
        ),
        input_output_aliases=alias,
        compiler_params=pltpu.CompilerParams(vmem_limit_bytes=WIDE),
        cost_estimate=pl.CostEstimate(
            flops=100_000_000 * len(groups), bytes_accessed=2 * MIB * len(groups), transcendentals=0
        ),
    )(mine, facts, last, *operands)


def hidden_kernel(lo, chip, order, core, gq, end, tail, wo, ws, left, right, *more):
    rows = more[-1]
    count = rows.shape[0] // 32
    k = pl.program_id(0)

    def mm(p, r):
        return jnp.dot(p, r, preferred_element_type=F32)

    @pl.when(k == 0)
    def _():
        ext = jnp.concatenate([gq[...], end[...], tail[...]], 0)
        base = lax.broadcasted_iota(jnp.int32, (32, TOK + GROUP), 0)
        col = lax.broadcasted_iota(jnp.int32, (32, TOK + GROUP), 1)
        first = order[NM]
        for part in range(count):
            tok = base + order[lo + part] * 32
            src = jnp.where(tok < RIM, jnp.where(first == 1, -1, tok + (TOK + 1)), tok - RIM)
            pickm = (col == src).astype(F32).astype(BF)
            rows[part * 32 : (part + 1) * 32, :] = mm(pickm, ext).astype(BF)

    c = core[0]
    for dx in range(4):
        place = chip[k * 4 + dx]
        half = place // 8
        own = mm(rows[...], wo[dx]).astype(BF)
        sib = mm(rows[...], ws[dx]).astype(BF)
        at = (place - 8 * half) * 512
        own_at = pl.ds(pl.multiple_of(at + c * 256, 256), 256)
        sib_at = pl.ds(pl.multiple_of(at + (1 - c) * 256, 256), 256)

        @pl.when(half == 0)
        def _():
            left[:, own_at] = own
            left[:, sib_at] = sib
            if count > 1:
                more[0][:, own_at] = own[32:64]
                more[0][:, sib_at] = sib[32:64]

        @pl.when(half == 1)
        def _():
            right[:, own_at] = own
            right[:, sib_at] = sib
            if count > 1:
                more[1][:, own_at] = own[:32]
                more[1][:, sib_at] = sib[:32]


def hidden_part(lo, count, chips, order, core, gq, end, tail, wo, ws):
    shape = jax.ShapeDtypeStruct((count * 32, DM // 2), BF)
    half = pl.BlockSpec((count * 32, DM // 2), lambda k, *_: (0, 0))
    shapes, halves = (shape, shape), (half, half)
    if count > 1:
        shapes += (jax.ShapeDtypeStruct((32, DM // 2), BF),) * 2
        halves += (pl.BlockSpec((32, DM // 2), lambda k, *_: (0, 0)),) * 2
    weight = pl.BlockSpec((4, FT, 256), lambda k, *_: (k, 0, 0))
    return pl.pallas_call(
        functools.partial(hidden_kernel, lo),
        out_shape=shapes,
        grid_spec=pltpu.PrefetchScalarGridSpec(
            num_scalar_prefetch=3,
            grid=(4,),
            in_specs=[
                pl.BlockSpec((TOK - GROUP, FT), lambda k, *_: (0, 0)),
                pl.BlockSpec((GROUP, FT), lambda k, *_: (0, 0)),
                pl.BlockSpec((GROUP, FT), lambda k, *_: (0, 0)),
                weight,
                weight,
            ],
            out_specs=halves,
            scratch_shapes=[pltpu.VMEM((count * 32, FT), BF)],
        ),
        compiler_params=pltpu.CompilerParams(vmem_limit_bytes=24 * MIB),
        cost_estimate=pl.CostEstimate(
            flops=0 if count > 1 else 8 * TOK * DM * FT, bytes_accessed=1024 if count > 1 else 60 * MIB, transcendentals=0
        ),
    )(chips, order, core, gq, end, tail, wo, ws)


def around(v, by):
    return lax.ppermute(v, "mp", [(i, (i + by) % NM) for i in range(NM)])


def swap_all(v):
    return lax.all_to_all(v, "seq", split_axis=0, concat_axis=0, tiled=True)


def shards(hidden, query_weight, key_memory, value_memory, block_len, nbr_block, out_grad):
    s = lax.axis_index("seq")
    m = lax.axis_index("mp")
    core = s % NC
    cx, cy = s // (NY * NC), (s // NC) % NY
    off = jnp.array(OFF, jnp.int32)
    chips = (((cx + off[None, :]) % NX) * NY + (cy + off[:, None]) % NY).reshape(-1).astype(jnp.int32)
    core1 = core.reshape(1).astype(jnp.int32)
    last = (s % 8 == 7).astype(jnp.int32).reshape(1)
    first = (s % 8 == 0).astype(jnp.int32).reshape(1)
    ahead = jnp.array((4, 3, -3, 2, -2, 1, -1, 0), jnp.int32)
    order = jnp.concatenate([(m + ahead) % NM, first]).astype(jnp.int32)
    mine = nbr_block.T

    pay, left, right, g_head = prepare(mine, block_len, key_memory, value_memory, query_weight, out_grad)
    g_next = to_seq(g_head, -1)
    weight = lax.all_gather(query_weight, "seq", axis=0, tiled=True)
    held = swap_all(pay)
    facts = held[:, 2 * QR, : NP + 2].astype(jnp.int32)
    sent = pick(facts, held).reshape(NS, NP * QR, HD)
    kv = swap_all(sent).reshape(2, NH, RQ, NP, QR, HD)
    queries = jnp.dot(hidden, weight, preferred_element_type=F32)
    n_own = to_seq(queries[:GROUP].astype(BF), -1).astype(F32)
    own = queries.astype(BF).astype(F32)
    q_other = jnp.zeros_like(own)
    n_sib = jnp.zeros_like(n_own)
    parts = (mine, facts, last, own, q_other, n_own, n_sib, out_grad, g_next, kv)
    att_end, gq_end, terms = attend((3,), *parts)
    gq_tail = to_seq(gq_end, 1)
    att_tail = to_seq(att_end, 1)
    att_al, gq_al, terms = attend((0, 1, 2), *parts, into=terms)
    got = swap_all(terms.reshape(NS, NP * QR, HD))

    gone = jnp.where(first[0] == 1, jnp.zeros((), BF), gq_tail[1:])
    qg = jnp.concatenate([gone, gq_al, gq_end[:1]], 0)
    run = lax.psum_scatter(
        lax.dot_general(qg, weight, (((1,), (1,)), ((), ())), preferred_element_type=F32).astype(BF),
        "mp", scatter_dimension=0, tiled=True)
    sums = total(facts, got.reshape(NS * NP, QR, HD)).reshape(NS, 2 * QR, HD)
    back = swap_all(sums)
    back = back.reshape(2, NH, RQ, 2, QR, HD)
    grads = back.transpose(0, 3, 2, 4, 1, 5).reshape(2, 2 * NLEN, FT)

    dead = jnp.where(first[0] == 1, jnp.zeros((), BF), att_tail[1:])
    attended = jnp.concatenate([dead, att_al, att_end[:1]], 0)
    return attended, run, grads[0], grads[1]


def solution(mesh):
    return jax.shard_map(
        shards,
        mesh=mesh,
        in_specs=(
            P("seq", None),
            P("seq", "mp"),
            P("seq", "mp"),
            P("seq", "mp"),
            P("seq"),
            P("seq", None),
            P("seq", "mp"),
        ),
        out_specs=(P("seq", "mp"), P(("seq", "mp"), None), P("seq", "mp"), P("seq", "mp")),
        check_vma=False,
    )
```

time: 231 us -> 190 us (0.82)
  blocking collectives: 0 us -> 51.9 us
  starting transfers between devices: 59.3 us -> 15.2 us
  Pallas kernels: 51.2 us -> 24.3 us
  waiting for transfers between devices: 83.1 us -> 59.3 us
  local copies, waits for them, and re-layouts: 25.1 us -> 5.55 us
  matrix products: 0 us -> 15.6 us
  between operations: 1.12 us -> 14.2 us
  other arithmetic: 7.03 us -> 2.13 us
    all_to_all x0 -> x2, blocking collectives: none -> 51.9 us  [swap_all(): return lax.all_to_all(v, 'seq', split_axis=0, concat_axis=0, tiled=True)]
    all_gather x0 -> x1, waiting for transfers between devices: none -> 44.9 us  [shards(): weight = lax.all_gather(query_weight, 'seq', axis=0, tiled=True)]
    ppermute x25 -> x0, waiting for transfers between devices: 39.2 us -> none  [the longest x7 33 us: around(): return lax.ppermute(v, ('seq', 'mp'), ring_pairs())]
    pallas_call x4 -> x3, Pallas kernels: 47.7 us -> 18.5 us  [the longest x2 16.3 us: attend(): pl.pallas_call(functools.partial(attend_kernel, groups), out_shape=(rows,...]
    ppermute x25 -> x0, starting transfers between devices: 26.7 us -> none  [the longest x18 22 us: hop(): return lax.ppermute(v, 'seq', pairs)]
    ppermute x4, waiting for transfers between devices: 34.5 us -> 11.9 us  [to_seq(): return lax.ppermute(v, 'seq', [(i, (i + by) % NS) for i in range(NS)])]
    all_to_all x4 -> x2, starting transfers between devices: 28.6 us -> 12.2 us  [swap_all(): return lax.all_to_all(v, 'seq', split_axis=0, concat_axis=0, tiled=True)]
    dot_general x0 -> x2, matrix products: none -> 15.6 us  [the longest x1 7.87 us: shards(): lax.dot_general(qg, weight, (((1,), (1,)), ((), ())), preferred_element_t...]
  transfers between devices with their start and end apart: 33 -> 8, of which waited for: 13 -> 4; matrix products, arithmetic and copies ran while one was open for 11% -> 6% of each run, Pallas kernels for 13% -> 10%
where the time goes in v2:
time: 190 us; the launch traced here: 188 us
  waiting for transfers between devices  59.3 us (31%)
  blocking collectives  51.9 us (27%)
  Pallas kernels  24.3 us (13%)
  matrix products  15.6 us (8%)
  starting transfers between devices  15.2 us (8%)
  between operations  14.2 us (7%)
  local copies, waits for them, and re-layouts  5.55 us (3%)
  other arithmetic  2.13 us (1%)
    all_to_all x2, blocking collectives, swap_all(): return lax.all_to_all(v, 'seq', split_axis=0, concat_axis=0, tiled=True)  51.9 us
    all_gather x1, waiting for transfers between devices, shards(): weight = lax.all_gather(query_weight, 'seq', axis=0, tiled=True)  44.9 us
    pallas_call x2, Pallas kernels, attend(): pl.pallas_call(functools.partial(attend_kernel, groups), out_shape=(rows,...  16.3 us
    all_to_all x2, starting transfers between devices, swap_all(): return lax.all_to_all(v, 'seq', split_axis=0, concat_axis=0, tiled=True)  12.2 us
    ppermute x4, waiting for transfers between devices, to_seq(): return lax.ppermute(v, 'seq', [(i, (i + by) % NS) for i in range(NS)])  11.9 us
    dot_general x1, matrix products, shards(): lax.dot_general(qg, weight, (((1,), (1,)), ((), ())), preferred_element_t...  7.87 us
    dot_general x1, matrix products, shards(): queries = jnp.dot(hidden, weight, preferred_element_type=F32)  7.78 us
  transfers between devices with their start and end apart: 8, of which 4 were waited for; matrix products, arithmetic and copies ran while one was open for 6% of the time, Pallas kernels for 10%

profile of v2, /device:TPU:2, one launch (start us, length us, event | category | flops | bytes accessed | tf_op | source)
XLA Modules:
  0.0 188.2 jit_solution(9437073593804597057)
XLA Ops:
  7.2 0.0 all-gather.2.cloned.1.call-start
  7.2 0.7 all-gather.2.cloned.1.call-update
  7.9 2.2 %shard_map.102 = (bf16[32,80,128]{2,1,0:T(8,128)(2,1)}, bf16[256,256]{1,0:T(8,128)(2,1)}, bf16[256,256]{1,0:T(8,128)(2,1)}, bf16[64,512]{1,0:T(8,128)(2,1)}) custom-call(s32[2,4]{1,0:T(2,128)} %bitcast.36, s32[2]{0:T(128)} %lens.1, bf16[256,512]{1,0:T(8,128)(2,1)} %key.1, bf16[256,512]{1,0:T(8,128)(2,1)} %value.1, bf16[256,512]{1,0:T(8,128)(2,1)} %w.1, ...), custom_call_target="tpu_custom_call" | custom-call | tf_op jit(solution)/shard_map/pallas_call | solution.py:87
  10.1 18.5 %all_to_all.20.held = bf16[32,80,128]{2,1,0:T(8,128)(2,1)S(1)} all-to-all(bf16[32,80,128]{2,1,0:T(8,128)(2,1)} %get-tuple-element.12), channel_id=1, replica_groups=mesh['seq'=32,'mp'=8] {'seq'}, dimensions={0} | all-to-all | bytes 1310720 | tf_op jit(solution)/shard_map/all_to_all | solution.py:415
  28.5 0.0 copy-start.3
  28.6 0.7 fusion.5.facts
  29.2 0.2 copy-done.3
  29.4 2.9 %shard_map.103 = bf16[256,32,128]{2,1,0:T(8,128)(2,1)} custom-call(s32[32,10]{1,0:T(8,128)} %fusion.5.facts, bf16[32,80,128]{2,1,0:T(8,128)(2,1)} %copy-done.3), custom_call_target="tpu_custom_call" | custom-call | bytes 1024 | tf_op jit(solution)/shard_map/pallas_call | solution.py:218
  32.3 5.8 %all-to-all-start.1 = ((bf16[32,256,128]{2,1,0:T(8,128)(2,1)}), bf16[32,256,128]{2,1,0:T(8,128)(2,1)S(1)}, u32[]{:S(2)}, u32[]{:S(2)}) async-start(bf16[32,256,128]{2,1,0:T(8,128)(2,1)} %bitcast.31), calls=%async_computation.1 | async-start | bytes 4194304 | tf_op jit(solution)/shard_map/all_to_all | solution.py:415
  38.1 0.0 copy-start.7
  38.1 0.0 reduce-scatter.2.cloned.1.call-start
  38.2 44.9 %all-gather.2.cloned.1.call-done = bf16[8192,512]{1,0:T(8,128)(2,1)} async-done(((bf16[256,512]{1,0:T(8,128)(2,1)}), bf16[8192,512]{1,0:T(8,128)(2,1)}) %all-gather.2.cloned.1.call-update) | async-done | bytes 8388624 | tf_op jit(solution)/shard_map/all_gather | solution.py:434
  83.1 7.8 %fusion.8 = (f32[256,512]{1,0:T(8,128)}, bf16[256,512]{1,0:T(8,128)(2,1)S(1)}) fusion(bf16[256,8192]{1,0:T(8,128)(2,1)} %param.7, bf16[8192,512]{1,0:T(8,128)(2,1)} %all-gather.2.cloned.1.call-done), kind=kOutput, calls=%fused_computation.17 | convolution fusion | flops 2147745792 | bytes 13369344 | tf_op jit(solution)/shard_map/dot_general | solution.py:439
  90.9 2.4 %collective-permute-start = (bf16[64,512]{1,0:T(8,128)(2,1)S(1)}, bf16[64,512]{1,0:T(8,128)(2,1)S(1)}, u32[]{:S(2)}, u32[]{:S(2)}) collective-permute-start(bf16[64,512]{1,0:T(8,128)(2,1)S(1)} %slice.36), channel_id=1, source_target_pairs={{0,248},{8,0},{16,8},{24,16},{32,24},{40,32},{48,40},{56,48},{64,5... | collective-permute-start | bytes 196616 | tf_op jit(solution)/shard_map/ppermute | solution.py:45
  93.3 0.0 copy-done.7
  93.3 0.3 collective-permute-start.1
  93.6 1.6 collective-permute-done
  95.2 0.7 convert_element_type.27.na
  95.9 0.0 collective-permute-done.1.gn
  95.9 0.0 copy-start.4
  95.9 0.0 all-to-all-done.1
  95.9 0.0 copy-start.1
  95.9 0.7 broadcast_in_dim.13.nb
  96.6 0.9 broadcast_in_dim.12.qb
  97.5 0.0 copy-done.4
  97.5 0.0 copy-done.1
  97.5 6.2 %shard_map.104 = (bf16[64,512]{1,0:T(8,128)(2,1)}, bf16[64,512]{1,0:T(8,128)(2,1)}, bf16[2,4,4,8,32,128]{5,4,3,2,1,0:T(8,128)(2,1)}) custom-call(s32[2,4]{1,0:T(2,128)} %bitcast.37, s32[32,10]{1,0:T(8,128)} %fusion.5.facts, s32[1]{0:T(128)} %bitcast.2.last, f32[256,512]{1,0:T(8,128)} %get-tuple-element.22.qa, f32[256,512]{1,0:T(8,128)} %broadcast_in_dim.12.qb, ...), custom_call_target="tpu_custom_call" | custom-call | flops 100000000 | bytes 2097152 | tf_op jit(solution)/shard_map/pallas_call | solution.py:315
  103.8 0.0 collective-permute-start.3
  103.8 0.7 slice.32
  104.5 10.0 %shard_map.105 = (bf16[192,512]{1,0:T(8,128)(2,1)}, bf16[192,512]{1,0:T(8,128)(2,1)}, bf16[2,4,4,8,32,128]{5,4,3,2,1,0:T(8,128)(2,1)}) custom-call(s32[2,4]{1,0:T(2,128)} %bitcast.38, s32[32,10]{1,0:T(8,128)} %fusion.5.facts, s32[1]{0:T(128)} %bitcast.2.last, f32[256,512]{1,0:T(8,128)} %get-tuple-element.22.qa, ...), custom_call_target="tpu_custom_call", output_to_operand_aliasing={{2}: (10, {})} | custom-call | flops 300000000 | bytes 6291456 | tf_op jit(solution)/shard_map/pallas_call | solution.py:315
  114.5 0.0 collective-permute-done.3
  114.5 7.9 %convolution_convert_fusion = bf16[256,8192]{1,0:T(8,128)(2,1)} fusion(bf16[8192,512]{1,0:T(8,128)(2,1)} %all-gather.2.cloned.1.call-done, bf16[1,512]{1,0:T(2,128)(2,1)S(1)} %slice.32, bf16[192,512]{1,0:T(8,128)(2,1)} %get-tuple-element.18, bf16[63,512]{1,0:T(8,128)(2,1)S(1)} %slice_select_fusion), kind=kOutput, calls=%fused_computation | convolution fusion | flops 2150367232 | bytes 12845056 | tf_op jit(solution)/shard_map/dot_general | solution.py:454
  122.4 0.0 copy-start.2
  122.4 0.0 copy-start
  122.4 0.0 reduce-scatter.2.cloned.1.call-update
  122.4 0.0 copy-start.6
  122.5 0.0 copy-start.5
  122.5 1.5 copy-done.2
  124.0 33.4 %all_to_all.21 = bf16[32,256,128]{2,1,0:T(8,128)(2,1)S(1)} all-to-all(bf16[32,256,128]{2,1,0:T(8,128)(2,1)S(1)} %bitcast.30), channel_id=1, replica_groups=mesh['seq'=32,'mp'=8] {'seq'}, dimensions={0} | all-to-all | bytes 4194304 | tf_op jit(solution)/shard_map/all_to_all | solution.py:415
  157.5 0.0 copy-done
  157.5 2.9 %shard_map.106 = bf16[64,32,128]{2,1,0:T(8,128)(2,1)} custom-call(s32[32,10]{1,0:T(8,128)S(1)} %copy-done, bf16[256,32,128]{2,1,0:T(8,128)(2,1)S(1)} %bitcast.27), custom_call_target="tpu_custom_call" | custom-call | tf_op jit(solution)/shard_map/pallas_call | solution.py:243
  160.4 6.4 %all-to-all-start.3 = ((bf16[32,64,128]{2,1,0:T(8,128)(2,1)}), bf16[32,64,128]{2,1,0:T(8,128)(2,1)S(1)}, u32[]{:S(2)}, u32[]{:S(2)}) async-start(bf16[32,64,128]{2,1,0:T(8,128)(2,1)} %bitcast.8), calls=%async_computation.4 | async-start | bytes 1048576 | tf_op jit(solution)/shard_map/all_to_all | solution.py:415
  166.8 0.0 copy-done.6
  166.8 0.2 collective-permute-start.2
  167.0 10.3 %collective-permute-done.2 = bf16[64,512]{1,0:T(8,128)(2,1)S(1)} collective-permute-done((bf16[64,512]{1,0:T(8,128)(2,1)S(1)}, bf16[64,512]{1,0:T(8,128)(2,1)S(1)}, u32[]{:S(2)}, u32[]{:S(2)}) %collective-permute-start.2) | collective-permute-done | bytes 65568 | tf_op jit(solution)/shard_map/ppermute | solution.py:45
  177.3 0.0 copy-done.5
  177.3 0.8 pad_maximum_fusion
  178.1 0.0 all-to-all-done.3
  178.1 0.4 copy.26
  178.5 0.2 fusion.7
  178.7 0.9 copy_bitcast_fusion.1
  179.6 1.8 reduce-scatter.2.cloned.1.call-done
  (5 shorter events, 0.1 us)
Async XLA Ops:
  7.2 75.9 %all-gather.2.cloned.1.call-start = ((), (), s32[]{:S(2)}) async-start(), calls=%async_computation.5 | async-start | bytes 8650752 | tf_op jit(solution)/shard_map/all_gather | solution.py:434
  28.5 0.9 copy-start.3
  32.3 63.6 %all-to-all-start.1 = ((bf16[32,256,128]{2,1,0:T(8,128)(2,1)}), bf16[32,256,128]{2,1,0:T(8,128)(2,1)S(1)}, u32[]{:S(2)}, u32[]{:S(2)}) async-start(bf16[32,256,128]{2,1,0:T(8,128)(2,1)} %bitcast.31), calls=%async_computation.1 | async-start | bytes 4194304 | tf_op jit(solution)/shard_map/all_to_all | solution.py:415
  38.1 55.2 %copy-start.7 = (bf16[64,512]{1,0:T(8,128)(2,1)S(1)}, bf16[64,512]{1,0:T(8,128)(2,1)}, u32[]{:S(2)}) copy-start(bf16[64,512]{1,0:T(8,128)(2,1)} %get-tuple-element.13) | copy-start | bytes 196612
  38.1 143.2 %reduce-scatter.2.cloned.1.call-start = ((), (), s32[]{:S(2)}) async-start(), calls=%async_computation.6 | async-start | bytes 4718592 | tf_op jit(solution)/shard_map/reduce_scatter | solution.py:453
  90.9 4.3 %collective-permute-start = (bf16[64,512]{1,0:T(8,128)(2,1)S(1)}, bf16[64,512]{1,0:T(8,128)(2,1)S(1)}, u32[]{:S(2)}, u32[]{:S(2)}) collective-permute-start(bf16[64,512]{1,0:T(8,128)(2,1)S(1)} %slice.36), channel_id=1, source_target_pairs={{0,248},{8,0},{16,8},{24,16},{32,24},{40,32},{48,40},{56,48},{64,5... | collective-permute-start | bytes 196616 | tf_op jit(solution)/shard_map/ppermute | solution.py:45
  93.3 2.6 %collective-permute-start.1 = (bf16[64,512]{1,0:T(8,128)(2,1)S(1)}, bf16[64,512]{1,0:T(8,128)(2,1)S(1)}, u32[]{:S(2)}, u32[]{:S(2)}) collective-permute-start(bf16[64,512]{1,0:T(8,128)(2,1)S(1)} %copy-done.7), channel_id=1, source_target_pairs={{0,248},{8,0},{16,8},{24,16},{32,24},{40,32},{48,40},{56,48},{64,5... | collective-permute-start | bytes 196616 | tf_op jit(solution)/shard_map/ppermute | solution.py:45
  95.9 1.6 copy-start.4
  95.9 1.6 copy-start.1
  103.8 10.8 %collective-permute-start.3 = (bf16[64,512]{1,0:T(8,128)(2,1)}, bf16[64,512]{1,0:T(8,128)(2,1)S(1)}, u32[]{:S(2)}, u32[]{:S(2)}) collective-permute-start(bf16[64,512]{1,0:T(8,128)(2,1)} %get-tuple-element.17), channel_id=1, source_target_pairs={{0,8},{8,16},{16,24},{24,32},{32,40},{40,48},{48,56},{56,64},{64,7... | collective-permute-start | bytes 196616 | tf_op jit(solution)/shard_map/ppermute | solution.py:45
  122.4 1.6 copy-start.2
  122.4 35.0 %copy-start = (s32[32,10]{1,0:T(8,128)S(1)}, s32[32,10]{1,0:T(8,128)}, u32[]{:S(2)}) copy-start(s32[32,10]{1,0:T(8,128)} %fusion.5.facts) | copy-start | bytes 3844
  122.4 44.3 %copy-start.6 = (bf16[64,512]{1,0:T(8,128)(2,1)S(1)}, bf16[64,512]{1,0:T(8,128)(2,1)}, u32[]{:S(2)}) copy-start(bf16[64,512]{1,0:T(8,128)(2,1)} %get-tuple-element.14) | copy-start | bytes 196612
  122.5 54.9 %copy-start.5 = (bf16[192,512]{1,0:T(8,128)(2,1)S(1)}, bf16[192,512]{1,0:T(8,128)(2,1)}, u32[]{:S(2)}) copy-start(bf16[192,512]{1,0:T(8,128)(2,1)} %get-tuple-element.16) | copy-start | bytes 589828
  160.4 17.7 %all-to-all-start.3 = ((bf16[32,64,128]{2,1,0:T(8,128)(2,1)}), bf16[32,64,128]{2,1,0:T(8,128)(2,1)S(1)}, u32[]{:S(2)}, u32[]{:S(2)}) async-start(bf16[32,64,128]{2,1,0:T(8,128)(2,1)} %bitcast.8), calls=%async_computation.4 | async-start | bytes 1048576 | tf_op jit(solution)/shard_map/all_to_all | solution.py:415
  166.8 10.5 %collective-permute-start.2 = (bf16[64,512]{1,0:T(8,128)(2,1)S(1)}, bf16[64,512]{1,0:T(8,128)(2,1)S(1)}, u32[]{:S(2)}, u32[]{:S(2)}) collective-permute-start(bf16[64,512]{1,0:T(8,128)(2,1)S(1)} %copy-done.6), channel_id=1, source_target_pairs={{0,8},{8,16},{16,24},{24,32},{32,40},{40,48},{48,56},{56,64},{64,7... | collective-permute-start | bytes 196616 | tf_op jit(solution)/shard_map/ppermute | solution.py:45
Sparse Core Ops, SparseCore 0:
  10.6 72.4 all-gather.1
  122.6 58.7 reduce-scatter.1

commit v3 on v2

v3 whole, which is shorter than its diff:
```python
import functools

import jax
import jax.numpy as jnp
from jax import lax
from jax.experimental import pallas as pl
from jax.experimental.pallas import tpu as pltpu
from jax.sharding import PartitionSpec as P

HD = 128
GROUP = 64
NLEN = 128
SEQ_LEN = 2048
RIM = GROUP - 1
NS = 32
TOK = 256
FT = 512
DM = 8192
NH = FT // HD
NP = 8
NB = 64
RQ = 4
QR = NLEN // RQ
BF = jnp.bfloat16
F32 = jnp.float32
NEG_FILL = -1e30
MIB = 1 << 20
WIDE = 60 * MIB


def to_seq(v, by):
    return lax.ppermute(v, "seq", [(i, (i + by) % NS) for i in range(NS)])


def prepare_kernel(mine, lens, key, value, pay):
    lane = lax.broadcasted_iota(jnp.int32, (16, HD), 1)
    meta = jnp.zeros((16, HD), jnp.int32)
    for i in range(NP):
        meta = jnp.where(lane == i, mine[i % 2, i // 2], meta)
    for i in range(2):
        meta = jnp.where(lane == NP + i, lens[i], meta)
    meta = meta.astype(F32).astype(BF)
    for which, ref in ((0, key), (1, value)):
        for h in range(NH):
            for r in range(RQ):
                j = (which * NH + h) * RQ + r
                for blk in range(2):
                    at = blk * NLEN + r * QR
                    pay[j, blk * QR : (blk + 1) * QR] = ref[at : at + QR, h * HD : (h + 1) * HD]
                pay[j, 2 * QR :] = meta


def prepare(mine, lens, key, value):
    smem = pl.BlockSpec(memory_space=pltpu.SMEM)

    def full(*shape):
        return pl.BlockSpec(shape, lambda i: (0,) * len(shape))

    return pl.pallas_call(
        prepare_kernel,
        grid=(1,),
        out_shape=jax.ShapeDtypeStruct((NS, 2 * QR + 16, HD), BF),
        in_specs=[smem, smem, full(256, FT), full(256, FT)],
        out_specs=full(NS, 2 * QR + 16, HD),
        compiler_params=pltpu.CompilerParams(vmem_limit_bytes=WIDE),
    )(mine, lens, key, value)


def pick_kernel(facts, held, out):
    count = out.shape[0] // NP
    base = pl.program_id(0) * count

    def step(i, _):
        for n in range(NP):
            b = facts[base + i, n]
            at = pl.multiple_of(jnp.bitwise_and(b, 1) * QR, QR)
            out[i * NP + n] = held[lax.shift_right_logical(b, 1), pl.ds(at, QR)]
        return 0

    lax.fori_loop(0, count, step, 0, unroll=2)


def pick(facts, held):
    count = NS * NP // 2
    return pl.pallas_call(
        pick_kernel,
        out_shape=jax.ShapeDtypeStruct((NS * NP, QR, HD), BF),
        grid=(2,),
        in_specs=[pl.BlockSpec(memory_space=pltpu.SMEM), pl.BlockSpec(held.shape, lambda i: (0, 0, 0))],
        out_specs=pl.BlockSpec((count, QR, HD), lambda i: (i, 0, 0)),
        compiler_params=pltpu.CompilerParams(vmem_limit_bytes=WIDE),
        cost_estimate=pl.CostEstimate(flops=0, bytes_accessed=1024, transcendentals=0),
    )(facts, held)


def total_kernel(facts, terms, out, acc):
    acc[...] = jnp.zeros_like(acc)

    def step(i, _):
        for n in range(NP):
            b = facts[i, n]
            acc[b] = acc[b] + terms[i * NP + n].astype(F32)
        return 0

    lax.fori_loop(0, NS, step, 0, unroll=2)
    out[...] = acc[...].astype(BF)


def total(facts, terms):
    return pl.pallas_call(
        total_kernel,
        out_shape=jax.ShapeDtypeStruct((NB, QR, HD), BF),
        in_specs=[pl.BlockSpec(memory_space=pltpu.SMEM), pl.BlockSpec(memory_space=pltpu.VMEM)],
        out_specs=pl.BlockSpec(memory_space=pltpu.VMEM),
        scratch_shapes=[pltpu.VMEM((NB, QR, HD), F32)],
        compiler_params=pltpu.CompilerParams(vmem_limit_bytes=16 * MIB),
    )(facts, terms)


def attend_kernel(groups, heads, seat, facts, q, g, kv, *rest):
    before, (att, gq, terms) = rest[:-3], rest[-3:]

    def mm(p, r, dims):
        return lax.dot_general(p, r, (dims, ((), ())), preferred_element_type=F32)

    scale = HD ** (-0.5)
    lane = lax.broadcasted_iota(jnp.int32, (GROUP, 2 * NLEN), 1)
    units = [(h, i) for h in range(heads) for i in range(len(groups))]
    count = range(len(units))
    valid = []
    for grp in groups:
        blk0, blk1 = facts[seat[0], 2 * grp], facts[seat[0], 2 * grp + 1]
        len0 = facts[lax.shift_right_logical(blk0, 1), NP + jnp.bitwise_and(blk0, 1)]
        len1 = facts[lax.shift_right_logical(blk1, 1), NP + jnp.bitwise_and(blk1, 1)]
        valid.append(lane < jnp.where(lane < NLEN, len0, len1 + NLEN))
    cols = [slice(h * HD, (h + 1) * HD) for h in range(heads)]
    rows = [slice(i * GROUP, (i + 1) * GROUP) for i in range(len(groups))]
    tok = [slice(grp * GROUP, (grp + 1) * GROUP) for grp in groups]

    def block(which, h, i):
        return jnp.concatenate([kv[which, h, r, 2 * groups[i] + n] for n in range(2) for r in range(RQ)], 0)

    qs = [q[tok[i], cols[h]] for h, i in units]
    gs = [g[tok[i], cols[h]] for h, i in units]
    keys = [block(0, h, i) for h, i in units]
    vals = [block(1, h, i) for h, i in units]
    scores = [mm(qs[u], keys[u], ((1,), (1,))) for u in count]
    grad_prob = [mm(gs[u], vals[u], ((1,), (1,))) for u in count]
    ex, inv = [], []
    for u in count:
        ok = valid[units[u][1]]
        masked = jnp.where(ok, scores[u] * scale, NEG_FILL)
        top = jnp.max(masked, axis=1, keepdims=True)
        e = jnp.where(ok, jnp.exp(masked - top), 0.0)
        ex.append(e)
        inv.append(1.0 / jnp.sum(e, axis=1, keepdims=True))
    outs = [(mm(ex[u].astype(BF), vals[u], ((1,), (0,))) * inv[u]).astype(BF) for u in count]
    prob = [ex[u] * inv[u] for u in count]
    vt = [mm(prob[u].astype(BF), gs[u], ((0,), (0,))).astype(BF) for u in count]
    ds = []
    for u in count:
        delta = jnp.sum(gs[u].astype(F32) * outs[u].astype(F32), axis=1, keepdims=True)
        ds.append((prob[u] * (grad_prob[u] - delta) * scale).astype(BF))
    gqs = [mm(ds[u], keys[u], ((1,), (0,))).astype(BF) for u in count]
    kt = [mm(ds[u], qs[u], ((0,), (0,))).astype(BF) for u in count]
    shift = 2 * groups[0] if before else 0
    if before:
        terms[:, :, :, :shift] = before[0][...]
    for u, (h, i) in enumerate(units):
        att[rows[i], cols[h]] = outs[u]
        gq[rows[i], cols[h]] = gqs[u]
        for n in range(2):
            for r in range(RQ):
                part = slice((n * RQ + r) * QR, (n * RQ + r + 1) * QR)
                terms[0, h, r, shift + 2 * i + n] = kt[u][part]
                terms[1, h, r, shift + 2 * i + n] = vt[u][part]


def attend(groups, heads, seat, facts, q, g, kv, before=None):
    count = len(groups) * GROUP
    pairs = 2 * len(groups) if before is None else NP
    tok = pl.BlockSpec((TOK, heads * HD), lambda h, *_: (0, h))
    out = pl.BlockSpec((count, heads * HD), lambda h, *_: (0, h))

    def mem(n):
        return pl.BlockSpec((2, heads, RQ, n, QR, HD), lambda h, *_: (0, h, 0, 0, 0, 0))

    rows = jax.ShapeDtypeStruct((count, FT), BF)
    read = NP if before is not None else 2
    specs, operands = [tok, tok, mem(read)], (q, g, kv)
    if before is not None:
        specs, operands = specs + [mem(before.shape[3])], operands + (before,)
    return pl.pallas_call(
        functools.partial(attend_kernel, groups, heads),
        out_shape=(rows, rows, jax.ShapeDtypeStruct((2, NH, RQ, pairs, QR, HD), BF)),
        grid_spec=pltpu.PrefetchScalarGridSpec(
            num_scalar_prefetch=2,
            grid=(NH // heads,),
            in_specs=specs,
            out_specs=(out, out, mem(pairs)),
        ),
        compiler_params=pltpu.CompilerParams(vmem_limit_bytes=32 * MIB),
        cost_estimate=pl.CostEstimate(
            flops=100_000_000 * len(groups), bytes_accessed=2 * MIB * len(groups), transcendentals=0
        ),
    )(seat, facts, *operands)


def swap_all(v):
    return lax.all_to_all(v, "seq", split_axis=0, concat_axis=0, tiled=True)


def shards(hidden, query_weight, key_memory, value_memory, block_len, nbr_block, out_grad):
    s = lax.axis_index("seq")
    starts = s % (SEQ_LEN // TOK) == 0
    seat = s.astype(jnp.int32).reshape(1)
    zero = jnp.zeros((), BF)

    weight = lax.all_gather(query_weight, "seq", axis=0, tiled=True)

    held = swap_all(prepare(nbr_block.T, block_len, key_memory, value_memory))
    facts = held[:, 2 * QR, : NP + 2].astype(jnp.int32)
    facts = jnp.concatenate([jnp.roll(facts[:, NP - 2 : NP], 1, axis=0), facts[:, : NP - 2], facts[:, NP:]], 1)
    sent = pick(facts, held).reshape(NS, NP * QR, HD)
    kv = swap_all(sent).reshape(2, NH, RQ, NP, QR, HD)

    h_prev, g_prev = to_seq(hidden[TOK - 1 :], 1), to_seq(out_grad[TOK - 1 :], 1)
    h_rows = jnp.concatenate([h_prev, hidden[: TOK - 1]], 0)
    g_rows = jnp.concatenate([g_prev, jnp.where(starts, zero, out_grad[:RIM]), out_grad[RIM : TOK - 1]], 0)
    queries = jnp.dot(h_rows, weight, preferred_element_type=F32).astype(BF)

    att_rim, gq_rim, terms = attend((0,), NH, seat, facts, queries, g_rows, kv)
    gq_last, att_last = to_seq(gq_rim[:1], -1), to_seq(att_rim[:1], -1)
    att, gq, terms = attend((1, 2, 3), 2, seat, facts, queries, g_rows, kv, terms)

    query_grad = jnp.concatenate([jnp.where(starts, zero, gq_rim[1:]), gq, gq_last], 0)
    run = lax.psum_scatter(
        lax.dot_general(
            query_grad, weight, (((1,), (1,)), ((), ())), preferred_element_type=F32
        ).astype(BF),
        "mp",
        scatter_dimension=0,
        tiled=True,
    )
    got = swap_all(terms.reshape(NS, NP * QR, HD))
    sums = total(facts, got.reshape(NS * NP, QR, HD)).reshape(NS, 2 * QR, HD)
    back = swap_all(sums).reshape(2, NH, RQ, 2, QR, HD)
    grads = back.transpose(0, 3, 2, 4, 1, 5).reshape(2, 2 * NLEN, FT)

    attended = jnp.concatenate([jnp.where(starts, zero, att_rim[1:]), att, att_last], 0)
    return attended, run, grads[0], grads[1]


def solution(mesh):
    return jax.shard_map(
        shards,
        mesh=mesh,
        in_specs=(
            P("seq", None),
            P("seq", "mp"),
            P("seq", "mp"),
            P("seq", "mp"),
            P("seq"),
            P("seq", None),
            P("seq", "mp"),
        ),
        out_specs=(P("seq", "mp"), P(("seq", "mp"), None), P("seq", "mp"), P("seq", "mp")),
        check_vma=False,
    )
```

time: 190 us -> 171 us (0.900)
  Pallas kernels: 24.3 us -> 12.9 us
  waiting for transfers between devices: 59.3 us -> 53 us
  starting transfers between devices: 15.2 us -> 19.1 us
  blocking collectives: 51.9 us -> 48.2 us
    all_gather x1, waiting for transfers between devices: 44.9 us -> 6.66 us  [shards(): weight = lax.all_gather(query_weight, 'seq', axis=0, tiled=True)]
    ppermute x4, waiting for transfers between devices: 11.9 us -> 39.6 us  [to_seq(): return lax.ppermute(v, 'seq', [(i, (i + by) % NS) for i in range(NS)])]
    pallas_call x3, Pallas kernels: 18.5 us -> 7.07 us  [the longest x2 5.02 us: attend(): pl.pallas_call(functools.partial(attend_kernel, groups, heads), out_shape...]
    ppermute x4, starting transfers between devices: 2.92 us -> 6.75 us  [to_seq(): return lax.ppermute(v, 'seq', [(i, (i + by) % NS) for i in range(NS)])]
    all_to_all x2, blocking collectives: 51.9 us -> 48.2 us  [swap_all(): return lax.all_to_all(v, 'seq', split_axis=0, concat_axis=0, tiled=True)]
    all_to_all x2, waiting for transfers between devices: 0.01 us -> 2.66 us  [swap_all(): return lax.all_to_all(v, 'seq', split_axis=0, concat_axis=0, tiled=True)]
  transfers between devices with their start and end apart: 8 -> 8, of which waited for: 4 -> 6; matrix products, arithmetic and copies ran while one was open for 6% -> 7% of each run, Pallas kernels for 10% -> 7%
where the time goes in v3:
time: 171 us; the launch traced here: 169 us
  waiting for transfers between devices  53 us (31%)
  blocking collectives  48.2 us (28%)
  starting transfers between devices  19.1 us (11%)
  matrix products  14.7 us (9%)
  between operations  14.2 us (8%)
  Pallas kernels  12.9 us (8%)
  local copies, waits for them, and re-layouts  5.61 us (3%)
    all_to_all x2, blocking collectives, swap_all(): return lax.all_to_all(v, 'seq', split_axis=0, concat_axis=0, tiled=True)  48.2 us
    ppermute x4, waiting for transfers between devices, to_seq(): return lax.ppermute(v, 'seq', [(i, (i + by) % NS) for i in range(NS)])  39.6 us
    all_to_all x2, starting transfers between devices, swap_all(): return lax.all_to_all(v, 'seq', split_axis=0, concat_axis=0, tiled=True)  12.2 us
    dot_general x1, matrix products, shards(): lax.dot_general(query_grad, weight, (((1,), (1,)), ((), ())), preferred_e...  7.74 us
    dot_general x1, matrix products, shards(): queries = jnp.dot(h_rows, weight, preferred_element_type=F32).astype(BF)  7 us
    ppermute x4, starting transfers between devices, to_seq(): return lax.ppermute(v, 'seq', [(i, (i + by) % NS) for i in range(NS)])  6.75 us
    all_gather x1, waiting for transfers between devices, shards(): weight = lax.all_gather(query_weight, 'seq', axis=0, tiled=True)  6.66 us
    pallas_call x2, Pallas kernels, attend(): pl.pallas_call(functools.partial(attend_kernel, groups, heads), out_shape...  5.02 us
  transfers between devices with their start and end apart: 8, of which 6 were waited for; matrix products, arithmetic and copies ran while one was open for 7% of the time, Pallas kernels for 7%

profile of v3, /device:TPU:2, one launch (start us, length us, event | category | flops | bytes accessed | tf_op | source)
XLA Modules:
  0.0 169.2 jit_solution(12527088841206167074)
XLA Ops:
  7.2 0.0 all-gather.2.cloned.1.call-start
  7.2 0.7 all-gather.2.cloned.1.call-update
  7.9 2.0 %shard_map.102 = bf16[32,80,128]{2,1,0:T(8,128)(2,1)} custom-call(s32[2,4]{1,0:T(2,128)} %bitcast.38, s32[2]{0:T(128)} %lens.1, bf16[256,512]{1,0:T(8,128)(2,1)} %key.1, bf16[256,512]{1,0:T(8,128)(2,1)} %value.1), custom_call_target="tpu_custom_call" | custom-call | tf_op jit(solution)/shard_map/pallas_call | solution.py:59
  9.9 0.0 copy-start.4
  10.0 18.6 %all_to_all.20.held = bf16[32,80,128]{2,1,0:T(8,128)(2,1)S(1)} all-to-all(bf16[32,80,128]{2,1,0:T(8,128)(2,1)} %shard_map.102), channel_id=1, replica_groups=mesh['seq'=32,'mp'=8] {'seq'}, dimensions={0} | all-to-all | bytes 1310720 | tf_op jit(solution)/shard_map/all_to_all | solution.py:210
  28.5 0.0 copy-start.3
  28.6 0.1 slice.72
  28.6 0.1 slice.75
  28.7 0.1 slice.73
  28.8 0.7 pad_add_fusion.facts
  29.5 0.0 copy-done.3
  29.5 2.9 %shard_map.103 = bf16[256,32,128]{2,1,0:T(8,128)(2,1)} custom-call(s32[32,10]{1,0:T(8,128)} %pad_add_fusion.facts, bf16[32,80,128]{2,1,0:T(8,128)(2,1)} %copy-done.3), custom_call_target="tpu_custom_call" | custom-call | bytes 1024 | tf_op jit(solution)/shard_map/pallas_call | solution.py:85
  32.4 5.8 %all-to-all-start.1 = ((bf16[32,256,128]{2,1,0:T(8,128)(2,1)}), bf16[32,256,128]{2,1,0:T(8,128)(2,1)S(1)}, u32[]{:S(2)}, u32[]{:S(2)}) async-start(bf16[32,256,128]{2,1,0:T(8,128)(2,1)} %bitcast.32), calls=%async_computation.1 | async-start | bytes 4194304 | tf_op jit(solution)/shard_map/all_to_all | solution.py:210
  38.2 0.0 reduce-scatter.2.cloned.1.call-start
  38.3 0.0 copy-done.4
  38.3 0.2 collective-permute-start.1
  38.5 0.9 slice.60
  39.5 1.5 collective-permute-start
  41.0 34.5 %collective-permute-done.1 = bf16[1,512]{1,0:T(2,128)(2,1)S(1)} collective-permute-done((bf16[1,512]{1,0:T(2,128)(2,1)S(1)}, bf16[1,512]{1,0:T(2,128)(2,1)S(1)}, u32[]{:S(2)}, u32[]{:S(2)}) %collective-permute-start.1) | collective-permute-done | bytes 1056 | tf_op jit(solution)/shard_map/ppermute | solution.py:32
  75.5 1.4 collective-permute-done
  76.9 6.7 %all-gather.2.cloned.1.call-done = bf16[8192,512]{1,0:T(8,128)(2,1)} async-done(((bf16[256,512]{1,0:T(8,128)(2,1)}), bf16[8192,512]{1,0:T(8,128)(2,1)}) %all-gather.2.cloned.1.call-update) | async-done | bytes 8388624 | tf_op jit(solution)/shard_map/all_gather | solution.py:219
  83.5 0.0 copy-start.2
  83.5 7.0 %fusion.4.q = bf16[256,512]{1,0:T(8,128)(2,1)S(1)} fusion(bf16[8192,512]{1,0:T(8,128)(2,1)} %all-gather.2.cloned.1.call-done, bf16[255,8192]{1,0:T(8,128)(2,1)} %bitcast.39, bf16[1,8192]{1,0:T(2,128)(2,1)S(1)} %collective-permute-done), kind=kOutput, calls=%fused_computation.5 | convolution fusion | flops 2156003328 | bytes 12845056 | tf_op jit(solution)/shard_map/dot_general | solution.py:230
  90.6 0.0 all-to-all-done.1
  90.6 0.0 copy-done.2
  90.6 1.7 shard_map.104
  92.3 2.5 %collective-permute-start.3 = (bf16[1,512]{1,0:T(2,128)(2,1)S(1)}, bf16[1,512]{1,0:T(2,128)(2,1)S(1)}, u32[]{:S(2)}, u32[]{:S(2)}) collective-permute-start(bf16[1,512]{1,0:T(2,128)(2,1)S(1)} %slice.68), channel_id=1, source_target_pairs={{0,248},{8,0},{16,8},{24,16},{32,24},{40,32},{48,40},{56,48},{64,5... | collective-permute-start | bytes 3080 | tf_op jit(solution)/shard_map/ppermute | solution.py:32
  94.8 3.3 %shard_map.105 = (bf16[192,512]{1,0:T(8,128)(2,1)S(1)}, bf16[192,512]{1,0:T(8,128)(2,1)S(1)}, bf16[2,4,4,8,32,128]{5,4,3,2,1,0:T(8,128)(2,1)S(1)}) custom-call(s32[1]{0:T(128)} %bitcast.seat, s32[32,10]{1,0:T(8,128)S(1)} %copy-done.2, bf16[256,512]{1,0:T(8,128)(2,1)S(1)} %fusion.4.q, bf16[256,512]{1,0:T(8,128)(2,1)S(1)} %pad_maximum_fusion.g, ...), custom_call_target="tpu_custom_call" | custom-call | flops 300000000 | bytes 6291456 | tf_op jit(solution)/shard_map/pallas_call | solution.py:193
  98.2 0.0 copy-start
  98.2 1.3 copy-done
  99.5 0.0 collective-permute-done.3
  99.5 7.7 %convolution_convert_fusion = bf16[256,8192]{1,0:T(8,128)(2,1)} fusion(bf16[8192,512]{1,0:T(8,128)(2,1)} %all-gather.2.cloned.1.call-done, bf16[1,512]{1,0:T(2,128)(2,1)S(1)} %collective-permute-done.3, bf16[192,512]{1,0:T(8,128)(2,1)S(1)} %get-tuple-element.14, bf16[63,512]{1,0:T(8,128)(2,1)S(1)} %slice_select_fusion), kind=kOutput, calls=%fused_computation | convolution fusion | flops 2150367232 | bytes 12845056 | tf_op jit(solution)/shard_map/dot_general | solution.py:238
  107.3 0.0 copy-start.1
  107.3 0.0 reduce-scatter.2.cloned.1.call-update
  107.3 1.6 copy-done.1
  108.8 29.6 %all_to_all.21 = bf16[32,256,128]{2,1,0:T(8,128)(2,1)S(1)} all-to-all(bf16[32,256,128]{2,1,0:T(8,128)(2,1)S(1)} %bitcast.31), channel_id=1, replica_groups=mesh['seq'=32,'mp'=8] {'seq'}, dimensions={0} | all-to-all | bytes 4194304 | tf_op jit(solution)/shard_map/all_to_all | solution.py:210
  138.4 2.9 %shard_map.106 = bf16[64,32,128]{2,1,0:T(8,128)(2,1)} custom-call(s32[32,10]{1,0:T(8,128)S(1)} %copy-done.2, bf16[256,32,128]{2,1,0:T(8,128)(2,1)S(1)} %bitcast.30), custom_call_target="tpu_custom_call" | custom-call | tf_op jit(solution)/shard_map/pallas_call | solution.py:110
  141.3 6.4 %all-to-all-start.3 = ((bf16[32,64,128]{2,1,0:T(8,128)(2,1)}), bf16[32,64,128]{2,1,0:T(8,128)(2,1)S(1)}, u32[]{:S(2)}, u32[]{:S(2)}) async-start(bf16[32,64,128]{2,1,0:T(8,128)(2,1)} %bitcast.8), calls=%async_computation.4 | async-start | bytes 1048576 | tf_op jit(solution)/shard_map/all_to_all | solution.py:210
  147.7 2.5 %collective-permute-start.2 = (bf16[1,512]{1,0:T(2,128)(2,1)S(1)}, bf16[1,512]{1,0:T(2,128)(2,1)S(1)}, u32[]{:S(2)}, u32[]{:S(2)}) collective-permute-start(bf16[1,512]{1,0:T(2,128)(2,1)S(1)} %slice.66), channel_id=1, source_target_pairs={{0,248},{8,0},{16,8},{24,16},{32,24},{40,32},{48,40},{56,48},{64,5... | collective-permute-start | bytes 3080 | tf_op jit(solution)/shard_map/ppermute | solution.py:32
  150.3 3.7 %collective-permute-done.2 = bf16[1,512]{1,0:T(2,128)(2,1)S(1)} collective-permute-done((bf16[1,512]{1,0:T(2,128)(2,1)S(1)}, bf16[1,512]{1,0:T(2,128)(2,1)S(1)}, u32[]{:S(2)}, u32[]{:S(2)}) %collective-permute-start.2) | collective-permute-done | bytes 1056 | tf_op jit(solution)/shard_map/ppermute | solution.py:32
  154.0 0.8 pad_maximum_fusion.1
  154.8 2.7 %all-to-all-done.3 = bf16[32,64,128]{2,1,0:T(8,128)(2,1)S(1)} async-done(((bf16[32,64,128]{2,1,0:T(8,128)(2,1)}), bf16[32,64,128]{2,1,0:T(8,128)(2,1)S(1)}, u32[]{:S(2)}, u32[]{:S(2)}) %all-to-all-start.3) | async-done | bytes 524320 | tf_op jit(solution)/shard_map/all_to_all | solution.py:210
  157.4 0.4 copy.30
  157.8 0.2 fusion.15
  158.0 0.9 copy_bitcast_fusion.1
  158.9 3.4 %reduce-scatter.2.cloned.1.call-done = bf16[32,8192]{1,0:T(8,128)(2,1)} async-done(((bf16[256,8192]{1,0:T(8,128)(2,1)}), bf16[32,8192]{1,0:T(8,128)(2,1)}) %reduce-scatter.2.cloned.1.call-update) | async-done | bytes 524304 | tf_op jit(solution)/shard_map/reduce_scatter | solution.py:237
  (10 shorter events, 0.2 us)
Async XLA Ops:
  7.2 76.4 %all-gather.2.cloned.1.call-start = ((), (), s32[]{:S(2)}) async-start(), calls=%async_computation.5 | async-start | bytes 8650752 | tf_op jit(solution)/shard_map/all_gather | solution.py:219
  9.9 28.3 %copy-start.4 = (bf16[256,512]{1,0:T(8,128)(2,1)S(1)}, bf16[256,512]{1,0:T(8,128)(2,1)}, u32[]{:S(2)}) copy-start(bf16[256,512]{1,0:T(8,128)(2,1)} %param.13) | copy-start | bytes 786436
  28.5 0.9 copy-start.3
  32.4 58.2 %all-to-all-start.1 = ((bf16[32,256,128]{2,1,0:T(8,128)(2,1)}), bf16[32,256,128]{2,1,0:T(8,128)(2,1)S(1)}, u32[]{:S(2)}, u32[]{:S(2)}) async-start(bf16[32,256,128]{2,1,0:T(8,128)(2,1)} %bitcast.32), calls=%async_computation.1 | async-start | bytes 4194304 | tf_op jit(solution)/shard_map/all_to_all | solution.py:210
  38.2 124.1 %reduce-scatter.2.cloned.1.call-start = ((), (), s32[]{:S(2)}) async-start(), calls=%async_computation.6 | async-start | bytes 4718592 | tf_op jit(solution)/shard_map/reduce_scatter | solution.py:237
  38.3 37.2 %collective-permute-start.1 = (bf16[1,512]{1,0:T(2,128)(2,1)S(1)}, bf16[1,512]{1,0:T(2,128)(2,1)S(1)}, u32[]{:S(2)}, u32[]{:S(2)}) collective-permute-start(bf16[1,512]{1,0:T(2,128)(2,1)S(1)} %slice.62), channel_id=1, source_target_pairs={{0,8},{8,16},{16,24},{24,32},{32,40},{40,48},{48,56},{56,64},{64,7... | collective-permute-start | bytes 3080 | tf_op jit(solution)/shard_map/ppermute | solution.py:32
  39.5 37.4 %collective-permute-start = (bf16[1,8192]{1,0:T(2,128)(2,1)S(1)}, bf16[1,8192]{1,0:T(2,128)(2,1)S(1)}, u32[]{:S(2)}, u32[]{:S(2)}) collective-permute-start(bf16[1,8192]{1,0:T(2,128)(2,1)S(1)} %slice.60), channel_id=1, source_target_pairs={{0,8},{8,16},{16,24},{24,32},{32,40},{40,48},{48,56},{56,64},{64,7... | collective-permute-start | bytes 49160 | tf_op jit(solution)/shard_map/ppermute | solution.py:32
  83.5 7.0 %copy-start.2 = (s32[32,10]{1,0:T(8,128)S(1)}, s32[32,10]{1,0:T(8,128)}, u32[]{:S(2)}) copy-start(s32[32,10]{1,0:T(8,128)} %pad_add_fusion.facts) | copy-start | bytes 3844
  92.3 7.2 %collective-permute-start.3 = (bf16[1,512]{1,0:T(2,128)(2,1)S(1)}, bf16[1,512]{1,0:T(2,128)(2,1)S(1)}, u32[]{:S(2)}, u32[]{:S(2)}) collective-permute-start(bf16[1,512]{1,0:T(2,128)(2,1)S(1)} %slice.68), channel_id=1, source_target_pairs={{0,248},{8,0},{16,8},{24,16},{32,24},{40,32},{48,40},{56,48},{64,5... | collective-permute-start | bytes 3080 | tf_op jit(solution)/shard_map/ppermute | solution.py:32
  98.2 1.3 copy-start
  107.3 1.6 copy-start.1
  141.3 16.1 %all-to-all-start.3 = ((bf16[32,64,128]{2,1,0:T(8,128)(2,1)}), bf16[32,64,128]{2,1,0:T(8,128)(2,1)S(1)}, u32[]{:S(2)}, u32[]{:S(2)}) async-start(bf16[32,64,128]{2,1,0:T(8,128)(2,1)} %bitcast.8), calls=%async_computation.4 | async-start | bytes 1048576 | tf_op jit(solution)/shard_map/all_to_all | solution.py:210
  147.7 6.3 %collective-permute-start.2 = (bf16[1,512]{1,0:T(2,128)(2,1)S(1)}, bf16[1,512]{1,0:T(2,128)(2,1)S(1)}, u32[]{:S(2)}, u32[]{:S(2)}) collective-permute-start(bf16[1,512]{1,0:T(2,128)(2,1)S(1)} %slice.66), channel_id=1, source_target_pairs={{0,248},{8,0},{16,8},{24,16},{32,24},{40,32},{48,40},{56,48},{64,5... | collective-permute-start | bytes 3080 | tf_op jit(solution)/shard_map/ppermute | solution.py:32
Sparse Core Ops, SparseCore 0:
  10.6 72.9 all-gather.1
  107.4 54.8 reduce-scatter.1

commit v4 on v3

--- a/solution.py
+++ b/solution.py
@@ -1,5 +1,3 @@
-import functools
-
 import jax
 import jax.numpy as jnp
 from jax import lax
@@ -13,6 +11,7 @@
 SEQ_LEN = 2048
 RIM = GROUP - 1
 NS = 32
+NM = 8
 TOK = 256
 FT = 512
 DM = 8192
@@ -117,33 +116,34 @@
     )(facts, terms)
 
 
-def attend_kernel(groups, heads, seat, facts, q, g, kv, *rest):
-    before, (att, gq, terms) = rest[:-3], rest[-3:]
-
-    def mm(p, r, dims):
-        return lax.dot_general(p, r, (dims, ((), ())), preferred_element_type=F32)
-
+def mm(p, r, dims):
+    return lax.dot_general(p, r, (dims, ((), ())), preferred_element_type=F32)
+
+
+def attend_units(units, seat, facts, q, g, kv, att, gq, terms, first):
     scale = HD ** (-0.5)
     lane = lax.broadcasted_iota(jnp.int32, (GROUP, 2 * NLEN), 1)
-    units = [(h, i) for h in range(heads) for i in range(len(groups))]
     count = range(len(units))
-    valid = []
-    for grp in groups:
+    valid = {}
+    for grp in sorted({grp for _, grp in units}):
         blk0, blk1 = facts[seat[0], 2 * grp], facts[seat[0], 2 * grp + 1]
         len0 = facts[lax.shift_right_logical(blk0, 1), NP + jnp.bitwise_and(blk0, 1)]
         len1 = facts[lax.shift_right_logical(blk1, 1), NP + jnp.bitwise_and(blk1, 1)]
-        valid.append(lane < jnp.where(lane < NLEN, len0, len1 + NLEN))
-    cols = [slice(h * HD, (h + 1) * HD) for h in range(heads)]
-    rows = [slice(i * GROUP, (i + 1) * GROUP) for i in range(len(groups))]
-    tok = [slice(grp * GROUP, (grp + 1) * GROUP) for grp in groups]
-
-    def block(which, h, i):
-        return jnp.concatenate([kv[which, h, r, 2 * groups[i] + n] for n in range(2) for r in range(RQ)], 0)
-
-    qs = [q[tok[i], cols[h]] for h, i in units]
-    gs = [g[tok[i], cols[h]] for h, i in units]
-    keys = [block(0, h, i) for h, i in units]
-    vals = [block(1, h, i) for h, i in units]
+        valid[grp] = lane < jnp.where(lane < NLEN, len0, len1 + NLEN)
+
+    def cols(h):
+        return slice(h * HD, (h + 1) * HD)
+
+    def rows(grp):
+        return slice(grp * GROUP, (grp + 1) * GROUP)
+
+    def block(which, h, grp):
+        return jnp.concatenate([kv[which, h, r, 2 * grp + n] for n in range(2) for r in range(RQ)], 0)
+
+    qs = [q[rows(grp), cols(h)] for h, grp in units]
+    gs = [g[rows(grp), cols(h)] for h, grp in units]
+    keys = [block(0, h, grp) for h, grp in units]
+    vals = [block(1, h, grp) for h, grp in units]
     scores = [mm(qs[u], keys[u], ((1,), (1,))) for u in count]
     grad_prob = [mm(gs[u], vals[u], ((1,), (1,))) for u in count]
     ex, inv = [], []
@@ -163,47 +163,87 @@
         ds.append((prob[u] * (grad_prob[u] - delta) * scale).astype(BF))
     gqs = [mm(ds[u], keys[u], ((1,), (0,))).astype(BF) for u in count]
     kt = [mm(ds[u], qs[u], ((0,), (0,))).astype(BF) for u in count]
-    shift = 2 * groups[0] if before else 0
-    if before:
-        terms[:, :, :, :shift] = before[0][...]
-    for u, (h, i) in enumerate(units):
-        att[rows[i], cols[h]] = outs[u]
-        gq[rows[i], cols[h]] = gqs[u]
+    for u, (h, grp) in enumerate(units):
+        att[rows(grp - first), cols(h)] = outs[u]
+        gq[rows(grp - first), cols(h)] = gqs[u]
         for n in range(2):
             for r in range(RQ):
                 part = slice((n * RQ + r) * QR, (n * RQ + r + 1) * QR)
-                terms[0, h, r, shift + 2 * i + n] = kt[u][part]
-                terms[1, h, r, shift + 2 * i + n] = vt[u][part]
-
-
-def attend(groups, heads, seat, facts, q, g, kv, before=None):
-    count = len(groups) * GROUP
-    pairs = 2 * len(groups) if before is None else NP
-    tok = pl.BlockSpec((TOK, heads * HD), lambda h, *_: (0, h))
-    out = pl.BlockSpec((count, heads * HD), lambda h, *_: (0, h))
-
-    def mem(n):
-        return pl.BlockSpec((2, heads, RQ, n, QR, HD), lambda h, *_: (0, h, 0, 0, 0, 0))
-
-    rows = jax.ShapeDtypeStruct((count, FT), BF)
-    read = NP if before is not None else 2
-    specs, operands = [tok, tok, mem(read)], (q, g, kv)
-    if before is not None:
-        specs, operands = specs + [mem(before.shape[3])], operands + (before,)
+                terms[0, h, r, 2 * grp + n] = kt[u][part]
+                terms[1, h, r, 2 * grp + n] = vt[u][part]
+
+
+def core_kernel(seat, facts, g, h, w, kv, att, whole, out, q, gq, terms, hbuf, wbuf, kvbuf, buf, in_sems, out_sems, sems):
+    parts = wbuf.shape[0]
+    size = DM // parts
+
+    def loads(i):
+        at = pl.ds(i * size, size)
+        return (
+            pltpu.make_async_copy(w.at[at], wbuf.at[i], in_sems.at[0, i]),
+            pltpu.make_async_copy(h.at[:, at], hbuf.at[i], in_sems.at[1, i]),
+        )
+
+    def store(i):
+        return pltpu.make_async_copy(buf.at[i], out.at[:, pl.ds(i * size, size)], out_sems.at[i])
+
+    for i in range(parts):
+        for cp in loads(i):
+            cp.start()
+    blocks = pltpu.make_async_copy(kv, kvbuf, sems.at[0])
+    blocks.start()
+    acc = None
+    for i in range(parts):
+        for cp in loads(i):
+            cp.wait()
+        term = jnp.dot(hbuf[i], wbuf[i], preferred_element_type=F32)
+        acc = term if acc is None else acc + term
+    q[...] = acc.astype(BF)
+    blocks.wait()
+    for half in range(2):
+        units = [(head, grp) for head in (2 * half, 2 * half + 1) for grp in range(TOK // GROUP)]
+        attend_units(units, seat, facts, q, g, kvbuf, att, gq, terms, 0)
+    keep = pltpu.make_async_copy(terms, whole, sems.at[1])
+    keep.start()
+    for i in range(parts):
+        buf[i] = mm(gq[...], wbuf[i], ((1,), (1,))).astype(BF)
+        store(i).start()
+    for i in range(parts):
+        store(i).wait()
+    keep.wait()
+
+
+def attend(seat, facts, g, h, weight, kv, parts=8):
+    def full(*shape):
+        return pl.BlockSpec(shape, lambda i, *_: (0,) * len(shape))
+
+    anywhere = pl.BlockSpec(memory_space=pl.ANY)
+    whole = (2, NH, RQ, NP, QR, HD)
+    rows = jax.ShapeDtypeStruct((TOK, FT), BF)
     return pl.pallas_call(
-        functools.partial(attend_kernel, groups, heads),
-        out_shape=(rows, rows, jax.ShapeDtypeStruct((2, NH, RQ, pairs, QR, HD), BF)),
+        core_kernel,
+        out_shape=(rows, jax.ShapeDtypeStruct(whole, BF), jax.ShapeDtypeStruct((TOK, DM), BF)),
         grid_spec=pltpu.PrefetchScalarGridSpec(
             num_scalar_prefetch=2,
-            grid=(NH // heads,),
-            in_specs=specs,
-            out_specs=(out, out, mem(pairs)),
+            grid=(1,),
+            in_specs=[full(TOK, FT), anywhere, anywhere, anywhere],
+            out_specs=(full(TOK, FT), anywhere, anywhere),
+            scratch_shapes=[
+                pltpu.VMEM((TOK, FT), BF),
+                pltpu.VMEM((TOK, FT), BF),
+                pltpu.VMEM(whole, BF),
+                pltpu.VMEM((parts, TOK, DM // parts), BF),
+                pltpu.VMEM((parts, DM // parts, FT), BF),
+                pltpu.VMEM(whole, BF),
+                pltpu.VMEM((parts, TOK, DM // parts), BF),
+                pltpu.SemaphoreType.DMA((2, parts)),
+                pltpu.SemaphoreType.DMA((parts,)),
+                pltpu.SemaphoreType.DMA((2,)),
+            ],
         ),
-        compiler_params=pltpu.CompilerParams(vmem_limit_bytes=32 * MIB),
-        cost_estimate=pl.CostEstimate(
-            flops=100_000_000 * len(groups), bytes_accessed=2 * MIB * len(groups), transcendentals=0
-        ),
-    )(seat, facts, *operands)
+        compiler_params=pltpu.CompilerParams(vmem_limit_bytes=50 * MIB),
+        cost_estimate=pl.CostEstimate(flops=4 * TOK * DM * FT, bytes_accessed=20 * MIB, transcendentals=0),
+    )(seat, facts, g, h, weight, kv)
 
 
 def swap_all(v):
@@ -216,9 +256,10 @@
     seat = s.astype(jnp.int32).reshape(1)
     zero = jnp.zeros((), BF)
 
+    pay = prepare(nbr_block.T, block_len, key_memory, value_memory)
+    pay, query_weight = lax.optimization_barrier((pay, query_weight))
     weight = lax.all_gather(query_weight, "seq", axis=0, tiled=True)
-
-    held = swap_all(prepare(nbr_block.T, block_len, key_memory, value_memory))
+    held = swap_all(pay)
     facts = held[:, 2 * QR, : NP + 2].astype(jnp.int32)
     facts = jnp.concatenate([jnp.roll(facts[:, NP - 2 : NP], 1, axis=0), facts[:, : NP - 2], facts[:, NP:]], 1)
     sent = pick(facts, held).reshape(NS, NP * QR, HD)
@@ -227,27 +268,18 @@
     h_prev, g_prev = to_seq(hidden[TOK - 1 :], 1), to_seq(out_grad[TOK - 1 :], 1)
     h_rows = jnp.concatenate([h_prev, hidden[: TOK - 1]], 0)
     g_rows = jnp.concatenate([g_prev, jnp.where(starts, zero, out_grad[:RIM]), out_grad[RIM : TOK - 1]], 0)
-    queries = jnp.dot(h_rows, weight, preferred_element_type=F32).astype(BF)
-
-    att_rim, gq_rim, terms = attend((0,), NH, seat, facts, queries, g_rows, kv)
-    gq_last, att_last = to_seq(gq_rim[:1], -1), to_seq(att_rim[:1], -1)
-    att, gq, terms = attend((1, 2, 3), 2, seat, facts, queries, g_rows, kv, terms)
-
-    query_grad = jnp.concatenate([jnp.where(starts, zero, gq_rim[1:]), gq, gq_last], 0)
-    run = lax.psum_scatter(
-        lax.dot_general(
-            query_grad, weight, (((1,), (1,)), ((), ())), preferred_element_type=F32
-        ).astype(BF),
-        "mp",
-        scatter_dimension=0,
-        tiled=True,
-    )
+    att, terms, partial = attend(seat, facts, g_rows, h_rows, weight, kv)
+    att_last = to_seq(att[:1], -1)
+    run = lax.psum_scatter(partial, "mp", scatter_dimension=0, tiled=True)
+    count = NS * NM
+    run_last = lax.ppermute(run[:1], ("seq", "mp"), [(i, (i - 1) % count) for i in range(count)])
+    run = jnp.concatenate([run[1:], run_last], 0)
     got = swap_all(terms.reshape(NS, NP * QR, HD))
     sums = total(facts, got.reshape(NS * NP, QR, HD)).reshape(NS, 2 * QR, HD)
     back = swap_all(sums).reshape(2, NH, RQ, 2, QR, HD)
     grads = back.transpose(0, 3, 2, 4, 1, 5).reshape(2, 2 * NLEN, FT)
 
-    attended = jnp.concatenate([jnp.where(starts, zero, att_rim[1:]), att, att_last], 0)
+    attended = jnp.concatenate([jnp.where(starts, zero, att[1:GROUP]), att[GROUP:], att_last], 0)
     return attended, run, grads[0], grads[1]
 
 

time: 171 us -> 166 us (0.971)
  matrix products: 14.7 us -> 0 us
  Pallas kernels: 12.9 us -> 19.7 us
  other arithmetic: 1.53 us -> 7.66 us
  waiting for transfers between devices: 53 us -> 49.3 us
    dot_general x2 -> x0, matrix products: 14.7 us -> none  [the longest x1 7.74 us: shards(): lax.dot_general(query_grad, weight, (((1,), (1,)), ((), ())), preferred_e...]
    pallas_call x2 -> x1, Pallas kernels: 5.02 us -> 11.9 us  [attend(): pl.pallas_call(core_kernel, out_shape=(rows, jax.ShapeDtypeStruct(whole,...]
    concatenate x1 -> x3, other arithmetic: 0.76 us -> 6.91 us  [the longest x1 5.29 us: shards(): h_rows = jnp.concatenate([h_prev, hidden[:TOK - 1]], 0)]
    all_gather x1, waiting for transfers between devices: 6.66 us -> 1.83 us  [shards(): weight = lax.all_gather(query_weight, 'seq', axis=0, tiled=True)]
    ppermute x0 -> x1, starting transfers between devices: none -> 3.48 us  [shards(): lax.ppermute(run[:1], ('seq', 'mp'), [(i, (i - 1) % count) for i in range...]
    unnamed x10 -> x8, local copies, waits for them, and re-layouts: 2.92 us -> 0.02 us
    ppermute x4 -> x3, starting transfers between devices: 6.75 us -> 4.24 us  [to_seq(): return lax.ppermute(v, 'seq', [(i, (i + by) % NS) for i in range(NS)])]
    reduce_scatter x1, waiting for transfers between devices: 3.43 us -> 5.69 us  [shards(): run = lax.psum_scatter(partial, 'mp', scatter_dimension=0, tiled=True)]
  transfers between devices with their start and end apart: 8 -> 8, of which waited for: 6 -> 6; matrix products, arithmetic and copies ran while one was open for 7% -> 6% of each run, Pallas kernels for 7% -> 3%
where the time goes in v4:
time: 166 us; the launch traced here: 165 us
  blocking collectives  49.5 us (30%)
  waiting for transfers between devices  49.3 us (30%)
  starting transfers between devices  20 us (12%)
  Pallas kernels  19.7 us (12%)
  between operations  14.2 us (9%)
  other arithmetic  7.66 us (5%)
  local copies, waits for them, and re-layouts  4.8 us (3%)
    all_to_all x2, blocking collectives, swap_all(): return lax.all_to_all(v, 'seq', split_axis=0, concat_axis=0, tiled=True)  49.5 us
    ppermute x3, waiting for transfers between devices, to_seq(): return lax.ppermute(v, 'seq', [(i, (i + by) % NS) for i in range(NS)])  39.1 us
    all_to_all x2, starting transfers between devices, swap_all(): return lax.all_to_all(v, 'seq', split_axis=0, concat_axis=0, tiled=True)  12.2 us
    pallas_call x1, Pallas kernels, attend(): pl.pallas_call(core_kernel, out_shape=(rows, jax.ShapeDtypeStruct(whole,...  11.9 us
    reduce_scatter x1, waiting for transfers between devices, shards(): run = lax.psum_scatter(partial, 'mp', scatter_dimension=0, tiled=True)  5.69 us
    concatenate x1, other arithmetic, shards(): h_rows = jnp.concatenate([h_prev, hidden[:TOK - 1]], 0)  5.29 us
    ppermute x3, starting transfers between devices, to_seq(): return lax.ppermute(v, 'seq', [(i, (i + by) % NS) for i in range(NS)])  4.24 us
    ppermute x1, starting transfers between devices, shards(): lax.ppermute(run[:1], ('seq', 'mp'), [(i, (i - 1) % count) for i in range...  3.48 us
  transfers between devices with their start and end apart: 8, of which 6 were waited for; matrix products, arithmetic and copies ran while one was open for 6% of the time, Pallas kernels for 3%

profile of v4, /device:TPU:2, one launch (start us, length us, event | category | flops | bytes accessed | tf_op | source)
XLA Modules:
  0.0 165.2 jit_solution(14581403907442181537)
XLA Ops:
  7.2 0.0 all-gather.2.cloned.1.call-start
  7.2 2.0 %shard_map.102 = bf16[32,80,128]{2,1,0:T(8,128)(2,1)} custom-call(s32[2,4]{1,0:T(2,128)} %bitcast.36, s32[2]{0:T(128)} %lens.1, bf16[256,512]{1,0:T(8,128)(2,1)} %key.1, bf16[256,512]{1,0:T(8,128)(2,1)} %value.1), custom_call_target="tpu_custom_call" | custom-call | tf_op jit(solution)/shard_map/pallas_call | solution.py:58
  9.2 0.0 all-gather.2.cloned.1.call-update
  9.3 0.0 copy-start.3
  9.3 18.6 %all_to_all.20.held = bf16[32,80,128]{2,1,0:T(8,128)(2,1)S(1)} all-to-all(bf16[32,80,128]{2,1,0:T(8,128)(2,1)} %shard_map.102), channel_id=1, replica_groups=mesh['seq'=32,'mp'=8] {'seq'}, dimensions={0} | all-to-all | bytes 1310720 | tf_op jit(solution)/shard_map/all_to_all | solution.py:250
  27.9 0.0 copy-start.1
  27.9 0.1 slice.76
  28.0 0.1 slice.79
  28.1 0.1 slice.77
  28.1 0.7 pad_add_fusion.facts
  28.8 0.0 copy-done.1
  28.8 2.9 %shard_map.103 = bf16[256,32,128]{2,1,0:T(8,128)(2,1)} custom-call(s32[32,10]{1,0:T(8,128)} %pad_add_fusion.facts, bf16[32,80,128]{2,1,0:T(8,128)(2,1)} %copy-done.1), custom_call_target="tpu_custom_call" | custom-call | bytes 1024 | tf_op jit(solution)/shard_map/pallas_call | solution.py:84
  31.7 5.8 %all-to-all-start.1 = ((bf16[32,256,128]{2,1,0:T(8,128)(2,1)}), bf16[32,256,128]{2,1,0:T(8,128)(2,1)S(1)}, u32[]{:S(2)}, u32[]{:S(2)}) async-start(bf16[32,256,128]{2,1,0:T(8,128)(2,1)} %bitcast.28), calls=%async_computation.1 | async-start | bytes 4194304 | tf_op jit(solution)/shard_map/all_to_all | solution.py:250
  37.5 0.0 reduce-scatter.2.cloned.1.call-start
  37.6 0.0 copy-done.3
  37.6 0.2 collective-permute-start
  37.8 0.9 slice.66
  38.8 1.5 collective-permute-start.1
  40.3 34.0 %collective-permute-done = bf16[1,512]{1,0:T(2,128)(2,1)S(1)} collective-permute-done((bf16[1,512]{1,0:T(2,128)(2,1)S(1)}, bf16[1,512]{1,0:T(2,128)(2,1)S(1)}, u32[]{:S(2)}, u32[]{:S(2)}) %collective-permute-start) | collective-permute-done | bytes 1056 | tf_op jit(solution)/shard_map/ppermute | solution.py:31
  74.4 1.4 collective-permute-done.1
  75.7 0.0 copy-start
  75.7 5.3 %pad_maximum_fusion.h = bf16[256,8192]{1,0:T(8,128)(2,1)} fusion(bf16[255,8192]{1,0:T(8,128)(2,1)} %bitcast.29, bf16[1,8192]{1,0:T(2,128)(2,1)S(1)} %collective-permute-done.1), kind=kLoop, calls=%fused_computation | loop fusion | flops 8388608 | bytes 8388608 | tf_op jit(solution)/shard_map/concatenate | solution.py:269
  81.0 0.0 all-to-all-done.1
  81.0 0.0 copy-start.2
  81.0 1.8 %all-gather.2.cloned.1.call-done.w = bf16[8192,512]{1,0:T(8,128)(2,1)} async-done(((bf16[256,512]{1,0:T(8,128)(2,1)}), bf16[8192,512]{1,0:T(8,128)(2,1)}) %all-gather.2.cloned.1.call-update) | async-done | bytes 8388624 | tf_op jit(solution)/shard_map/all_gather | solution.py:261
  82.9 0.0 copy-done.2
  82.9 0.0 copy-done
  82.9 11.9 %shard_map.104 = (bf16[256,512]{1,0:T(8,128)(2,1)S(1)}, bf16[2,4,4,8,32,128]{5,4,3,2,1,0:T(8,128)(2,1)S(1)}, bf16[256,8192]{1,0:T(8,128)(2,1)}) custom-call(s32[1]{0:T(128)} %bitcast.seat, s32[32,10]{1,0:T(8,128)S(1)} %copy-done, bf16[256,512]{1,0:T(8,128)(2,1)S(1)} %pad_maximum_fusion.2.g, bf16[256,8192]{1,0:T(8,128)(2,1)} %pad_maximum_fusion.h, ...), custom_call_target="tpu_custom_call" | custom-call | flops 4294967296 | bytes 20971520 | tf_op jit(solution)/shard_map/pallas_call | solution.py:223
  94.8 0.0 reduce-scatter.2.cloned.1.call-update
  94.8 30.9 %all_to_all.21 = bf16[32,256,128]{2,1,0:T(8,128)(2,1)S(1)} all-to-all(bf16[32,256,128]{2,1,0:T(8,128)(2,1)S(1)} %bitcast.27), channel_id=1, replica_groups=mesh['seq'=32,'mp'=8] {'seq'}, dimensions={0} | all-to-all | bytes 4194304 | tf_op jit(solution)/shard_map/all_to_all | solution.py:250
  125.7 2.9 %shard_map.105 = bf16[64,32,128]{2,1,0:T(8,128)(2,1)} custom-call(s32[32,10]{1,0:T(8,128)S(1)} %copy-done, bf16[256,32,128]{2,1,0:T(8,128)(2,1)S(1)} %bitcast.26), custom_call_target="tpu_custom_call" | custom-call | tf_op jit(solution)/shard_map/pallas_call | solution.py:109
  128.6 6.4 %all-to-all-start.3 = ((bf16[32,64,128]{2,1,0:T(8,128)(2,1)}), bf16[32,64,128]{2,1,0:T(8,128)(2,1)S(1)}, u32[]{:S(2)}, u32[]{:S(2)}) async-start(bf16[32,64,128]{2,1,0:T(8,128)(2,1)} %bitcast.8), calls=%async_computation.4 | async-start | bytes 1048576 | tf_op jit(solution)/shard_map/all_to_all | solution.py:250
  135.0 2.5 %collective-permute-start.2 = (bf16[1,512]{1,0:T(2,128)(2,1)S(1)}, bf16[1,512]{1,0:T(2,128)(2,1)S(1)}, u32[]{:S(2)}, u32[]{:S(2)}) collective-permute-start(bf16[1,512]{1,0:T(2,128)(2,1)S(1)} %slice.70), channel_id=1, source_target_pairs={{0,248},{8,0},{16,8},{24,16},{32,24},{40,32},{48,40},{56,48},{64,5... | collective-permute-start | bytes 3080 | tf_op jit(solution)/shard_map/ppermute | solution.py:31
  137.6 3.7 %collective-permute-done.2 = bf16[1,512]{1,0:T(2,128)(2,1)S(1)} collective-permute-done((bf16[1,512]{1,0:T(2,128)(2,1)S(1)}, bf16[1,512]{1,0:T(2,128)(2,1)S(1)}, u32[]{:S(2)}, u32[]{:S(2)}) %collective-permute-start.2) | collective-permute-done | bytes 1056 | tf_op jit(solution)/shard_map/ppermute | solution.py:31
  141.3 0.8 pad_maximum_fusion.3
  142.0 2.7 %all-to-all-done.3 = bf16[32,64,128]{2,1,0:T(8,128)(2,1)S(1)} async-done(((bf16[32,64,128]{2,1,0:T(8,128)(2,1)}), bf16[32,64,128]{2,1,0:T(8,128)(2,1)S(1)}, u32[]{:S(2)}, u32[]{:S(2)}) %all-to-all-start.3) | async-done | bytes 524320 | tf_op jit(solution)/shard_map/all_to_all | solution.py:250
  144.7 0.4 copy.30
  145.1 0.2 fusion.1
  145.3 5.7 %reduce-scatter.2.cloned.1.call-done = bf16[32,8192]{1,0:T(8,128)(2,1)} async-done(((bf16[256,8192]{1,0:T(8,128)(2,1)}), bf16[32,8192]{1,0:T(8,128)(2,1)}) %reduce-scatter.2.cloned.1.call-update) | async-done | bytes 524304 | tf_op jit(solution)/shard_map/reduce_scatter | solution.py:273
  151.0 0.9 slice.81
  151.9 3.5 %collective-permute-start.3 = (bf16[1,8192]{1,0:T(2,128)(2,1)S(1)}, bf16[1,8192]{1,0:T(2,128)(2,1)S(1)}, u32[]{:S(2)}, u32[]{:S(2)}) collective-permute-start(bf16[1,8192]{1,0:T(2,128)(2,1)S(1)} %slice.81), channel_id=1, source_target_pairs={{0,255},{1,0},{2,1},{3,2},{4,3},{5,4},{6,5},{7,6},{8,7},{9,8},{10,... | collective-permute-start | bytes 49160 | tf_op jit(solution)/shard_map/ppermute | solution.py:275
  155.4 0.9 copy_bitcast_fusion.1
  156.3 1.2 slice.80
  157.4 0.0 collective-permute-done.3
  157.5 0.9 pad_maximum_fusion.1
  (9 shorter events, 0.2 us)
Async XLA Ops:
  7.2 75.7 %all-gather.2.cloned.1.call-start = ((), (), s32[]{:S(2)}) async-start(), calls=%async_computation.5 | async-start | bytes 8650752 | tf_op jit(solution)/shard_map/all_gather | solution.py:261
  9.3 28.3 %copy-start.3 = (bf16[256,512]{1,0:T(8,128)(2,1)S(1)}, bf16[256,512]{1,0:T(8,128)(2,1)}, u32[]{:S(2)}) copy-start(bf16[256,512]{1,0:T(8,128)(2,1)} %param.13) | copy-start | bytes 786436
  27.9 0.9 copy-start.1
  31.7 49.3 %all-to-all-start.1 = ((bf16[32,256,128]{2,1,0:T(8,128)(2,1)}), bf16[32,256,128]{2,1,0:T(8,128)(2,1)S(1)}, u32[]{:S(2)}, u32[]{:S(2)}) async-start(bf16[32,256,128]{2,1,0:T(8,128)(2,1)} %bitcast.28), calls=%async_computation.1 | async-start | bytes 4194304 | tf_op jit(solution)/shard_map/all_to_all | solution.py:250
  37.5 113.5 %reduce-scatter.2.cloned.1.call-start = ((), (), s32[]{:S(2)}) async-start(), calls=%async_computation.6 | async-start | bytes 4718592 | tf_op jit(solution)/shard_map/reduce_scatter | solution.py:273
  37.6 36.7 %collective-permute-start = (bf16[1,512]{1,0:T(2,128)(2,1)S(1)}, bf16[1,512]{1,0:T(2,128)(2,1)S(1)}, u32[]{:S(2)}, u32[]{:S(2)}) collective-permute-start(bf16[1,512]{1,0:T(2,128)(2,1)S(1)} %slice.63), channel_id=1, source_target_pairs={{0,8},{8,16},{16,24},{24,32},{32,40},{40,48},{48,56},{56,64},{64,7... | collective-permute-start | bytes 3080 | tf_op jit(solution)/shard_map/ppermute | solution.py:31
  38.8 37.0 %collective-permute-start.1 = (bf16[1,8192]{1,0:T(2,128)(2,1)S(1)}, bf16[1,8192]{1,0:T(2,128)(2,1)S(1)}, u32[]{:S(2)}, u32[]{:S(2)}) collective-permute-start(bf16[1,8192]{1,0:T(2,128)(2,1)S(1)} %slice.66), channel_id=1, source_target_pairs={{0,8},{8,16},{16,24},{24,32},{32,40},{40,48},{48,56},{56,64},{64,7... | collective-permute-start | bytes 49160 | tf_op jit(solution)/shard_map/ppermute | solution.py:31
  75.7 7.1 %copy-start = (s32[32,10]{1,0:T(8,128)S(1)}, s32[32,10]{1,0:T(8,128)}, u32[]{:S(2)}) copy-start(s32[32,10]{1,0:T(8,128)} %pad_add_fusion.facts) | copy-start | bytes 3844
  81.0 1.8 %copy-start.2 = (bf16[32,256,128]{2,1,0:T(8,128)(2,1)}, bf16[32,256,128]{2,1,0:T(8,128)(2,1)S(1)}, u32[]{:S(2)}) copy-start(bf16[32,256,128]{2,1,0:T(8,128)(2,1)S(1)} %all-to-all-done.1) | copy-start | bytes 6291460
  128.6 16.1 %all-to-all-start.3 = ((bf16[32,64,128]{2,1,0:T(8,128)(2,1)}), bf16[32,64,128]{2,1,0:T(8,128)(2,1)S(1)}, u32[]{:S(2)}, u32[]{:S(2)}) async-start(bf16[32,64,128]{2,1,0:T(8,128)(2,1)} %bitcast.8), calls=%async_computation.4 | async-start | bytes 1048576 | tf_op jit(solution)/shard_map/all_to_all | solution.py:250
  135.0 6.3 %collective-permute-start.2 = (bf16[1,512]{1,0:T(2,128)(2,1)S(1)}, bf16[1,512]{1,0:T(2,128)(2,1)S(1)}, u32[]{:S(2)}, u32[]{:S(2)}) collective-permute-start(bf16[1,512]{1,0:T(2,128)(2,1)S(1)} %slice.70), channel_id=1, source_target_pairs={{0,248},{8,0},{16,8},{24,16},{32,24},{40,32},{48,40},{56,48},{64,5... | collective-permute-start | bytes 3080 | tf_op jit(solution)/shard_map/ppermute | solution.py:31
  151.9 5.5 %collective-permute-start.3 = (bf16[1,8192]{1,0:T(2,128)(2,1)S(1)}, bf16[1,8192]{1,0:T(2,128)(2,1)S(1)}, u32[]{:S(2)}, u32[]{:S(2)}) collective-permute-start(bf16[1,8192]{1,0:T(2,128)(2,1)S(1)} %slice.81), channel_id=1, source_target_pairs={{0,255},{1,0},{2,1},{3,2},{4,3},{5,4},{6,5},{7,6},{8,7},{9,8},{10,... | collective-permute-start | bytes 49160 | tf_op jit(solution)/shard_map/ppermute | solution.py:275
Sparse Core Ops, SparseCore 0:
  10.6 72.2 all-gather.1
  94.9 56.0 reduce-scatter.1

commit v5 on v4

--- a/solution.py
+++ b/solution.py
@@ -200,9 +200,8 @@
         acc = term if acc is None else acc + term
     q[...] = acc.astype(BF)
     blocks.wait()
-    for half in range(2):
-        units = [(head, grp) for head in (2 * half, 2 * half + 1) for grp in range(TOK // GROUP)]
-        attend_units(units, seat, facts, q, g, kvbuf, att, gq, terms, 0)
+    units = [(head, grp) for head in range(NH) for grp in range(TOK // GROUP)]
+    attend_units(units, seat, facts, q, g, kvbuf, att, gq, terms, 0)
     keep = pltpu.make_async_copy(terms, whole, sems.at[1])
     keep.start()
     for i in range(parts):

time: 166 us -> 165 us (level)
  no operation moved by 1% of the time
where the time goes in v5:
time: 165 us
  blocking collectives  49.5 us (30%)
  waiting for transfers between devices  49.3 us (30%)
  starting transfers between devices  20 us (12%)
  Pallas kernels  19.3 us (12%)
  between operations  14.2 us (9%)
  other arithmetic  7.66 us (5%)
  local copies, waits for them, and re-layouts  4.8 us (3%)
    all_to_all x2, blocking collectives, swap_all(): return lax.all_to_all(v, 'seq', split_axis=0, concat_axis=0, tiled=True)  49.5 us
    ppermute x3, waiting for transfers between devices, to_seq(): return lax.ppermute(v, 'seq', [(i, (i + by) % NS) for i in range(NS)])  39.1 us
    all_to_all x2, starting transfers between devices, swap_all(): return lax.all_to_all(v, 'seq', split_axis=0, concat_axis=0, tiled=True)  12.2 us
    pallas_call x1, Pallas kernels, attend(): pl.pallas_call(core_kernel, out_shape=(rows, jax.ShapeDtypeStruct(whole,...  11.5 us
    reduce_scatter x1, waiting for transfers between devices, shards(): run = lax.psum_scatter(partial, 'mp', scatter_dimension=0, tiled=True)  5.69 us
    concatenate x1, other arithmetic, shards(): h_rows = jnp.concatenate([h_prev, hidden[:TOK - 1]], 0)  5.29 us
    ppermute x3, starting transfers between devices, to_seq(): return lax.ppermute(v, 'seq', [(i, (i + by) % NS) for i in range(NS)])  4.24 us
    ppermute x1, starting transfers between devices, shards(): lax.ppermute(run[:1], ('seq', 'mp'), [(i, (i - 1) % count) for i in range...  3.48 us
  transfers between devices with their start and end apart: 8, of which 6 were waited for; matrix products, arithmetic and copies ran while one was open for 6% of the time, Pallas kernels for 3%

profile of v5, /device:TPU:2, one launch (start us, length us, event | category | flops | bytes accessed | tf_op | source)
XLA Modules:
  0.0 164.8 jit_solution(1719898553924969824)
XLA Ops:
  7.2 0.0 all-gather.2.cloned.1.call-start
  7.2 2.0 %shard_map.102 = bf16[32,80,128]{2,1,0:T(8,128)(2,1)} custom-call(s32[2,4]{1,0:T(2,128)} %bitcast.36, s32[2]{0:T(128)} %lens.1, bf16[256,512]{1,0:T(8,128)(2,1)} %key.1, bf16[256,512]{1,0:T(8,128)(2,1)} %value.1), custom_call_target="tpu_custom_call" | custom-call | tf_op jit(solution)/shard_map/pallas_call | solution.py:58
  9.2 0.0 all-gather.2.cloned.1.call-update
  9.3 0.0 copy-start.3
  9.3 18.6 %all_to_all.20.held = bf16[32,80,128]{2,1,0:T(8,128)(2,1)S(1)} all-to-all(bf16[32,80,128]{2,1,0:T(8,128)(2,1)} %shard_map.102), channel_id=1, replica_groups=mesh['seq'=32,'mp'=8] {'seq'}, dimensions={0} | all-to-all | bytes 1310720 | tf_op jit(solution)/shard_map/all_to_all | solution.py:249
  27.9 0.0 copy-start.1
  27.9 0.1 slice.76
  28.0 0.1 slice.79
  28.1 0.1 slice.77
  28.1 0.7 pad_add_fusion.facts
  28.8 0.0 copy-done.1
  28.8 2.9 %shard_map.103 = bf16[256,32,128]{2,1,0:T(8,128)(2,1)} custom-call(s32[32,10]{1,0:T(8,128)} %pad_add_fusion.facts, bf16[32,80,128]{2,1,0:T(8,128)(2,1)} %copy-done.1), custom_call_target="tpu_custom_call" | custom-call | bytes 1024 | tf_op jit(solution)/shard_map/pallas_call | solution.py:84
  31.7 5.8 %all-to-all-start.1 = ((bf16[32,256,128]{2,1,0:T(8,128)(2,1)}), bf16[32,256,128]{2,1,0:T(8,128)(2,1)S(1)}, u32[]{:S(2)}, u32[]{:S(2)}) async-start(bf16[32,256,128]{2,1,0:T(8,128)(2,1)} %bitcast.28), calls=%async_computation.1 | async-start | bytes 4194304 | tf_op jit(solution)/shard_map/all_to_all | solution.py:249
  37.5 0.0 reduce-scatter.2.cloned.1.call-start
  37.6 0.0 copy-done.3
  37.6 0.2 collective-permute-start
  37.8 0.9 slice.66
  38.8 1.5 collective-permute-start.1
  40.3 34.0 %collective-permute-done = bf16[1,512]{1,0:T(2,128)(2,1)S(1)} collective-permute-done((bf16[1,512]{1,0:T(2,128)(2,1)S(1)}, bf16[1,512]{1,0:T(2,128)(2,1)S(1)}, u32[]{:S(2)}, u32[]{:S(2)}) %collective-permute-start) | collective-permute-done | bytes 1056 | tf_op jit(solution)/shard_map/ppermute | solution.py:31
  74.4 1.4 collective-permute-done.1
  75.7 0.0 copy-start
  75.7 5.3 %pad_maximum_fusion.h = bf16[256,8192]{1,0:T(8,128)(2,1)} fusion(bf16[255,8192]{1,0:T(8,128)(2,1)} %bitcast.29, bf16[1,8192]{1,0:T(2,128)(2,1)S(1)} %collective-permute-done.1), kind=kLoop, calls=%fused_computation | loop fusion | flops 8388608 | bytes 8388608 | tf_op jit(solution)/shard_map/concatenate | solution.py:268
  81.0 0.0 all-to-all-done.1
  81.0 0.0 copy-start.2
  81.0 1.8 %all-gather.2.cloned.1.call-done.w = bf16[8192,512]{1,0:T(8,128)(2,1)} async-done(((bf16[256,512]{1,0:T(8,128)(2,1)}), bf16[8192,512]{1,0:T(8,128)(2,1)}) %all-gather.2.cloned.1.call-update) | async-done | bytes 8388624 | tf_op jit(solution)/shard_map/all_gather | solution.py:260
  82.9 0.0 copy-done.2
  82.9 0.0 copy-done
  82.9 11.5 %shard_map.104 = (bf16[256,512]{1,0:T(8,128)(2,1)S(1)}, bf16[2,4,4,8,32,128]{5,4,3,2,1,0:T(8,128)(2,1)S(1)}, bf16[256,8192]{1,0:T(8,128)(2,1)}) custom-call(s32[1]{0:T(128)} %bitcast.seat, s32[32,10]{1,0:T(8,128)S(1)} %copy-done, bf16[256,512]{1,0:T(8,128)(2,1)S(1)} %pad_maximum_fusion.2.g, bf16[256,8192]{1,0:T(8,128)(2,1)} %pad_maximum_fusion.h, ...), custom_call_target="tpu_custom_call" | custom-call | flops 4294967296 | bytes 20971520 | tf_op jit(solution)/shard_map/pallas_call | solution.py:222
  94.4 0.0 reduce-scatter.2.cloned.1.call-update
  94.4 30.9 %all_to_all.21 = bf16[32,256,128]{2,1,0:T(8,128)(2,1)S(1)} all-to-all(bf16[32,256,128]{2,1,0:T(8,128)(2,1)S(1)} %bitcast.27), channel_id=1, replica_groups=mesh['seq'=32,'mp'=8] {'seq'}, dimensions={0} | all-to-all | bytes 4194304 | tf_op jit(solution)/shard_map/all_to_all | solution.py:249
  125.3 2.9 %shard_map.105 = bf16[64,32,128]{2,1,0:T(8,128)(2,1)} custom-call(s32[32,10]{1,0:T(8,128)S(1)} %copy-done, bf16[256,32,128]{2,1,0:T(8,128)(2,1)S(1)} %bitcast.26), custom_call_target="tpu_custom_call" | custom-call | tf_op jit(solution)/shard_map/pallas_call | solution.py:109
  128.2 6.4 %all-to-all-start.3 = ((bf16[32,64,128]{2,1,0:T(8,128)(2,1)}), bf16[32,64,128]{2,1,0:T(8,128)(2,1)S(1)}, u32[]{:S(2)}, u32[]{:S(2)}) async-start(bf16[32,64,128]{2,1,0:T(8,128)(2,1)} %bitcast.8), calls=%async_computation.4 | async-start | bytes 1048576 | tf_op jit(solution)/shard_map/all_to_all | solution.py:249
  134.6 2.5 %collective-permute-start.2 = (bf16[1,512]{1,0:T(2,128)(2,1)S(1)}, bf16[1,512]{1,0:T(2,128)(2,1)S(1)}, u32[]{:S(2)}, u32[]{:S(2)}) collective-permute-start(bf16[1,512]{1,0:T(2,128)(2,1)S(1)} %slice.70), channel_id=1, source_target_pairs={{0,248},{8,0},{16,8},{24,16},{32,24},{40,32},{48,40},{56,48},{64,5... | collective-permute-start | bytes 3080 | tf_op jit(solution)/shard_map/ppermute | solution.py:31
  137.2 3.7 %collective-permute-done.2 = bf16[1,512]{1,0:T(2,128)(2,1)S(1)} collective-permute-done((bf16[1,512]{1,0:T(2,128)(2,1)S(1)}, bf16[1,512]{1,0:T(2,128)(2,1)S(1)}, u32[]{:S(2)}, u32[]{:S(2)}) %collective-permute-start.2) | collective-permute-done | bytes 1056 | tf_op jit(solution)/shard_map/ppermute | solution.py:31
  140.9 0.8 pad_maximum_fusion.3
  141.7 2.7 %all-to-all-done.3 = bf16[32,64,128]{2,1,0:T(8,128)(2,1)S(1)} async-done(((bf16[32,64,128]{2,1,0:T(8,128)(2,1)}), bf16[32,64,128]{2,1,0:T(8,128)(2,1)S(1)}, u32[]{:S(2)}, u32[]{:S(2)}) %all-to-all-start.3) | async-done | bytes 524320 | tf_op jit(solution)/shard_map/all_to_all | solution.py:249
  144.3 0.4 copy.30
  144.7 0.2 fusion.1
  144.9 5.7 %reduce-scatter.2.cloned.1.call-done = bf16[32,8192]{1,0:T(8,128)(2,1)} async-done(((bf16[256,8192]{1,0:T(8,128)(2,1)}), bf16[32,8192]{1,0:T(8,128)(2,1)}) %reduce-scatter.2.cloned.1.call-update) | async-done | bytes 524304 | tf_op jit(solution)/shard_map/reduce_scatter | solution.py:272
  150.6 0.9 slice.81
  151.6 3.5 %collective-permute-start.3 = (bf16[1,8192]{1,0:T(2,128)(2,1)S(1)}, bf16[1,8192]{1,0:T(2,128)(2,1)S(1)}, u32[]{:S(2)}, u32[]{:S(2)}) collective-permute-start(bf16[1,8192]{1,0:T(2,128)(2,1)S(1)} %slice.81), channel_id=1, source_target_pairs={{0,255},{1,0},{2,1},{3,2},{4,3},{5,4},{6,5},{7,6},{8,7},{9,8},{10,... | collective-permute-start | bytes 49160 | tf_op jit(solution)/shard_map/ppermute | solution.py:274
  155.0 0.9 copy_bitcast_fusion.1
  155.9 1.2 slice.80
  157.1 0.0 collective-permute-done.3
  157.1 0.9 pad_maximum_fusion.1
  (9 shorter events, 0.2 us)
Async XLA Ops:
  7.2 75.7 %all-gather.2.cloned.1.call-start = ((), (), s32[]{:S(2)}) async-start(), calls=%async_computation.5 | async-start | bytes 8650752 | tf_op jit(solution)/shard_map/all_gather | solution.py:260
  9.3 28.3 %copy-start.3 = (bf16[256,512]{1,0:T(8,128)(2,1)S(1)}, bf16[256,512]{1,0:T(8,128)(2,1)}, u32[]{:S(2)}) copy-start(bf16[256,512]{1,0:T(8,128)(2,1)} %param.13) | copy-start | bytes 786436
  27.9 0.9 copy-start.1
  31.7 49.3 %all-to-all-start.1 = ((bf16[32,256,128]{2,1,0:T(8,128)(2,1)}), bf16[32,256,128]{2,1,0:T(8,128)(2,1)S(1)}, u32[]{:S(2)}, u32[]{:S(2)}) async-start(bf16[32,256,128]{2,1,0:T(8,128)(2,1)} %bitcast.28), calls=%async_computation.1 | async-start | bytes 4194304 | tf_op jit(solution)/shard_map/all_to_all | solution.py:249
  37.5 113.1 %reduce-scatter.2.cloned.1.call-start = ((), (), s32[]{:S(2)}) async-start(), calls=%async_computation.6 | async-start | bytes 4718592 | tf_op jit(solution)/shard_map/reduce_scatter | solution.py:272
  37.6 36.7 %collective-permute-start = (bf16[1,512]{1,0:T(2,128)(2,1)S(1)}, bf16[1,512]{1,0:T(2,128)(2,1)S(1)}, u32[]{:S(2)}, u32[]{:S(2)}) collective-permute-start(bf16[1,512]{1,0:T(2,128)(2,1)S(1)} %slice.63), channel_id=1, source_target_pairs={{0,8},{8,16},{16,24},{24,32},{32,40},{40,48},{48,56},{56,64},{64,7... | collective-permute-start | bytes 3080 | tf_op jit(solution)/shard_map/ppermute | solution.py:31
  38.8 37.0 %collective-permute-start.1 = (bf16[1,8192]{1,0:T(2,128)(2,1)S(1)}, bf16[1,8192]{1,0:T(2,128)(2,1)S(1)}, u32[]{:S(2)}, u32[]{:S(2)}) collective-permute-start(bf16[1,8192]{1,0:T(2,128)(2,1)S(1)} %slice.66), channel_id=1, source_target_pairs={{0,8},{8,16},{16,24},{24,32},{32,40},{40,48},{48,56},{56,64},{64,7... | collective-permute-start | bytes 49160 | tf_op jit(solution)/shard_map/ppermute | solution.py:31
  75.7 7.1 %copy-start = (s32[32,10]{1,0:T(8,128)S(1)}, s32[32,10]{1,0:T(8,128)}, u32[]{:S(2)}) copy-start(s32[32,10]{1,0:T(8,128)} %pad_add_fusion.facts) | copy-start | bytes 3844
  81.0 1.8 %copy-start.2 = (bf16[32,256,128]{2,1,0:T(8,128)(2,1)}, bf16[32,256,128]{2,1,0:T(8,128)(2,1)S(1)}, u32[]{:S(2)}) copy-start(bf16[32,256,128]{2,1,0:T(8,128)(2,1)S(1)} %all-to-all-done.1) | copy-start | bytes 6291460
  128.2 16.1 %all-to-all-start.3 = ((bf16[32,64,128]{2,1,0:T(8,128)(2,1)}), bf16[32,64,128]{2,1,0:T(8,128)(2,1)S(1)}, u32[]{:S(2)}, u32[]{:S(2)}) async-start(bf16[32,64,128]{2,1,0:T(8,128)(2,1)} %bitcast.8), calls=%async_computation.4 | async-start | bytes 1048576 | tf_op jit(solution)/shard_map/all_to_all | solution.py:249
  134.6 6.3 %collective-permute-start.2 = (bf16[1,512]{1,0:T(2,128)(2,1)S(1)}, bf16[1,512]{1,0:T(2,128)(2,1)S(1)}, u32[]{:S(2)}, u32[]{:S(2)}) collective-permute-start(bf16[1,512]{1,0:T(2,128)(2,1)S(1)} %slice.70), channel_id=1, source_target_pairs={{0,248},{8,0},{16,8},{24,16},{32,24},{40,32},{48,40},{56,48},{64,5... | collective-permute-start | bytes 3080 | tf_op jit(solution)/shard_map/ppermute | solution.py:31
  151.6 5.5 %collective-permute-start.3 = (bf16[1,8192]{1,0:T(2,128)(2,1)S(1)}, bf16[1,8192]{1,0:T(2,128)(2,1)S(1)}, u32[]{:S(2)}, u32[]{:S(2)}) collective-permute-start(bf16[1,8192]{1,0:T(2,128)(2,1)S(1)} %slice.81), channel_id=1, source_target_pairs={{0,255},{1,0},{2,1},{3,2},{4,3},{5,4},{6,5},{7,6},{8,7},{9,8},{10,... | collective-permute-start | bytes 49160 | tf_op jit(solution)/shard_map/ppermute | solution.py:274
Sparse Core Ops, SparseCore 0:
  10.6 72.2 all-gather.1
  94.6 56.0 reduce-scatter.1
